TPU v7x, 32 devices: a whole 2x2x4 slice. The times are simulated.
32 devices in a mesh: row: 4 (over y, x), col: 8 (over z, core).
Axes of the slice: x: 2, y: 2, z: 4, core: 2. Of those that a mesh axis runs over, the one named last changes fastest.
Arguments:
- hidden_states: bfloat16 [512, 5120], P('row', 'col'), may hold values from -6 to 6
- clip_lengths: int32 [4, 2], P('row'), may hold values from 1 to 64, as said below
- modulation: bfloat16 [8, 3, 5120], P('row', None, 'col'), may hold values from -4 to 4
- fc1_weight: bfloat16 [5120, 13824], P('row', 'col'), may hold values from -0.078125 to 0.078125
- fc2_weight: bfloat16 [13824, 5120], P('col', 'row'), may hold values from -0.0546875 to 0.0546875
- out_grad: bfloat16 [512, 5120], P('row', 'col'), may hold values from -6 to 6
Outputs:
- block_out: bfloat16 [512, 5120], P('row', 'col')
- input_grad: bfloat16 [512, 5120], P('row', 'col')
- modulation_grad: float32 [8, 3, 5120], P('row', None, 'col')
Inputs may be any that keep to these rules, and one draw needn't show every extreme that they name: `clip_lengths`: in every draw the clip windows of some grid row all have 64 tokens.
All inputs are finite; a program needn't handle non-finite values.
Results may differ from a plain program's by a relative error of at most 0.0055.
Values may be sent and summed in bfloat16 or wider, within the bound.
No kernel may reach another device: no remote copies, remote signals or barrier semaphores. Data moves between devices by JAX's collectives and lax.ppermute only.
A program may use at most 128 MiB of HBM per device.

v0:
```python
import jax
import jax.numpy as jnp
from jax import lax
from jax.sharding import PartitionSpec as P

epsilon = 1e-06


def gelu_slope(value):
    coeff = 0.7978845608028654
    inner = coeff * (value + 0.044715 * value * value * value)
    tangent = jnp.tanh(inner)
    return 0.5 * (1.0 + tangent) + 0.5 * value * (1.0 - tangent * tangent) * coeff * (
        1.0 + 3.0 * 0.044715 * value * value
    )


def body(hidden_states, clip_lengths, modulation, fc1_weight, fc2_weight, out_grad):
    tok_rows, slice_width = hidden_states.shape
    clip_count = modulation.shape[0]
    full_width = slice_width * lax.axis_size("col")
    clip_ends = jnp.cumsum(clip_lengths[0])
    places = jnp.arange(tok_rows, dtype=jnp.int32)
    segment = jnp.sum((places[:, None] >= clip_ends[None, :]).astype(jnp.int32), axis=1)
    onehot = (segment[:, None] == jnp.arange(clip_count, dtype=jnp.int32)[None, :]).astype(
        jnp.float32
    )
    live_rows = (segment < clip_count).astype(jnp.float32)[:, None]
    local_mod = jnp.einsum(
        "tc,cd->td", onehot, modulation.astype(jnp.float32).reshape(clip_count, 3 * slice_width)
    )
    local_mod = local_mod.reshape(tok_rows, 3, slice_width)
    scale_here = local_mod[:, 1]
    gate_here = local_mod[:, 2]
    x_here = hidden_states.astype(jnp.float32)
    x_all, mod_all = (
        lax.all_gather(hidden_states, "col", axis=1, tiled=True),
        lax.all_gather(modulation, "col", axis=2, tiled=True),
    )
    x_full = x_all.astype(jnp.float32)
    centre = jnp.mean(x_full, axis=1, keepdims=True)
    deviation = x_full - centre
    inverse = lax.rsqrt(jnp.mean(deviation * deviation, axis=1, keepdims=True) + epsilon)
    token_all = jnp.einsum(
        "tc,cd->td", onehot, mod_all.astype(jnp.float32).reshape(clip_count, 3 * full_width)
    )
    token_all = token_all.reshape(tok_rows, 3, full_width)
    modulated = (deviation * inverse * (1.0 + token_all[:, 1]) + token_all[:, 0]).astype(
        jnp.bfloat16
    )
    normed = (x_here - centre) * inverse
    first_full, second_full = (
        lax.all_gather(fc1_weight, "row", axis=0, tiled=True),
        lax.all_gather(fc2_weight, "row", axis=1, tiled=True),
    )
    pre_act = jnp.dot(modulated, first_full, preferred_element_type=jnp.float32)
    activated = jax.nn.gelu(pre_act, approximate=True).astype(jnp.bfloat16)
    z_terms = jnp.dot(activated, second_full, preferred_element_type=jnp.float32)
    projected = lax.psum_scatter(z_terms, "col", scatter_dimension=1, tiled=True)
    block_out = (live_rows * (x_here + gate_here * projected)).astype(jnp.bfloat16)
    grad_float = out_grad.astype(jnp.float32)
    z_grad = (live_rows * gate_here * grad_float).astype(jnp.bfloat16)
    z_grad_full = lax.all_gather(z_grad, "col", axis=1, tiled=True)
    act_grad = lax.dot_general(
        z_grad_full, second_full, (((1,), (1,)), ((), ())), preferred_element_type=jnp.float32
    )
    pre_grad = (act_grad * gelu_slope(pre_act)).astype(jnp.bfloat16)
    in_terms = lax.dot_general(
        pre_grad, first_full, (((1,), (1,)), ((), ())), preferred_element_type=jnp.float32
    )
    mod_in_grad = lax.psum_scatter(in_terms, "col", scatter_dimension=1, tiled=True)
    norm_grad = mod_in_grad * (1.0 + scale_here)
    back_sums = lax.psum((jnp.sum(norm_grad, axis=1), jnp.sum(norm_grad * normed, axis=1)), "col")
    first_mean = (back_sums[0] / full_width)[:, None]
    second_mean = (back_sums[1] / full_width)[:, None]
    input_grad = (
        live_rows * (grad_float + inverse * (norm_grad - first_mean - normed * second_mean))
    ).astype(jnp.bfloat16)
    shift_grad = jnp.einsum("tc,td->cd", onehot, mod_in_grad)
    scale_grad = jnp.einsum("tc,td->cd", onehot, mod_in_grad * normed)
    gate_grad = jnp.einsum("tc,td->cd", onehot, projected * grad_float)
    modulation_grad = jnp.stack([shift_grad, scale_grad, gate_grad], axis=1)
    return (block_out, input_grad, modulation_grad)


def solution(mesh):
    return jax.shard_map(
        body,
        mesh=mesh,
        in_specs=(
            P("row", "col"),
            P("row", None),
            P("row", None, "col"),
            P("row", "col"),
            P("col", "row"),
            P("row", "col"),
        ),
        out_specs=(P("row", "col"), P("row", "col"), P("row", None, "col")),
        check_vma=False,
    )
```

profile of v0, /device:TPU:0, one launch (start us, length us, event | category | flops | bytes accessed | tf_op | source)
XLA Modules:
  0.0 504.9 jit_solution(15770883024290043815)
XLA Ops:
  7.2 0.0 copy-start.4
  7.2 0.0 copy-start.3
  7.2 0.0 all-gather.5.cloned.1.call-start
  7.2 0.7 all-gather.5.cloned.1.call-update
  7.9 0.0 copy-start.2
  7.9 0.0 all-gather.7.cloned.1.call-start
  8.0 0.7 all-gather.7.cloned.1.call-update
  8.7 0.0 all-gather.11.cloned.1.call-start
  8.7 0.0 copy-done.4
  8.7 0.2 reduce-window.8
  8.9 0.1 fusion.63
  9.0 0.0 copy-done.3
  9.0 0.3 fusion.59
  9.4 0.0 copy-done.2
  9.4 0.8 fusion.50
  10.1 0.0 all-gather.11.cloned.1.call-update
  10.2 0.0 all-gather.9.cloned.1.call-start
  10.2 0.5 all-gather.9.cloned.1.call-update
  10.7 0.0 reduce-scatter.5.cloned.1.call-start
  10.8 15.6 %all_gather.16 = bf16[2,3,5120]{2,0,1:T(2,128)(2,1)S(1)} all-gather(bf16[2,3,640]{2,0,1:T(2,128)(2,1)S(1)} %copy-done.3), channel_id=1, replica_groups=mesh['row'=4,'col'=8] {'col'}, dimensions={2}, use_global_device_ids=true | all-gather | bytes 69120 | tf_op jit(solution)/shard_map/all_gather | solution.py:38
  26.4 4.4 fusion.57
  30.8 5.3 %all-gather.5.cloned.1.call-done = bf16[128,5120]{1,0:T(8,128)(2,1)} async-done(((bf16[128,640]{1,0:T(8,128)(2,1)}), bf16[128,5120]{1,0:T(8,128)(2,1)}) %all-gather.5.cloned.1.call-update) | async-done | bytes 1310736 | tf_op jit(solution)/shard_map/all_gather | solution.py:37
  36.1 0.0 copy-start
  36.1 1.7 convert_reduce_fusion
  37.8 1.8 fusion.2
  39.6 164.1 %all-gather.7.cloned.1.call-done = bf16[5120,1728]{0,1:T(8,128)(2,1)} async-done(((bf16[1280,1728]{0,1:T(8,128)(2,1)}), bf16[5120,1728]{0,1:T(8,128)(2,1)}) %all-gather.7.cloned.1.call-update) | async-done | bytes 17694736 | tf_op jit(solution)/shard_map/all_gather | solution.py:53
  203.7 0.0 copy-done
  203.7 10.2 %fusion.8 = f32[128,1728]{0,1:T(8,128)S(1)} fusion(bf16[5120,1728]{0,1:T(8,128)(2,1)} %all-gather.7.cloned.1.call-done, bf16[128,5120]{1,0:T(8,128)(2,1)S(1)} %copy-done, f32[128,3,5120]{2,0,1:T(8,128)} %fusion.57, f32[128]{0:T(128)S(1)} %add_rsqrt_fusion, f32[128]{0:T(128)S(1)} %broadcast_multiply_fusion.2), kind=kOutput, calls=%fused_computation.16 | convolution fusion | flops 2269511680 | bytes 25134080 | tf_op jit(solution)/shard_map/dot_general | solution.py:56
  213.9 15.6 %all-gather.11.cloned.1.call-done = bf16[128,5120]{1,0:T(8,128)(2,1)} async-done(((bf16[128,640]{1,0:T(8,128)(2,1)}), bf16[128,5120]{1,0:T(8,128)(2,1)}) %all-gather.11.cloned.1.call-update) | async-done | bytes 1310736 | tf_op jit(solution)/shard_map/all_gather | solution.py:63
  229.5 167.5 %all-gather.9.cloned.1.call-done = bf16[1728,5120]{1,0:T(8,128)(2,1)} async-done(((bf16[1728,1280]{1,0:T(8,128)(2,1)}), bf16[1728,5120]{1,0:T(8,128)(2,1)}) %all-gather.9.cloned.1.call-update) | async-done | bytes 17694736 | tf_op jit(solution)/shard_map/all_gather | solution.py:54
  397.0 21.0 %fusion.26 = f32[128,5120]{1,0:T(8,128)} fusion(bf16[5120,1728]{0,1:T(8,128)(2,1)} %all-gather.7.cloned.1.call-done, bf16[128,5120]{1,0:T(8,128)(2,1)} %all-gather.11.cloned.1.call-done, bf16[1728,5120]{1,0:T(8,128)(2,1)} %all-gather.9.cloned.1.call-done, f32[128,1728]{0,1:T(8,128)S(1)} %fusion.8), kind=kOutput, calls=%fused_computation.36 | convolution fusion | flops 4534050816 | bytes 40206336 | tf_op jit(solution)/shard_map/dot_general | solution.py:68
  418.0 0.0 reduce-scatter.5.cloned.1.call-update
  418.1 0.2 reduce-scatter.3.cloned.1.call-start
  418.3 10.4 %fusion.29 = f32[128,5120]{1,0:T(8,128)} fusion(bf16[1728,5120]{1,0:T(8,128)(2,1)} %all-gather.9.cloned.1.call-done, f32[128,1728]{0,1:T(8,128)S(1)} %fusion.8), kind=kOutput, calls=%fused_computation.41 | convolution fusion | flops 2266914816 | bytes 21200896 | tf_op jit(solution)/shard_map/dot_general | solution.py:58
  428.7 0.0 copy-start.1
  428.7 0.0 reduce-scatter.3.cloned.1.call-update
  428.7 27.0 %reduce-scatter.5.cloned.1.call-done = f32[128,640]{1,0:T(8,128)} async-done(((f32[128,5120]{1,0:T(8,128)}), f32[128,640]{1,0:T(8,128)}) %reduce-scatter.5.cloned.1.call-update) | async-done | bytes 327696 | tf_op jit(solution)/shard_map/reduce_scatter | solution.py:71
  455.7 0.0 copy-done.1
  455.7 1.2 fusion.79
  456.9 15.4 %all-reduce = (f32[128]{0:T(128)S(1)}, f32[128]{0:T(128)S(1)}) all-reduce(f32[128]{0:T(128)S(1)} %get-tuple-element.4, f32[128]{0:T(128)S(1)} %get-tuple-element.3), channel_id=1, replica_groups=mesh['row'=4,'col'=8] {'col'}, use_global_device_ids=true, to_apply=%region_9.10 | all-reduce | flops 256 | bytes 2048 | tf_op jit(solution)/shard_map/psum | solution.py:73
  472.3 1.1 convolution_bitcast_fusion.2
  473.4 1.2 convolution_bitcast_fusion.1
  474.6 19.7 %reduce-scatter.3.cloned.1.call-done = f32[128,640]{1,0:T(8,128)} async-done(((f32[128,5120]{1,0:T(8,128)}), f32[128,640]{1,0:T(8,128)}) %reduce-scatter.3.cloned.1.call-update) | async-done | bytes 327696 | tf_op jit(solution)/shard_map/reduce_scatter | solution.py:59
  494.3 1.1 convolution_bitcast_fusion
  495.4 0.6 pad_maximum_fusion
  496.0 2.0 fusion.52
  (4 shorter events, 0.0 us)
Async XLA Ops:
  7.2 1.6 copy-start.4
  7.2 1.8 copy-start.3
  7.2 28.9 %all-gather.5.cloned.1.call-start = ((), (), s32[]{:S(2)}) async-start(), calls=%async_computation.2 | async-start | bytes 1474560 | tf_op jit(solution)/shard_map/all_gather | solution.py:37
  7.9 1.4 copy-start.2
  7.9 195.8 %all-gather.7.cloned.1.call-start = ((), (), s32[]{:S(2)}) async-start(), calls=%async_computation.3 | async-start | bytes 22118400 | tf_op jit(solution)/shard_map/all_gather | solution.py:53
  8.7 220.9 %all-gather.11.cloned.1.call-start = ((), (), s32[]{:S(2)}) async-start(), calls=%async_computation.6 | async-start | bytes 1474560 | tf_op jit(solution)/shard_map/all_gather | solution.py:63
  10.2 386.9 %all-gather.9.cloned.1.call-start = ((), (), s32[]{:S(2)}) async-start(), calls=%async_computation.4 | async-start | bytes 22118400 | tf_op jit(solution)/shard_map/all_gather | solution.py:54
  10.7 445.0 %reduce-scatter.5.cloned.1.call-start = ((), (), s32[]{:S(2)}) async-start(), calls=%async_computation.7 | async-start | bytes 2949120 | tf_op jit(solution)/shard_map/reduce_scatter | solution.py:71
  36.1 167.6 %copy-start = (bf16[128,5120]{1,0:T(8,128)(2,1)S(1)}, bf16[128,5120]{1,0:T(8,128)(2,1)}, u32[]{:S(2)}) copy-start(bf16[128,5120]{1,0:T(8,128)(2,1)} %all-gather.5.cloned.1.call-done) | copy-start | bytes 3932164
  418.1 76.2 %reduce-scatter.3.cloned.1.call-start = ((), (), s32[]{:S(2)}) async-start(), calls=%async_computation.5 | async-start | bytes 2949120 | tf_op jit(solution)/shard_map/reduce_scatter | solution.py:59
  428.7 27.0 %copy-start.1 = (bf16[128,640]{1,0:T(8,128)(2,1)S(1)}, bf16[128,640]{1,0:T(8,128)(2,1)}, u32[]{:S(2)}) copy-start(bf16[128,640]{1,0:T(8,128)(2,1)} %param.6) | copy-start | bytes 491524
Sparse Core Ops, SparseCore 0:
  9.6 26.3 all-gather.4
  37.9 165.7 all-gather.6
  205.9 23.6 all-gather.10
  231.3 165.7 all-gather.8
  418.2 37.5 reduce-scatter.4
  457.9 36.3 reduce-scatter.2
where the time goes:
time: 505 us
  waiting for transfers between devices  401 us (79%)
  matrix products  49.8 us (10%)
  blocking collectives  31 us (6%)
  between operations  14.2 us (3%)
  other arithmetic  8.38 us (2%)
    all_gather x1, waiting for transfers between devices, body(): lax.all_gather(fc2_weight, 'row', axis=1, tiled=True)  167 us
    all_gather x1, waiting for transfers between devices, body(): lax.all_gather(fc1_weight, 'row', axis=0, tiled=True)  164 us
    reduce_scatter x1, waiting for transfers between devices, body(): lax.psum_scatter(in_terms, 'col', scatter_dimension=1, tiled=True)  27 us
    dot_general x1, matrix products, body(): lax.dot_general(pre_grad, first_full, (((1,), (1,)), ((), ())), preferred...  21 us
    reduce_scatter x1, waiting for transfers between devices, body(): lax.psum_scatter(z_terms, 'col', scatter_dimension=1, tiled=True)  19.7 us
    all_gather x1, waiting for transfers between devices, body(): z_grad_full = lax.all_gather(z_grad, 'col', axis=1, tiled=True)  15.6 us
    all_gather x1, blocking collectives, body(): lax.all_gather(modulation, 'col', axis=2, tiled=True)  15.6 us
    psum x1, blocking collectives, body(): lax.psum((jnp.sum(norm_grad, axis=1), jnp.sum(norm_grad * normed, axis=1)...  15.4 us
  transfers between devices with their start and end apart: 6, of which 6 were waited for; matrix products, arithmetic and copies ran while one was open for 7% of the time, Pallas kernels for 0%

commit v1 on v0

v1 whole, which is shorter than its diff:
```python
import jax
import jax.numpy as jnp
from jax import lax
from jax.sharding import PartitionSpec as P

epsilon = 1e-06
BF = jnp.bfloat16
F32 = jnp.float32


def gelu_and_slope(value):
    coeff = 0.7978845608028654
    inner = coeff * (value + 0.044715 * value * value * value)
    tangent = jnp.tanh(inner)
    half = 0.5 * (1.0 + tangent)
    slope = half + 0.5 * value * (1.0 - tangent * tangent) * coeff * (
        1.0 + 3.0 * 0.044715 * value * value
    )
    return value * half, slope


def make_body(rows, cols):
    depth = cols // 2
    bits = [1 << b for b in range(rows.bit_length() - 1)]

    def over_row(value, flip):
        return lax.ppermute(value, "row", [(i, i ^ flip) for i in range(rows)])

    def over_z(value, flip):
        return lax.ppermute(value, "col", [(i, i ^ (2 * flip)) for i in range(cols)])

    def over_core(value):
        return lax.ppermute(value, "col", [(i, i ^ 1) for i in range(cols)])

    def transpose_owner(value):
        pairs = []
        for r in range(rows):
            for c in range(cols):
                pairs.append((r * cols + c, (c // 2) * cols + 2 * r + c % 2))
        return lax.ppermute(value, ("row", "col"), pairs)

    def reduce_rows(blocks, order):
        blocks = dict(enumerate(blocks))
        for flip in order:
            sent = [j for j in sorted(blocks) if j & flip]
            came = over_row(jnp.stack([blocks[j].astype(BF) for j in sent]), flip)
            for place, j in enumerate(sent):
                blocks[j ^ flip] = blocks[j ^ flip] + came[place].astype(F32)
                del blocks[j]
        return blocks[0]

    def gather_rows(value, order):
        have = {0: value}
        for flip in order:
            sent = sorted(have)
            came = over_row(jnp.stack([have[j] for j in sent]), flip)
            for place, j in enumerate(sent):
                have[j ^ flip] = came[place]
        return [have[j] for j in range(rows)]

    def reduce_scatter_rows(share, tok_rows):
        half = tok_rows // 2
        parts = share.reshape(rows, tok_rows, share.shape[1])
        first = reduce_rows([parts[j, :half] for j in range(rows)], bits)
        second = reduce_rows([parts[j, half:] for j in range(rows)], bits[::-1])
        return jnp.concatenate([first, second], axis=0)

    def all_gather_rows(value):
        half = value.shape[0] // 2
        first = gather_rows(value[:half], bits)
        second = gather_rows(value[half:], bits[::-1])
        return jnp.concatenate([p for pair in zip(first, second) for p in pair], axis=0)

    def body(hidden_states, clip_lengths, modulation, fc1_weight, fc2_weight, out_grad):
        tok_rows, width = hidden_states.shape
        clip_count = modulation.shape[0]
        full_width = width * cols
        r = lax.axis_index("row")
        c = lax.axis_index("col")
        z, core = c // 2, c % 2

        clip_ends = jnp.cumsum(clip_lengths[0])
        places = jnp.arange(tok_rows, dtype=jnp.int32)
        segment = jnp.sum((places[:, None] >= clip_ends[None, :]).astype(jnp.int32), axis=1)
        onehot = (segment[:, None] == jnp.arange(clip_count, dtype=jnp.int32)[None, :]).astype(F32)
        live = (segment < clip_count).astype(F32)[:, None]

        def per_token(vectors):
            total = onehot[:, 0:1] * vectors[0:1].astype(F32)
            for i in range(1, clip_count):
                total = total + onehot[:, i : i + 1] * vectors[i : i + 1].astype(F32)
            return total

        def to_rows(pick):
            got = [pick(r)] + [over_row(pick(r ^ i), i) for i in range(1, rows)]
            own = jnp.concatenate(got, axis=0)
            other = over_core(own)
            low = jnp.where(core == 0, own, other)
            high = jnp.where(core == 0, other, own)
            return jnp.concatenate([low, high], axis=1)

        def to_owner(share):
            low, high = share[:, :width], share[:, width:]
            kept = jnp.where(core == 0, low, high)
            given = jnp.where(core == 0, high, low)
            both = kept + over_core(given.astype(BF)).astype(F32)
            both = both.reshape(rows, tok_rows, width)

            def group(flip):
                return lax.dynamic_index_in_dim(both, r ^ z ^ flip, 0, keepdims=False)

            total = group(0)
            for flip in range(1, depth):
                total = total + over_z(group(flip).astype(BF), flip).astype(F32)
            return transpose_owner(total.astype(BF)).astype(F32)

        x_here = hidden_states.astype(F32)
        g_here = out_grad.astype(F32)
        scale_here = per_token(modulation[:, 1])
        gate_here = per_token(modulation[:, 2])

        fill = -(tok_rows + 2 * clip_count) % 16
        packed = jnp.concatenate(
            [hidden_states, modulation[:, 0], modulation[:, 1], jnp.zeros((fill, width), BF)], axis=0
        )
        chunks = jnp.stack([packed] + [over_z(packed, i) for i in range(1, depth)])
        x_part = chunks[:, :tok_rows].astype(F32)
        mean_part = jnp.mean(x_part, axis=(0, 2))
        spread = x_part - mean_part[None, :, None]
        square_part = jnp.sum(spread * spread, axis=(0, 2))
        theirs = over_core(jnp.stack([mean_part, square_part]))
        centre = 0.5 * (mean_part + theirs[0])
        gap = mean_part - theirs[0]
        square = square_part + theirs[1] + gap * gap * (full_width / 4)
        inverse = lax.rsqrt(square / full_width + epsilon)[:, None]
        centre = centre[:, None]
        normed = (x_here - centre) * inverse

        def pick_modulated(j):
            chunk = lax.dynamic_index_in_dim(chunks, z ^ j, 0, keepdims=False)
            shift = per_token(chunk[tok_rows : tok_rows + clip_count])
            scale = per_token(chunk[tok_rows + clip_count : tok_rows + 2 * clip_count])
            x = chunk[:tok_rows].astype(F32)
            return ((x - centre) * inverse * (1.0 + scale) + shift).astype(BF)

        z_grad = (live * gate_here * g_here).astype(BF)
        z_grad, _ = lax.optimization_barrier((z_grad, chunks))
        z_chunks = jnp.stack([z_grad] + [over_z(z_grad, i) for i in range(1, depth)])

        def pick_z_grad(j):
            return lax.dynamic_index_in_dim(z_chunks, z ^ j, 0, keepdims=False)

        modulated = to_rows(pick_modulated)
        pre_share = jnp.dot(modulated, fc1_weight, preferred_element_type=F32)
        pre_act = reduce_scatter_rows(pre_share, tok_rows)
        z_rows = to_rows(pick_z_grad)
        act_share = lax.dot_general(
            z_rows, fc2_weight, (((1,), (1,)), ((), ())), preferred_element_type=F32
        )
        act_grad = reduce_scatter_rows(act_share, tok_rows)
        activated, slope = gelu_and_slope(pre_act)
        activated_rows = all_gather_rows(activated.astype(BF))
        pre_grad_rows = all_gather_rows((act_grad * slope).astype(BF))
        in_share = lax.dot_general(
            pre_grad_rows, fc1_weight, (((1,), (1,)), ((), ())), preferred_element_type=F32
        )
        out_share = jnp.dot(activated_rows, fc2_weight, preferred_element_type=F32)
        mod_in_grad = to_owner(in_share)
        projected = to_owner(out_share)

        block_out = (live * (x_here + gate_here * projected)).astype(BF)
        norm_grad = mod_in_grad * (1.0 + scale_here)
        sums = jnp.stack([jnp.sum(norm_grad, axis=1), jnp.sum(norm_grad * normed, axis=1)])
        sums = sums + over_core(sums)
        sums = sums + sum(over_z(sums, i) for i in range(1, depth))
        first_mean = (sums[0] / full_width)[:, None]
        second_mean = (sums[1] / full_width)[:, None]
        input_grad = (
            live * (g_here + inverse * (norm_grad - first_mean - normed * second_mean))
        ).astype(BF)

        def per_clip(values):
            return jnp.stack(
                [jnp.sum(onehot[:, i : i + 1] * values, axis=0) for i in range(clip_count)]
            )

        modulation_grad = jnp.stack(
            [per_clip(mod_in_grad), per_clip(mod_in_grad * normed), per_clip(projected * g_here)],
            axis=1,
        )
        return (block_out, input_grad, modulation_grad)

    return body


def solution(mesh):
    rows, cols = mesh.shape["row"], mesh.shape["col"]
    return jax.shard_map(
        make_body(rows, cols),
        mesh=mesh,
        in_specs=(
            P("row", "col"),
            P("row", None),
            P("row", None, "col"),
            P("row", "col"),
            P("col", "row"),
            P("row", "col"),
        ),
        out_specs=(P("row", "col"), P("row", "col"), P("row", None, "col")),
        check_vma=False,
    )
```

time: 505 us -> 210 us (0.42)
  waiting for transfers between devices: 401 us -> 113 us
  starting transfers between devices: 0.42 us -> 61.1 us
  matrix products: 49.8 us -> 12.5 us
  blocking collectives: 31 us -> 0 us
  between operations: 14.2 us -> 1.29 us
  other arithmetic: 8.38 us -> 15.6 us
    all_gather x4 -> x0, waiting for transfers between devices: 353 us -> none  [the longest x1 167 us: body(): lax.all_gather(fc2_weight, 'row', axis=1, tiled=True)]
    ppermute x0 -> x45, waiting for transfers between devices: none -> 113 us  [the longest x22 61.5 us: over_row(): return lax.ppermute(value, 'row', [(i, i ^ flip) for i in range(rows)])]
    ppermute x0 -> x45, starting transfers between devices: none -> 61.1 us  [the longest x15 34.8 us: over_z(): return lax.ppermute(value, 'col', [(i, i ^ 2 * flip) for i in range(cols)])]
    reduce_scatter x2 -> x0, waiting for transfers between devices: 46.6 us -> none  [the longest x1 27 us: body(): lax.psum_scatter(in_terms, 'col', scatter_dimension=1, tiled=True)]
    dot_general x8 -> x2, matrix products: 49.8 us -> 5.1 us  [the longest x1 2.55 us: body(): lax.dot_general(pre_grad_rows, fc1_weight, (((1,), (1,)), ((), ())), pref...]
    all_gather x1 -> x0, blocking collectives: 15.6 us -> none  [body(): lax.all_gather(modulation, 'col', axis=2, tiled=True)]
    psum x1 -> x0, blocking collectives: 15.4 us -> none  [body(): lax.psum((jnp.sum(norm_grad, axis=1), jnp.sum(norm_grad * normed, axis=1)...]
    reshape x0 -> x2, matrix products: none -> 7.42 us  [reduce_scatter_rows(): parts = share.reshape(rows, tok_rows, share.shape[1])]
  transfers between devices with their start and end apart: 6 -> 45, of which waited for: 6 -> 23; matrix products, arithmetic and copies ran while one was open for 7% -> 8% of each run, Pallas kernels for 0% -> 0%
where the time goes in v1:
time: 210 us; the launch traced here: 207 us
  waiting for transfers between devices  113 us (54%)
  starting transfers between devices  61.1 us (29%)
  other arithmetic  15.6 us (7%)
  matrix products  12.5 us (6%)
  local copies, waits for them, and re-layouts  2.94 us (1%)
    ppermute x22, waiting for transfers between devices, over_row(): return lax.ppermute(value, 'row', [(i, i ^ flip) for i in range(rows)])  61.5 us
    ppermute x15, waiting for transfers between devices, over_z(): return lax.ppermute(value, 'col', [(i, i ^ 2 * flip) for i in range(cols)])  47.5 us
    ppermute x15, starting transfers between devices, over_z(): return lax.ppermute(value, 'col', [(i, i ^ 2 * flip) for i in range(cols)])  34.8 us
    ppermute x22, starting transfers between devices, over_row(): return lax.ppermute(value, 'row', [(i, i ^ flip) for i in range(rows)])  24.2 us
    reshape x2, matrix products, reduce_scatter_rows(): parts = share.reshape(rows, tok_rows, share.shape[1])  7.42 us
    ppermute x6, waiting for transfers between devices, over_core(): return lax.ppermute(value, 'col', [(i, i ^ 1) for i in range(cols)])  4.25 us
  transfers between devices with their start and end apart: 45, of which 23 were waited for; matrix products, arithmetic and copies ran while one was open for 8% of the time, Pallas kernels for 0%

profile of v1, /device:TPU:0, one launch (start us, length us, event | category | flops | bytes accessed | tf_op | source)
XLA Modules:
  0.0 206.6 jit_solution(10086106088259312134)
XLA Ops:
  0.6 0.7 slice_bitcast_fusion.13
  1.4 1.1 maximum_maximum_fusion
  2.5 4.1 %collective-permute-start.1 = (bf16[144,640]{1,0:T(8,128)(2,1)S(1)}, bf16[144,640]{1,0:T(8,128)(2,1)S(1)}, u32[]{:S(2)}, u32[]{:S(2)}) collective-permute-start(bf16[144,640]{1,0:T(8,128)(2,1)S(1)} %maximum_maximum_fusion), channel_id=1, source_target_pairs={{0,4},{1,5},{2,6},{3,7},{4,0},{5,1},{6,2},{7,3},{8,12},{9,13},{10,... | collective-permute-start | bytes 552968 | tf_op jit(solution)/shard_map/ppermute | solution.py:30
  6.6 1.6 collective-permute-start
  8.2 0.8 convert_reduce_fusion.2
  9.0 1.0 fusion.132
  10.0 0.8 reduce-window.8
  10.9 5.9 %collective-permute-done.1 = bf16[144,640]{1,0:T(8,128)(2,1)S(1)} collective-permute-done((bf16[144,640]{1,0:T(8,128)(2,1)S(1)}, bf16[144,640]{1,0:T(8,128)(2,1)S(1)}, u32[]{:S(2)}, u32[]{:S(2)}) %collective-permute-start.1) | collective-permute-done | bytes 184352 | tf_op jit(solution)/shard_map/ppermute | solution.py:30
  16.8 3.5 %collective-permute-done.2 = bf16[144,640]{1,0:T(8,128)(2,1)S(1)} collective-permute-done((bf16[144,640]{1,0:T(8,128)(2,1)S(1)}, bf16[144,640]{1,0:T(8,128)(2,1)S(1)}, u32[]{:S(2)}, u32[]{:S(2)}) %collective-permute-start.2) | collective-permute-done | bytes 184352 | tf_op jit(solution)/shard_map/ppermute | solution.py:30
  21.2 1.0 collective-permute-done.3
  22.6 2.5 %collective-permute-start.23 = (bf16[128,640]{1,0:T(8,128)(2,1)S(1)}, bf16[128,640]{1,0:T(8,128)(2,1)S(1)}, u32[]{:S(2)}, u32[]{:S(2)}) collective-permute-start(bf16[128,640]{1,0:T(8,128)(2,1)S(1)} %get-tuple-element.4), channel_id=1, source_target_pairs={{0,6},{1,7},{2,4},{3,5},{4,2},{5,3},{6,0},{7,1},{8,14},{9,15},{10,... | collective-permute-start | bytes 491528 | tf_op jit(solution)/shard_map/ppermute | solution.py:30
  25.2 3.0 %collective-permute-start.22 = (bf16[128,640]{1,0:T(8,128)(2,1)S(1)}, bf16[128,640]{1,0:T(8,128)(2,1)S(1)}, u32[]{:S(2)}, u32[]{:S(2)}) collective-permute-start(bf16[128,640]{1,0:T(8,128)(2,1)S(1)} %get-tuple-element.4), channel_id=1, source_target_pairs={{0,4},{1,5},{2,6},{3,7},{4,0},{5,1},{6,2},{7,3},{8,12},{9,13},{10,... | collective-permute-start | bytes 491528 | tf_op jit(solution)/shard_map/ppermute | solution.py:30
  29.0 1.5 collective-permute-start.4
  30.6 1.5 collective-permute-start.6
  32.6 8.8 %collective-permute-done.22 = bf16[128,640]{1,0:T(8,128)(2,1)S(1)} collective-permute-done((bf16[128,640]{1,0:T(8,128)(2,1)S(1)}, bf16[128,640]{1,0:T(8,128)(2,1)S(1)}, u32[]{:S(2)}, u32[]{:S(2)}) %collective-permute-start.22) | collective-permute-done | bytes 163872 | tf_op jit(solution)/shard_map/ppermute | solution.py:30
  41.5 2.5 %collective-permute-start.26 = (bf16[128,640]{1,0:T(8,128)(2,1)S(1)}, bf16[128,640]{1,0:T(8,128)(2,1)S(1)}, u32[]{:S(2)}, u32[]{:S(2)}) collective-permute-start(bf16[128,640]{1,0:T(8,128)(2,1)S(1)} %get-tuple-element.64), channel_id=1, source_target_pairs={{0,24},{8,16},{16,8},{24,0},{1,25},{9,17},{17,9},{25,1},{2,26},{10... | collective-permute-start | bytes 491528 | tf_op jit(solution)/shard_map/ppermute | solution.py:27
  45.2 4.3 %collective-permute-done.26 = bf16[128,640]{1,0:T(8,128)(2,1)S(1)} collective-permute-done((bf16[128,640]{1,0:T(8,128)(2,1)S(1)}, bf16[128,640]{1,0:T(8,128)(2,1)S(1)}, u32[]{:S(2)}, u32[]{:S(2)}) %collective-permute-start.26) | collective-permute-done | bytes 163872 | tf_op jit(solution)/shard_map/ppermute | solution.py:27
  49.5 2.6 %collective-permute-done.25 = bf16[128,640]{1,0:T(8,128)(2,1)S(1)} collective-permute-done((bf16[128,640]{1,0:T(8,128)(2,1)S(1)}, bf16[128,640]{1,0:T(8,128)(2,1)S(1)}, u32[]{:S(2)}, u32[]{:S(2)}) %collective-permute-start.25) | collective-permute-done | bytes 163872 | tf_op jit(solution)/shard_map/ppermute | solution.py:27
  52.4 2.2 %collective-permute-done.27 = bf16[512,640]{1,0:T(8,128)(2,1)} collective-permute-done((bf16[512,640]{1,0:T(8,128)(2,1)S(1)}, bf16[512,640]{1,0:T(8,128)(2,1)}, u32[]{:S(2)}, u32[]{:S(2)}) %collective-permute-start.27) | collective-permute-done | bytes 655392 | tf_op jit(solution)/shard_map/ppermute | solution.py:33
  54.6 1.8 broadcast_select_fusion.1
  56.4 4.9 %fusion.6 = f32[512,1728]{1,0:T(8,128)S(1)} fusion(bf16[1728,1280]{1,0:T(8,128)(2,1)} %param.10, bf16[512,640]{1,0:T(8,128)(2,1)S(1)} %get-tuple-element.51, bf16[512,640]{1,0:T(8,128)(2,1)S(1)} %get-tuple-element.50), kind=kOutput, calls=%fused_computation.10 | convolution fusion | flops 2267545600 | bytes 9273344 | tf_op jit(solution)/shard_map/reshape | solution.py:63
  61.5 1.6 collective-permute-start.28
  63.1 2.6 %fusion.2 = f32[512,1728]{1,0:T(8,128)S(1)} fusion(bf16[1280,1728]{0,1:T(8,128)(2,1)S(1)} %bitcast.204, bf16[512,640]{1,0:T(8,128)(2,1)S(1)} %get-tuple-element.83, bf16[512,640]{1,0:T(8,128)(2,1)S(1)} %get-tuple-element.84), kind=kOutput, calls=%fused_computation.6 | convolution fusion | flops 2267545600 | bytes 9273344 | tf_op jit(solution)/shard_map/reshape | solution.py:63
  66.0 0.8 collective-permute-start.30
  66.8 1.3 collective-permute-start.8
  68.7 6.3 %collective-permute-done.28 = bf16[2,64,1728]{2,1,0:T(8,128)(2,1)S(1)} collective-permute-done((bf16[2,64,1728]{2,1,0:T(8,128)(2,1)S(1)}, bf16[2,64,1728]{2,1,0:T(8,128)(2,1)S(1)}, u32[]{:S(2)}, u32[]{:S(2)}) %collective-permute-start.28) | collective-permute-done | bytes 442400 | tf_op jit(solution)/shard_map/ppermute | solution.py:27
  75.0 1.5 collective-permute-start.29
  76.5 7.5 %collective-permute-done.8 = bf16[2,64,1728]{2,1,0:T(8,128)(2,1)S(1)} collective-permute-done((bf16[2,64,1728]{2,1,0:T(8,128)(2,1)S(1)}, bf16[2,64,1728]{2,1,0:T(8,128)(2,1)S(1)}, u32[]{:S(2)}, u32[]{:S(2)}) %collective-permute-start.8) | collective-permute-done | bytes 442400 | tf_op jit(solution)/shard_map/ppermute | solution.py:27
  84.0 1.5 collective-permute-start.9
  85.5 8.6 %collective-permute-done.29 = bf16[1,64,1728]{2,1,0:T(8,128)(2,1)S(1)} collective-permute-done((bf16[1,64,1728]{2,1,0:T(8,128)(2,1)S(1)}, bf16[1,64,1728]{2,1,0:T(8,128)(2,1)S(1)}, u32[]{:S(2)}, u32[]{:S(2)}) %collective-permute-start.29) | collective-permute-done | bytes 221216 | tf_op jit(solution)/shard_map/ppermute | solution.py:27
  94.9 3.1 %collective-permute-done.9 = bf16[1,64,1728]{2,1,0:T(8,128)(2,1)S(1)} collective-permute-done((bf16[1,64,1728]{2,1,0:T(8,128)(2,1)S(1)}, bf16[1,64,1728]{2,1,0:T(8,128)(2,1)S(1)}, u32[]{:S(2)}, u32[]{:S(2)}) %collective-permute-start.9) | collective-permute-done | bytes 221216 | tf_op jit(solution)/shard_map/ppermute | solution.py:27
  98.7 2.2 %collective-permute-done.31 = bf16[1,64,1728]{2,1,0:T(8,128)(2,1)S(1)} collective-permute-done((bf16[1,64,1728]{2,1,0:T(8,128)(2,1)S(1)}, bf16[1,64,1728]{2,1,0:T(8,128)(2,1)S(1)}, u32[]{:S(2)}, u32[]{:S(2)}) %collective-permute-start.31) | collective-permute-done | bytes 221216 | tf_op jit(solution)/shard_map/ppermute | solution.py:27
  101.0 4.3 %collective-permute-done.11 = bf16[1,64,1728]{2,1,0:T(8,128)(2,1)S(1)} collective-permute-done((bf16[1,64,1728]{2,1,0:T(8,128)(2,1)S(1)}, bf16[1,64,1728]{2,1,0:T(8,128)(2,1)S(1)}, u32[]{:S(2)}, u32[]{:S(2)}) %collective-permute-start.11) | collective-permute-done | bytes 221216 | tf_op jit(solution)/shard_map/ppermute | solution.py:27
  106.7 1.5 collective-permute-start.33
  108.2 0.8 collective-permute-start.32
  109.0 1.3 collective-permute-start.13
  110.3 4.4 %collective-permute-done.12 = bf16[1,64,1728]{2,1,0:T(8,128)(2,1)S(1)} collective-permute-done((bf16[1,64,1728]{2,1,0:T(8,128)(2,1)S(1)}, bf16[1,64,1728]{2,1,0:T(8,128)(2,1)S(1)}, u32[]{:S(2)}, u32[]{:S(2)}) %collective-permute-start.12) | collective-permute-done | bytes 221216 | tf_op jit(solution)/shard_map/ppermute | solution.py:27
  114.7 0.8 collective-permute-start.15
  115.5 4.7 %collective-permute-done.13 = bf16[1,64,1728]{2,1,0:T(8,128)(2,1)S(1)} collective-permute-done((bf16[1,64,1728]{2,1,0:T(8,128)(2,1)S(1)}, bf16[1,64,1728]{2,1,0:T(8,128)(2,1)S(1)}, u32[]{:S(2)}, u32[]{:S(2)}) %collective-permute-start.13) | collective-permute-done | bytes 221216 | tf_op jit(solution)/shard_map/ppermute | solution.py:27
  120.3 1.6 collective-permute-start.14
  121.9 0.8 collective-permute-start.35
  122.7 1.3 collective-permute-start.34
  124.1 13.4 %collective-permute-done.34 = bf16[2,64,1728]{2,1,0:T(8,128)(2,1)S(1)} collective-permute-done((bf16[2,64,1728]{2,1,0:T(8,128)(2,1)S(1)}, bf16[2,64,1728]{2,1,0:T(8,128)(2,1)S(1)}, u32[]{:S(2)}, u32[]{:S(2)}) %collective-permute-start.34) | collective-permute-done | bytes 442400 | tf_op jit(solution)/shard_map/ppermute | solution.py:27
  137.6 2.5 %fusion.125 = f32[512,1280]{1,0:T(8,128)S(1)} fusion(bf16[512,1728]{1,0:T(8,128)(2,1)S(1)} %fusion.65, bf16[1280,1728]{0,1:T(8,128)(2,1)S(1)} %bitcast.204), kind=kOutput, calls=%fused_computation.252 | convolution fusion | flops 2264924160 | bytes 8814592 | tf_op jit(solution)/shard_map/dot_general | solution.py:164
  140.2 1.2 select_convert_fusion
  141.5 2.5 %fusion.124 = f32[512,1280]{1,0:T(8,128)S(1)} fusion(bf16[512,1728]{1,0:T(8,128)(2,1)S(1)} %fusion.69, bf16[1728,1280]{1,0:T(8,128)(2,1)S(1)} %bitcast.206), kind=kOutput, calls=%fused_computation.251 | convolution fusion | flops 2264924160 | bytes 8814592 | tf_op jit(solution)/shard_map/dot_general | solution.py:167
  144.1 1.5 copy-done
  145.6 1.0 select_convert_fusion.1
  147.4 2.5 %collective-permute-start.39 = (bf16[128,640]{1,0:T(8,128)(2,1)S(1)}, bf16[128,640]{1,0:T(8,128)(2,1)S(1)}, u32[]{:S(2)}, u32[]{:S(2)}) collective-permute-start(bf16[128,640]{1,0:T(8,128)(2,1)S(1)} %get-tuple-element.48), channel_id=1, source_target_pairs={{0,6},{1,7},{2,4},{3,5},{4,2},{5,3},{6,0},{7,1},{8,14},{9,15},{10,... | collective-permute-start | bytes 491528 | tf_op jit(solution)/shard_map/ppermute | solution.py:30
  149.9 1.0 collective-permute-start.38
  150.8 1.3 convert_add_fusion.1
  152.2 1.0 collective-permute-start.17
  153.2 2.4 %collective-permute-start.19 = (bf16[128,640]{1,0:T(8,128)(2,1)S(1)}, bf16[128,640]{1,0:T(8,128)(2,1)S(1)}, u32[]{:S(2)}, u32[]{:S(2)}) collective-permute-start(bf16[128,640]{1,0:T(8,128)(2,1)S(1)} %get-tuple-element.53), channel_id=1, source_target_pairs={{0,6},{1,7},{2,4},{3,5},{4,2},{5,3},{6,0},{7,1},{8,14},{9,15},{10,... | collective-permute-start | bytes 491528 | tf_op jit(solution)/shard_map/ppermute | solution.py:30
  155.7 1.3 collective-permute-start.18
  157.0 1.4 collective-permute-done.39
  158.4 15.1 %collective-permute-done.38 = bf16[128,640]{1,0:T(8,128)(2,1)S(1)} collective-permute-done((bf16[128,640]{1,0:T(8,128)(2,1)S(1)}, bf16[128,640]{1,0:T(8,128)(2,1)S(1)}, u32[]{:S(2)}, u32[]{:S(2)}) %collective-permute-start.38) | collective-permute-done | bytes 163872 | tf_op jit(solution)/shard_map/ppermute | solution.py:30
  174.2 9.9 %collective-permute-done.18 = bf16[128,640]{1,0:T(8,128)(2,1)S(1)} collective-permute-done((bf16[128,640]{1,0:T(8,128)(2,1)S(1)}, bf16[128,640]{1,0:T(8,128)(2,1)S(1)}, u32[]{:S(2)}, u32[]{:S(2)}) %collective-permute-start.18) | collective-permute-done | bytes 163872 | tf_op jit(solution)/shard_map/ppermute | solution.py:30
  184.9 1.2 multiply_reduce_fusion.3
  186.3 1.1 collective-permute-done.41
  187.4 7.8 %collective-permute-start.44 = (f32[2,128]{1,0:T(2,128)S(1)}, f32[2,128]{1,0:T(2,128)S(1)}, u32[]{:S(2)}, u32[]{:S(2)}) collective-permute-start(f32[2,128]{1,0:T(2,128)S(1)} %fusion.120), channel_id=1, source_target_pairs={{0,6},{1,7},{2,4},{3,5},{4,2},{5,3},{6,0},{7,1},{8,14},{9,15},{10,... | collective-permute-start | bytes 3080 | tf_op jit(solution)/shard_map/ppermute | solution.py:30
  195.1 6.9 %collective-permute-start.43 = (f32[2,128]{1,0:T(2,128)S(1)}, f32[2,128]{1,0:T(2,128)S(1)}, u32[]{:S(2)}, u32[]{:S(2)}) collective-permute-start(f32[2,128]{1,0:T(2,128)S(1)} %fusion.120), channel_id=1, source_target_pairs={{0,4},{1,5},{2,6},{3,7},{4,0},{5,1},{6,2},{7,3},{8,12},{9,13},{10,... | collective-permute-start | bytes 3080 | tf_op jit(solution)/shard_map/ppermute | solution.py:30
  202.7 0.9 collective-permute-done.43
  203.6 2.0 collective-permute-done.42
  205.7 0.9 fusion.39
  (130 shorter events, 12.2 us)
Async XLA Ops:
  1.4 20.8 %copy-start.3 = (bf16[128,640]{1,0:T(8,128)(2,1)S(1)}, bf16[128,640]{1,0:T(8,128)(2,1)}, u32[]{:S(2)}) copy-start(bf16[128,640]{1,0:T(8,128)(2,1)} %param.11) | copy-start | bytes 491524
  2.5 14.3 %collective-permute-start.1 = (bf16[144,640]{1,0:T(8,128)(2,1)S(1)}, bf16[144,640]{1,0:T(8,128)(2,1)S(1)}, u32[]{:S(2)}, u32[]{:S(2)}) collective-permute-start(bf16[144,640]{1,0:T(8,128)(2,1)S(1)} %maximum_maximum_fusion), channel_id=1, source_target_pairs={{0,4},{1,5},{2,6},{3,7},{4,0},{5,1},{6,2},{7,3},{8,12},{9,13},{10,... | collective-permute-start | bytes 552968 | tf_op jit(solution)/shard_map/ppermute | solution.py:30
  6.6 10.2 %collective-permute-start = (bf16[144,640]{1,0:T(8,128)(2,1)S(1)}, bf16[144,640]{1,0:T(8,128)(2,1)S(1)}, u32[]{:S(2)}, u32[]{:S(2)}) collective-permute-start(bf16[144,640]{1,0:T(8,128)(2,1)S(1)} %maximum_maximum_fusion), channel_id=1, source_target_pairs={{0,2},{1,3},{2,0},{3,1},{4,6},{5,7},{6,4},{7,5},{8,10},{9,11},{10,... | collective-permute-start | bytes 552968 | tf_op jit(solution)/shard_map/ppermute | solution.py:30
  8.2 12.2 %collective-permute-start.2 = (bf16[144,640]{1,0:T(8,128)(2,1)S(1)}, bf16[144,640]{1,0:T(8,128)(2,1)S(1)}, u32[]{:S(2)}, u32[]{:S(2)}) collective-permute-start(bf16[144,640]{1,0:T(8,128)(2,1)S(1)} %maximum_maximum_fusion), channel_id=1, source_target_pairs={{0,6},{1,7},{2,4},{3,5},{4,2},{5,3},{6,0},{7,1},{8,14},{9,15},{10,... | collective-permute-start | bytes 552968 | tf_op jit(solution)/shard_map/ppermute | solution.py:30
  21.0 1.2 collective-permute-start.3
  22.6 9.4 %collective-permute-start.23 = (bf16[128,640]{1,0:T(8,128)(2,1)S(1)}, bf16[128,640]{1,0:T(8,128)(2,1)S(1)}, u32[]{:S(2)}, u32[]{:S(2)}) collective-permute-start(bf16[128,640]{1,0:T(8,128)(2,1)S(1)} %get-tuple-element.4), channel_id=1, source_target_pairs={{0,6},{1,7},{2,4},{3,5},{4,2},{5,3},{6,0},{7,1},{8,14},{9,15},{10,... | collective-permute-start | bytes 491528 | tf_op jit(solution)/shard_map/ppermute | solution.py:30
  25.2 16.1 %collective-permute-start.22 = (bf16[128,640]{1,0:T(8,128)(2,1)S(1)}, bf16[128,640]{1,0:T(8,128)(2,1)S(1)}, u32[]{:S(2)}, u32[]{:S(2)}) collective-permute-start(bf16[128,640]{1,0:T(8,128)(2,1)S(1)} %get-tuple-element.4), channel_id=1, source_target_pairs={{0,4},{1,5},{2,6},{3,7},{4,0},{5,1},{6,2},{7,3},{8,12},{9,13},{10,... | collective-permute-start | bytes 491528 | tf_op jit(solution)/shard_map/ppermute | solution.py:30
  28.2 13.2 %collective-permute-start.21 = (bf16[128,640]{1,0:T(8,128)(2,1)S(1)}, bf16[128,640]{1,0:T(8,128)(2,1)S(1)}, u32[]{:S(2)}, u32[]{:S(2)}) collective-permute-start(bf16[128,640]{1,0:T(8,128)(2,1)S(1)} %get-tuple-element.4), channel_id=1, source_target_pairs={{0,2},{1,3},{2,0},{3,1},{4,6},{5,7},{6,4},{7,5},{8,10},{9,11},{10,... | collective-permute-start | bytes 491528 | tf_op jit(solution)/shard_map/ppermute | solution.py:30
  29.0 15.5 %collective-permute-start.4 = (bf16[128,640]{1,0:T(8,128)(2,1)S(1)}, bf16[128,640]{1,0:T(8,128)(2,1)S(1)}, u32[]{:S(2)}, u32[]{:S(2)}) collective-permute-start(bf16[128,640]{1,0:T(8,128)(2,1)S(1)} %get-tuple-element.61), channel_id=1, source_target_pairs={{0,8},{8,0},{16,24},{24,16},{1,9},{9,1},{17,25},{25,17},{2,10},{10... | collective-permute-start | bytes 491528 | tf_op jit(solution)/shard_map/ppermute | solution.py:27
  30.6 14.5 %collective-permute-start.6 = (bf16[128,640]{1,0:T(8,128)(2,1)S(1)}, bf16[128,640]{1,0:T(8,128)(2,1)S(1)}, u32[]{:S(2)}, u32[]{:S(2)}) collective-permute-start(bf16[128,640]{1,0:T(8,128)(2,1)S(1)} %get-tuple-element.62), channel_id=1, source_target_pairs={{0,24},{8,16},{16,8},{24,0},{1,25},{9,17},{17,9},{25,1},{2,26},{10... | collective-permute-start | bytes 491528 | tf_op jit(solution)/shard_map/ppermute | solution.py:27
  32.1 13.0 %collective-permute-start.5 = (bf16[128,640]{1,0:T(8,128)(2,1)S(1)}, bf16[128,640]{1,0:T(8,128)(2,1)S(1)}, u32[]{:S(2)}, u32[]{:S(2)}) collective-permute-start(bf16[128,640]{1,0:T(8,128)(2,1)S(1)} %get-tuple-element.60), channel_id=1, source_target_pairs={{0,16},{8,24},{16,0},{24,8},{1,17},{9,25},{17,1},{25,9},{2,18},{10... | collective-permute-start | bytes 491528 | tf_op jit(solution)/shard_map/ppermute | solution.py:27
  41.5 8.0 %collective-permute-start.26 = (bf16[128,640]{1,0:T(8,128)(2,1)S(1)}, bf16[128,640]{1,0:T(8,128)(2,1)S(1)}, u32[]{:S(2)}, u32[]{:S(2)}) collective-permute-start(bf16[128,640]{1,0:T(8,128)(2,1)S(1)} %get-tuple-element.64), channel_id=1, source_target_pairs={{0,24},{8,16},{16,8},{24,0},{1,25},{9,17},{17,9},{25,1},{2,26},{10... | collective-permute-start | bytes 491528 | tf_op jit(solution)/shard_map/ppermute | solution.py:27
  44.0 8.1 %collective-permute-start.25 = (bf16[128,640]{1,0:T(8,128)(2,1)S(1)}, bf16[128,640]{1,0:T(8,128)(2,1)S(1)}, u32[]{:S(2)}, u32[]{:S(2)}) collective-permute-start(bf16[128,640]{1,0:T(8,128)(2,1)S(1)} %get-tuple-element.65), channel_id=1, source_target_pairs={{0,16},{8,24},{16,0},{24,8},{1,17},{9,25},{17,1},{25,9},{2,18},{10... | collective-permute-start | bytes 491528 | tf_op jit(solution)/shard_map/ppermute | solution.py:27
  44.5 7.7 %collective-permute-start.24 = (bf16[128,640]{1,0:T(8,128)(2,1)S(1)}, bf16[128,640]{1,0:T(8,128)(2,1)S(1)}, u32[]{:S(2)}, u32[]{:S(2)}) collective-permute-start(bf16[128,640]{1,0:T(8,128)(2,1)S(1)} %get-tuple-element.66), channel_id=1, source_target_pairs={{0,8},{8,0},{16,24},{24,16},{1,9},{9,1},{17,25},{25,17},{2,10},{10... | collective-permute-start | bytes 491528 | tf_op jit(solution)/shard_map/ppermute | solution.py:27
  45.1 7.3 %collective-permute-start.7 = (bf16[512,640]{1,0:T(8,128)(2,1)S(1)}, bf16[512,640]{1,0:T(8,128)(2,1)S(1)}, u32[]{:S(2)}, u32[]{:S(2)}) collective-permute-start(bf16[512,640]{1,0:T(8,128)(2,1)S(1)} %pad_maximum_fusion.2), channel_id=1, source_target_pairs={{0,1},{1,0},{2,3},{3,2},{4,5},{5,4},{6,7},{7,6},{8,9},{9,8},{10,11... | collective-permute-start | bytes 1966088 | tf_op jit(solution)/shard_map/ppermute | solution.py:33
  52.3 2.3 %collective-permute-start.27 = (bf16[512,640]{1,0:T(8,128)(2,1)S(1)}, bf16[512,640]{1,0:T(8,128)(2,1)}, u32[]{:S(2)}, u32[]{:S(2)}) collective-permute-start(bf16[512,640]{1,0:T(8,128)(2,1)S(1)} %pad_maximum_fusion.4), channel_id=1, source_target_pairs={{0,1},{1,0},{2,3},{3,2},{4,5},{5,4},{6,7},{7,6},{8,9},{9,8},{10,11... | collective-permute-start | bytes 1966088 | tf_op jit(solution)/shard_map/ppermute | solution.py:33
  54.6 8.5 %slice-start = ((s8[4423680]{0:T(1024)(128)(4,1)}), s8[4194304]{0:T(1024)(128)(4,1)S(1)}, s32[]{:S(2)}) async-start(s8[4423680]{0:T(1024)(128)(4,1)} %bitcast.203), calls=%async_computation | async-start | bytes 8388608
  56.4 6.7 %slice-start.1 = ((s8[4423680]{0:T(1024)(128)(4,1)}), s8[229376]{0:T(1024)(128)(4,1)S(1)}, s32[]{:S(2)}) async-start(s8[4423680]{0:T(1024)(128)(4,1)} %bitcast.203), calls=%async_computation.1 | async-start | bytes 458752
  61.5 13.4 %collective-permute-start.28 = (bf16[2,64,1728]{2,1,0:T(8,128)(2,1)S(1)}, bf16[2,64,1728]{2,1,0:T(8,128)(2,1)S(1)}, u32[]{:S(2)}, u32[]{:S(2)}) collective-permute-start(bf16[2,64,1728]{2,1,0:T(8,128)(2,1)S(1)} %pad_maximum_fusion.8), channel_id=1, source_target_pairs={{0,8},{8,0},{16,24},{24,16},{1,9},{9,1},{17,25},{25,17},{2,10},{10... | collective-permute-start | bytes 1327112 | tf_op jit(solution)/shard_map/ppermute | solution.py:27
  66.0 19.6 %collective-permute-start.30 = (bf16[2,64,1728]{2,1,0:T(8,128)(2,1)S(1)}, bf16[2,64,1728]{2,1,0:T(8,128)(2,1)S(1)}, u32[]{:S(2)}, u32[]{:S(2)}) collective-permute-start(bf16[2,64,1728]{2,1,0:T(8,128)(2,1)S(1)} %slice.418), channel_id=1, source_target_pairs={{0,16},{8,24},{16,0},{24,8},{1,17},{9,25},{17,1},{25,9},{2,18},{10... | collective-permute-start | bytes 1327112 | tf_op jit(solution)/shard_map/ppermute | solution.py:27
  66.8 17.2 %collective-permute-start.8 = (bf16[2,64,1728]{2,1,0:T(8,128)(2,1)S(1)}, bf16[2,64,1728]{2,1,0:T(8,128)(2,1)S(1)}, u32[]{:S(2)}, u32[]{:S(2)}) collective-permute-start(bf16[2,64,1728]{2,1,0:T(8,128)(2,1)S(1)} %pad_maximum_fusion.5), channel_id=1, source_target_pairs={{0,8},{8,0},{16,24},{24,16},{1,9},{9,1},{17,25},{25,17},{2,10},{10... | collective-permute-start | bytes 1327112 | tf_op jit(solution)/shard_map/ppermute | solution.py:27
  68.1 26.8 %collective-permute-start.10 = (bf16[2,64,1728]{2,1,0:T(8,128)(2,1)S(1)}, bf16[2,64,1728]{2,1,0:T(8,128)(2,1)S(1)}, u32[]{:S(2)}, u32[]{:S(2)}) collective-permute-start(bf16[2,64,1728]{2,1,0:T(8,128)(2,1)S(1)} %slice.399), channel_id=1, source_target_pairs={{0,16},{8,24},{16,0},{24,8},{1,17},{9,25},{17,1},{25,9},{2,18},{10... | collective-permute-start | bytes 1327112 | tf_op jit(solution)/shard_map/ppermute | solution.py:27
  75.0 19.2 %collective-permute-start.29 = (bf16[1,64,1728]{2,1,0:T(8,128)(2,1)S(1)}, bf16[1,64,1728]{2,1,0:T(8,128)(2,1)S(1)}, u32[]{:S(2)}, u32[]{:S(2)}) collective-permute-start(bf16[1,64,1728]{2,1,0:T(8,128)(2,1)S(1)} %fusion.20), channel_id=1, source_target_pairs={{0,16},{8,24},{16,0},{24,8},{1,17},{9,25},{17,1},{25,9},{2,18},{10... | collective-permute-start | bytes 663560 | tf_op jit(solution)/shard_map/ppermute | solution.py:27
  84.0 13.9 %collective-permute-start.9 = (bf16[1,64,1728]{2,1,0:T(8,128)(2,1)S(1)}, bf16[1,64,1728]{2,1,0:T(8,128)(2,1)S(1)}, u32[]{:S(2)}, u32[]{:S(2)}) collective-permute-start(bf16[1,64,1728]{2,1,0:T(8,128)(2,1)S(1)} %fusion.26), channel_id=1, source_target_pairs={{0,16},{8,24},{16,0},{24,8},{1,17},{9,25},{17,1},{25,9},{2,18},{10... | collective-permute-start | bytes 663560 | tf_op jit(solution)/shard_map/ppermute | solution.py:27
  94.3 6.6 %collective-permute-start.31 = (bf16[1,64,1728]{2,1,0:T(8,128)(2,1)S(1)}, bf16[1,64,1728]{2,1,0:T(8,128)(2,1)S(1)}, u32[]{:S(2)}, u32[]{:S(2)}) collective-permute-start(bf16[1,64,1728]{2,1,0:T(8,128)(2,1)S(1)} %get-tuple-element.40), channel_id=1, source_target_pairs={{0,8},{8,0},{16,24},{24,16},{1,9},{9,1},{17,25},{25,17},{2,10},{10... | collective-permute-start | bytes 663560 | tf_op jit(solution)/shard_map/ppermute | solution.py:27
  98.1 7.2 %collective-permute-start.11 = (bf16[1,64,1728]{2,1,0:T(8,128)(2,1)S(1)}, bf16[1,64,1728]{2,1,0:T(8,128)(2,1)S(1)}, u32[]{:S(2)}, u32[]{:S(2)}) collective-permute-start(bf16[1,64,1728]{2,1,0:T(8,128)(2,1)S(1)} %get-tuple-element.42), channel_id=1, source_target_pairs={{0,8},{8,0},{16,24},{24,16},{1,9},{9,1},{17,25},{25,17},{2,10},{10... | collective-permute-start | bytes 663560 | tf_op jit(solution)/shard_map/ppermute | solution.py:27
  106.1 8.6 %collective-permute-start.12 = (bf16[1,64,1728]{2,1,0:T(8,128)(2,1)S(1)}, bf16[1,64,1728]{2,1,0:T(8,128)(2,1)S(1)}, u32[]{:S(2)}, u32[]{:S(2)}) collective-permute-start(bf16[1,64,1728]{2,1,0:T(8,128)(2,1)S(1)} %get-tuple-element.70), channel_id=1, source_target_pairs={{0,8},{8,0},{16,24},{24,16},{1,9},{9,1},{17,25},{25,17},{2,10},{10... | collective-permute-start | bytes 663560 | tf_op jit(solution)/shard_map/ppermute | solution.py:27
  106.7 16.0 %collective-permute-start.33 = (bf16[1,64,1728]{2,1,0:T(8,128)(2,1)S(1)}, bf16[1,64,1728]{2,1,0:T(8,128)(2,1)S(1)}, u32[]{:S(2)}, u32[]{:S(2)}) collective-permute-start(bf16[1,64,1728]{2,1,0:T(8,128)(2,1)S(1)} %get-tuple-element.67), channel_id=1, source_target_pairs={{0,16},{8,24},{16,0},{24,8},{1,17},{9,25},{17,1},{25,9},{2,18},{10... | collective-permute-start | bytes 663560 | tf_op jit(solution)/shard_map/ppermute | solution.py:27
  108.2 13.6 %collective-permute-start.32 = (bf16[1,64,1728]{2,1,0:T(8,128)(2,1)S(1)}, bf16[1,64,1728]{2,1,0:T(8,128)(2,1)S(1)}, u32[]{:S(2)}, u32[]{:S(2)}) collective-permute-start(bf16[1,64,1728]{2,1,0:T(8,128)(2,1)S(1)} %get-tuple-element.68), channel_id=1, source_target_pairs={{0,8},{8,0},{16,24},{24,16},{1,9},{9,1},{17,25},{25,17},{2,10},{10... | collective-permute-start | bytes 663560 | tf_op jit(solution)/shard_map/ppermute | solution.py:27
  109.0 11.2 %collective-permute-start.13 = (bf16[1,64,1728]{2,1,0:T(8,128)(2,1)S(1)}, bf16[1,64,1728]{2,1,0:T(8,128)(2,1)S(1)}, u32[]{:S(2)}, u32[]{:S(2)}) collective-permute-start(bf16[1,64,1728]{2,1,0:T(8,128)(2,1)S(1)} %get-tuple-element.69), channel_id=1, source_target_pairs={{0,16},{8,24},{16,0},{24,8},{1,17},{9,25},{17,1},{25,9},{2,18},{10... | collective-permute-start | bytes 663560 | tf_op jit(solution)/shard_map/ppermute | solution.py:27
  114.7 26.6 %collective-permute-start.15 = (bf16[2,64,1728]{2,1,0:T(8,128)(2,1)S(1)}, bf16[2,64,1728]{2,1,0:T(8,128)(2,1)S(1)}, u32[]{:S(2)}, u32[]{:S(2)}) collective-permute-start(bf16[2,64,1728]{2,1,0:T(8,128)(2,1)S(1)} %pad_maximum_fusion.7), channel_id=1, source_target_pairs={{0,16},{8,24},{16,0},{24,8},{1,17},{9,25},{17,1},{25,9},{2,18},{10... | collective-permute-start | bytes 1327112 | tf_op jit(solution)/shard_map/ppermute | solution.py:27
  120.3 21.1 %collective-permute-start.14 = (bf16[2,64,1728]{2,1,0:T(8,128)(2,1)S(1)}, bf16[2,64,1728]{2,1,0:T(8,128)(2,1)S(1)}, u32[]{:S(2)}, u32[]{:S(2)}) collective-permute-start(bf16[2,64,1728]{2,1,0:T(8,128)(2,1)S(1)} %pad_maximum_fusion.6), channel_id=1, source_target_pairs={{0,8},{8,0},{16,24},{24,16},{1,9},{9,1},{17,25},{25,17},{2,10},{10... | collective-permute-start | bytes 1327112 | tf_op jit(solution)/shard_map/ppermute | solution.py:27
  121.9 15.6 %collective-permute-start.35 = (bf16[2,64,1728]{2,1,0:T(8,128)(2,1)S(1)}, bf16[2,64,1728]{2,1,0:T(8,128)(2,1)S(1)}, u32[]{:S(2)}, u32[]{:S(2)}) collective-permute-start(bf16[2,64,1728]{2,1,0:T(8,128)(2,1)S(1)} %pad_maximum_fusion.10), channel_id=1, source_target_pairs={{0,16},{8,24},{16,0},{24,8},{1,17},{9,25},{17,1},{25,9},{2,18},{10... | collective-permute-start | bytes 1327112 | tf_op jit(solution)/shard_map/ppermute | solution.py:27
  122.7 14.7 %collective-permute-start.34 = (bf16[2,64,1728]{2,1,0:T(8,128)(2,1)S(1)}, bf16[2,64,1728]{2,1,0:T(8,128)(2,1)S(1)}, u32[]{:S(2)}, u32[]{:S(2)}) collective-permute-start(bf16[2,64,1728]{2,1,0:T(8,128)(2,1)S(1)} %pad_maximum_fusion.9), channel_id=1, source_target_pairs={{0,8},{8,0},{16,24},{24,16},{1,9},{9,1},{17,25},{25,17},{2,10},{10... | collective-permute-start | bytes 1327112 | tf_op jit(solution)/shard_map/ppermute | solution.py:27
  137.6 3.9 %slice-start.2 = ((s8[4423680]{0:T(1024)(128)(4,1)}), s8[4194304]{0:T(1024)(128)(4,1)S(1)}, s32[]{:S(2)}) async-start(s8[4423680]{0:T(1024)(128)(4,1)} %bitcast.205), calls=%async_computation.2 | async-start | bytes 8388608
  137.6 3.9 %slice-start.3 = ((s8[4423680]{0:T(1024)(128)(4,1)}), s8[229376]{0:T(1024)(128)(4,1)S(1)}, s32[]{:S(2)}) async-start(s8[4423680]{0:T(1024)(128)(4,1)} %bitcast.205), calls=%async_computation.3 | async-start | bytes 458752
  141.3 5.7 %collective-permute-start.36 = (bf16[512,640]{1,0:T(8,128)(2,1)}, bf16[512,640]{1,0:T(8,128)(2,1)S(1)}, u32[]{:S(2)}, u32[]{:S(2)}) collective-permute-start(bf16[512,640]{1,0:T(8,128)(2,1)} %select_convert_fusion), channel_id=1, source_target_pairs={{0,1},{1,0},{2,3},{3,2},{4,5},{5,4},{6,7},{7,6},{8,9},{9,8},{10,11... | collective-permute-start | bytes 1966088 | tf_op jit(solution)/shard_map/ppermute | solution.py:33
  144.1 1.5 copy-start
  146.5 4.3 %collective-permute-start.16 = (bf16[512,640]{1,0:T(8,128)(2,1)}, bf16[512,640]{1,0:T(8,128)(2,1)}, u32[]{:S(2)}, u32[]{:S(2)}) collective-permute-start(bf16[512,640]{1,0:T(8,128)(2,1)} %select_convert_fusion.1), channel_id=1, source_target_pairs={{0,1},{1,0},{2,3},{3,2},{4,5},{5,4},{6,7},{7,6},{8,9},{9,8},{10,11... | collective-permute-start | bytes 1966088 | tf_op jit(solution)/shard_map/ppermute | solution.py:33
  147.0 3.8 %copy-start.1 = (f32[512,1280]{1,0:T(8,128)S(1)}, f32[512,1280]{1,0:T(8,128)}, u32[]{:S(2)}) copy-start(f32[512,1280]{1,0:T(8,128)} %copy-done) | copy-start | bytes 7864324
  147.3 8.4 %collective-permute-start.37 = (bf16[128,640]{1,0:T(8,128)(2,1)S(1)}, bf16[128,640]{1,0:T(8,128)(2,1)S(1)}, u32[]{:S(2)}, u32[]{:S(2)}) collective-permute-start(bf16[128,640]{1,0:T(8,128)(2,1)S(1)} %get-tuple-element.47), channel_id=1, source_target_pairs={{0,2},{1,3},{2,0},{3,1},{4,6},{5,7},{6,4},{7,5},{8,10},{9,11},{10,... | collective-permute-start | bytes 491528 | tf_op jit(solution)/shard_map/ppermute | solution.py:30
  147.4 11.0 %collective-permute-start.39 = (bf16[128,640]{1,0:T(8,128)(2,1)S(1)}, bf16[128,640]{1,0:T(8,128)(2,1)S(1)}, u32[]{:S(2)}, u32[]{:S(2)}) collective-permute-start(bf16[128,640]{1,0:T(8,128)(2,1)S(1)} %get-tuple-element.48), channel_id=1, source_target_pairs={{0,6},{1,7},{2,4},{3,5},{4,2},{5,3},{6,0},{7,1},{8,14},{9,15},{10,... | collective-permute-start | bytes 491528 | tf_op jit(solution)/shard_map/ppermute | solution.py:30
  149.9 23.6 %collective-permute-start.38 = (bf16[128,640]{1,0:T(8,128)(2,1)S(1)}, bf16[128,640]{1,0:T(8,128)(2,1)S(1)}, u32[]{:S(2)}, u32[]{:S(2)}) collective-permute-start(bf16[128,640]{1,0:T(8,128)(2,1)S(1)} %get-tuple-element.49), channel_id=1, source_target_pairs={{0,4},{1,5},{2,6},{3,7},{4,0},{5,1},{6,2},{7,3},{8,12},{9,13},{10,... | collective-permute-start | bytes 491528 | tf_op jit(solution)/shard_map/ppermute | solution.py:30
  152.1 32.8 %copy-start.2 = (bf16[128,640]{1,0:T(8,128)(2,1)S(1)}, bf16[128,640]{1,0:T(8,128)(2,1)}, u32[]{:S(2)}) copy-start(bf16[128,640]{1,0:T(8,128)(2,1)} %param.6) | copy-start | bytes 491524
  152.2 22.0 %collective-permute-start.17 = (bf16[128,640]{1,0:T(8,128)(2,1)S(1)}, bf16[128,640]{1,0:T(8,128)(2,1)S(1)}, u32[]{:S(2)}, u32[]{:S(2)}) collective-permute-start(bf16[128,640]{1,0:T(8,128)(2,1)S(1)} %get-tuple-element.52), channel_id=1, source_target_pairs={{0,2},{1,3},{2,0},{3,1},{4,6},{5,7},{6,4},{7,5},{8,10},{9,11},{10,... | collective-permute-start | bytes 491528 | tf_op jit(solution)/shard_map/ppermute | solution.py:30
  153.2 21.0 %collective-permute-start.19 = (bf16[128,640]{1,0:T(8,128)(2,1)S(1)}, bf16[128,640]{1,0:T(8,128)(2,1)S(1)}, u32[]{:S(2)}, u32[]{:S(2)}) collective-permute-start(bf16[128,640]{1,0:T(8,128)(2,1)S(1)} %get-tuple-element.53), channel_id=1, source_target_pairs={{0,6},{1,7},{2,4},{3,5},{4,2},{5,3},{6,0},{7,1},{8,14},{9,15},{10,... | collective-permute-start | bytes 491528 | tf_op jit(solution)/shard_map/ppermute | solution.py:30
  155.7 28.4 %collective-permute-start.18 = (bf16[128,640]{1,0:T(8,128)(2,1)S(1)}, bf16[128,640]{1,0:T(8,128)(2,1)S(1)}, u32[]{:S(2)}, u32[]{:S(2)}) collective-permute-start(bf16[128,640]{1,0:T(8,128)(2,1)S(1)} %get-tuple-element.54), channel_id=1, source_target_pairs={{0,4},{1,5},{2,6},{3,7},{4,0},{5,1},{6,2},{7,3},{8,12},{9,13},{10,... | collective-permute-start | bytes 491528 | tf_op jit(solution)/shard_map/ppermute | solution.py:30
  173.5 11.3 %collective-permute-start.40 = (bf16[128,640]{1,0:T(8,128)(2,1)S(1)}, bf16[128,640]{1,0:T(8,128)(2,1)S(1)}, u32[]{:S(2)}, u32[]{:S(2)}) collective-permute-start(bf16[128,640]{1,0:T(8,128)(2,1)S(1)} %fusion.60), channel_id=1, source_target_pairs={{0,0},{1,1},{2,8},{3,9},{4,16},{5,17},{6,24},{7,25},{8,2},{9,3},{1... | collective-permute-start | bytes 491528 | tf_op jit(solution)/shard_map/ppermute | solution.py:40
  184.2 0.7 collective-permute-start.20
  186.1 1.2 collective-permute-start.41
  187.4 15.3 %collective-permute-start.44 = (f32[2,128]{1,0:T(2,128)S(1)}, f32[2,128]{1,0:T(2,128)S(1)}, u32[]{:S(2)}, u32[]{:S(2)}) collective-permute-start(f32[2,128]{1,0:T(2,128)S(1)} %fusion.120), channel_id=1, source_target_pairs={{0,6},{1,7},{2,4},{3,5},{4,2},{5,3},{6,0},{7,1},{8,14},{9,15},{10,... | collective-permute-start | bytes 3080 | tf_op jit(solution)/shard_map/ppermute | solution.py:30
  195.1 8.5 %collective-permute-start.43 = (f32[2,128]{1,0:T(2,128)S(1)}, f32[2,128]{1,0:T(2,128)S(1)}, u32[]{:S(2)}, u32[]{:S(2)}) collective-permute-start(f32[2,128]{1,0:T(2,128)S(1)} %fusion.120), channel_id=1, source_target_pairs={{0,4},{1,5},{2,6},{3,7},{4,0},{5,1},{6,2},{7,3},{8,12},{9,13},{10,... | collective-permute-start | bytes 3080 | tf_op jit(solution)/shard_map/ppermute | solution.py:30
  202.1 3.6 %collective-permute-start.42 = (f32[2,128]{1,0:T(2,128)S(1)}, f32[2,128]{1,0:T(2,128)S(1)}, u32[]{:S(2)}, u32[]{:S(2)}) collective-permute-start(f32[2,128]{1,0:T(2,128)S(1)} %fusion.120), channel_id=1, source_target_pairs={{0,2},{1,3},{2,0},{3,1},{4,6},{5,7},{6,4},{7,5},{8,10},{9,11},{10,... | collective-permute-start | bytes 3080 | tf_op jit(solution)/shard_map/ppermute | solution.py:30

commit v2 on v1

v2 whole, which is shorter than its diff:
```python
import jax
import jax.numpy as jnp
from jax import lax
from jax.experimental.layout import Layout, with_layout_constraint
from jax.sharding import PartitionSpec as P

epsilon = 1e-06
BF = jnp.bfloat16
F32 = jnp.float32


def gelu_and_slope(value):
    coeff = 0.7978845608028654
    inner = coeff * (value + 0.044715 * value * value * value)
    tangent = jnp.tanh(inner)
    half = 0.5 * (1.0 + tangent)
    slope = half + 0.5 * value * (1.0 - tangent * tangent) * coeff * (
        1.0 + 3.0 * 0.044715 * value * value
    )
    return value * half, slope


def dot(a, b):
    return jnp.dot(a, b, preferred_element_type=F32)


def dot_t(a, b):
    return lax.dot_general(a, b, (((1,), (1,)), ((), ())), preferred_element_type=F32)


def after(value, *events):
    return lax.optimization_barrier((value, *events))[0]


def row_major(value):
    return with_layout_constraint(value, Layout(major_to_minor=(0, 1)))


def flips_of(size):
    return [1 << bit for bit in range(size.bit_length() - 1)]


def reduce_steps(move, sides, orders, events=None):
    sides = [dict(enumerate(side)) for side in sides]
    marks = ()
    for flips in zip(*orders):
        came = []
        for side, flip in zip(sides, flips):
            sent = [j for j in sorted(side) if j & flip]
            sent = jnp.stack([side.pop(j).astype(BF) for j in sent])
            if marks and events:
                sent = after(sent, *events(marks))
            came.append(move(sent, flip))
        if len(came) > 1:
            came = lax.optimization_barrier(tuple(came))
        marks = marks + (tuple(came),)
        for side, got in zip(sides, came):
            for place, j in enumerate(sorted(side)):
                side[j] = side[j].astype(F32) + got[place].astype(F32)
    return [side[0] for side in sides], marks


def gather_steps(move, values, orders, events=None):
    sides = [{0: value} for value in values]
    marks = ()
    for flips in zip(*orders):
        came = []
        for side, flip in zip(sides, flips):
            sent = jnp.stack([side[j] for j in sorted(side)])
            if marks and events:
                sent = after(sent, *events(marks))
            came.append(move(sent, flip))
        if len(came) > 1:
            came = lax.optimization_barrier(tuple(came))
        marks = marks + (tuple(came),)
        for side, got, flip in zip(sides, came, flips):
            for place, j in enumerate(sorted(side)):
                side[j ^ flip] = got[place]
    return [[side[j] for j in range(len(side))] for side in sides], marks


def make_body(rows, cols):
    depth = cols // 2
    assert depth == rows and rows & (rows - 1) == 0
    up = flips_of(rows)
    down = up[::-1]

    def over_row(value, flip):
        return lax.ppermute(value, "row", [(i, i ^ flip) for i in range(rows)])

    def over_z(value, flip):
        return lax.ppermute(value, "col", [(i, i ^ (2 * flip)) for i in range(cols)])

    def over_core(value):
        return lax.ppermute(value, "col", [(i, i ^ 1) for i in range(cols)])

    def scatter_rows(share, tok_rows, events=None):
        half = tok_rows // 2
        parts = share.reshape(rows, tok_rows, share.shape[1])
        sides = [[parts[j, :half] for j in range(rows)], [parts[j, half:] for j in range(rows)]]
        sums, marks = reduce_steps(over_row, sides, [up, down], events)
        return jnp.concatenate(sums, axis=0), marks

    def gather_rows(value, events=None):
        half = value.shape[0] // 2
        sides, marks = gather_steps(over_row, [value[:half], value[half:]], [up, down], events)
        return jnp.concatenate([s[j] for j in range(rows) for s in sides], axis=0), marks

    def gather_z(value):
        sides, _ = gather_steps(over_z, [value], [down])
        return jnp.stack(sides[0])

    def body(hidden_states, clip_lengths, modulation, fc1_weight, fc2_weight, out_grad):
        tok_rows, width = hidden_states.shape
        clip_count = modulation.shape[0]
        full_width = width * cols
        r = lax.axis_index("row")
        c = lax.axis_index("col")
        z, core = c // 2, c % 2

        places = lax.broadcasted_iota(jnp.int32, (tok_rows, 1), 0)
        member, end = [], 0
        for i in range(clip_count):
            begin, end = end, end + clip_lengths[0, i]
            member.append(((places >= begin) & (places < end)).astype(F32))
        live = sum(member)

        def per_token(vectors):
            return sum(member[i] * vectors[i : i + 1].astype(F32) for i in range(clip_count))

        x_here = hidden_states.astype(F32)
        g_here = out_grad.astype(F32)
        scale_here = per_token(modulation[:, 1])
        gate_here = per_token(modulation[:, 2])

        last = tok_rows + 2 * clip_count
        packed = jnp.concatenate(
            [
                hidden_states,
                modulation[:, 0],
                modulation[:, 1],
                jnp.zeros((-last % 16, width), BF),
            ],
            axis=0,
        )
        with jax.named_scope("x_over_z"):
            chunks = jnp.stack([packed] + [over_z(packed, i) for i in range(1, depth)])
        z_grad = (live * gate_here * g_here).astype(BF)

        def own_and_other(weight):
            own = lax.dynamic_slice_in_dim(weight, core * width, width, 1)
            other = lax.dynamic_slice_in_dim(weight, (1 - core) * width, width, 1)
            return row_major(own), row_major(other)

        first_own, first_other = own_and_other(fc1_weight.T)
        second_own, second_other = own_and_other(fc2_weight)
        chunks = after(chunks, first_own, first_other)

        x_part = chunks[:, :tok_rows].astype(F32)
        mean_part = jnp.mean(x_part, axis=(0, 2))
        spread = x_part - mean_part[None, :, None]
        square_part = jnp.sum(spread * spread, axis=(0, 2))
        theirs = over_core(jnp.stack([mean_part, square_part]))
        centre = 0.5 * (mean_part + theirs[0])
        gap = mean_part - theirs[0]
        square = square_part + theirs[1] + gap * gap * (full_width / 4)
        inverse = lax.rsqrt(square / full_width + epsilon)[:, None]
        centre = centre[:, None]
        normed = (x_here - centre) * inverse

        def message(j):
            chunk = lax.dynamic_index_in_dim(chunks, z ^ j, 0, keepdims=False)
            shift = per_token(chunk[tok_rows : tok_rows + clip_count])
            scale = per_token(chunk[tok_rows + clip_count : last])
            x = chunk[:tok_rows].astype(F32)
            return ((x - centre) * inverse * (1.0 + scale) + shift).astype(BF)

        with jax.named_scope("modulated_over_row"):
            arrived = [message(r)] + [over_row(message(r ^ i), i) for i in range(1, rows)]
        arrived[-1] = after(arrived[-1], second_own, second_other)
        mod_own = lax.optimization_barrier(jnp.concatenate(arrived, axis=0))
        mod_other = over_core(mod_own)

        pre_share = dot_t(mod_own, first_own) + dot_t(mod_other, first_other)
        pre_share = row_major(pre_share.astype(BF))
        z_grad = after(z_grad, pre_share)
        with jax.named_scope("z_grad_over_z"):
            z_came = [over_z(z_grad, i) for i in range(1, depth)]
            z_chunks = jnp.stack([z_grad] + z_came)
        with jax.named_scope("pre_act_scatter"):
            pre_act, scatter_marks = scatter_rows(pre_share, tok_rows)
        z_chunks = after(z_chunks, *scatter_marks[0])

        def z_pick(i):
            return lax.dynamic_index_in_dim(z_chunks, r ^ z ^ i, 0, keepdims=False)

        with jax.named_scope("z_grad_over_row"):
            z_arrived = [over_row(z_pick(i), i) for i in range(1, rows)]
        z_own = jnp.concatenate([z_pick(0)] + z_arrived, axis=0)
        z_own = lax.optimization_barrier(z_own)
        z_other = over_core(z_own)

        act_share = dot_t(z_own, second_own) + dot_t(z_other, second_other)
        act_share = row_major(act_share.astype(BF))
        act_share = after(act_share, *scatter_marks[-1])
        activated, slope = gelu_and_slope(pre_act)
        with jax.named_scope("activated_gather"):
            act_all, gather_marks = gather_rows(activated.astype(BF))
        with jax.named_scope("act_grad_scatter"):
            act_grad, act_marks = scatter_rows(act_share, tok_rows, lambda marks: gather_marks[0])
        pre_grad = after((act_grad * slope).astype(BF), *gather_marks[-1])

        def core_sum(given, kept):
            kept = lax.optimization_barrier(kept)
            both = kept + over_core(given.astype(BF)).astype(F32)
            return both.reshape(rows, tok_rows, width)

        def to_rows(both):
            both = both.astype(BF)
            return jnp.stack([both[0]] + [over_row(both[i], i) for i in range(1, rows)])

        def groups_of(parts):
            return [
                lax.dynamic_index_in_dim(parts, r ^ z ^ i, 0, keepdims=False) for i in range(depth)
            ]

        def to_depth(groups, events=None):
            (total,), marks = reduce_steps(over_z, [groups], [up], events)
            return total, marks

        act_all = after(act_all, act_share)
        out_both = core_sum(dot(act_all, second_other), dot(act_all, second_own))
        out_both = out_both.astype(BF)
        with jax.named_scope("projected_home"):
            projected, depth_marks = to_depth(groups_of(to_rows(after(out_both, *act_marks[-1]))))
        with jax.named_scope("pre_grad_gather"):
            pre_grad_all, _ = gather_rows(pre_grad, lambda marks: (out_both,))
        in_both = core_sum(dot(pre_grad_all, first_other), dot(pre_grad_all, first_own))
        with jax.named_scope("in_grad_to_row"):
            in_groups = groups_of(to_rows(in_both))
        first_sum = jnp.zeros((tok_rows,), F32)
        second_sum = jnp.zeros((tok_rows,), F32)
        for i in range(depth):
            share = in_groups[i].astype(F32)
            chunk = chunks[i]
            scaled = 1.0 + per_token(chunk[tok_rows + clip_count : last])
            share = share * scaled
            first_sum = first_sum + jnp.sum(share, axis=1)
            deviation = chunk[:tok_rows].astype(F32) - centre
            second_sum = second_sum + jnp.sum(share * deviation, axis=1)
        sums = jnp.stack([first_sum, second_sum * inverse[:, 0]])
        with jax.named_scope("norm_sums"):
            sums = sums + over_core(sums)
            for flip in up:
                sums = sums + over_z(sums, flip)
        with jax.named_scope("in_grad_over_z"):
            mod_in_grad, _ = to_depth([after(in_groups[0], *depth_marks[0]), *in_groups[1:]], lambda marks: (sums,))
        projected = after(projected, mod_in_grad)
        norm_grad = mod_in_grad * (1.0 + scale_here)
        first_mean = (sums[0] / full_width)[:, None]
        second_mean = (sums[1] / full_width)[:, None]
        input_grad = (
            live * (g_here + inverse * (norm_grad - first_mean - normed * second_mean))
        ).astype(BF)
        block_out = (live * (x_here + gate_here * projected)).astype(BF)

        def per_clip(values):
            return jnp.stack([jnp.sum(member[i] * values, axis=0) for i in range(clip_count)])

        modulation_grad = jnp.stack(
            [per_clip(mod_in_grad), per_clip(mod_in_grad * normed), per_clip(projected * g_here)],
            axis=1,
        )
        return block_out, input_grad, modulation_grad

    return body


def solution(mesh):
    rows, cols = mesh.shape["row"], mesh.shape["col"]
    return jax.shard_map(
        make_body(rows, cols),
        mesh=mesh,
        in_specs=(
            P("row", "col"),
            P("row", None),
            P("row", None, "col"),
            P("row", "col"),
            P("col", "row"),
            P("row", "col"),
        ),
        out_specs=(P("row", "col"), P("row", "col"), P("row", None, "col")),
        check_vma=False,
    )
```

time: 210 us -> 177 us (0.84); the launches traced: 207 us -> 177 us
  waiting for transfers between devices: 113 us -> 85.8 us
  starting transfers between devices: 61.1 us -> 46.8 us
  local copies, waits for them, and re-layouts: 2.94 us -> 13 us
    ppermute x15 -> x12, waiting for transfers between devices: 47.5 us -> 26.5 us  [over_z(): return lax.ppermute(value, 'col', [(i, i ^ 2 * flip) for i in range(cols)])]
    ppermute x15 -> x12, starting transfers between devices: 34.8 us -> 16.3 us  [over_z(): return lax.ppermute(value, 'col', [(i, i ^ 2 * flip) for i in range(cols)])]
    dot_general x2 -> x8, matrix products: 5.1 us -> 13.1 us  [the longest x4 6.56 us: dot_t(): lax.dot_general(a, b, (((1,), (1,)), ((), ())), preferred_element_type=F32)]
    dynamic_slice x0 -> x3, local copies, waits for them, and re-layouts: none -> 7.52 us  [the longest x2 7.49 us: own_and_other(): other = lax.dynamic_slice_in_dim(weight, (1 - core) * width, width, 1)]
    reshape x2 -> x0, matrix products: 7.42 us -> none  [reduce_scatter_rows(): parts = share.reshape(rows, tok_rows, share.shape[1])]
    ppermute x22 -> x28, starting transfers between devices: 24.2 us -> 30.1 us  [over_row(): return lax.ppermute(value, 'row', [(i, i ^ flip) for i in range(rows)])]
    ppermute x22 -> x28, waiting for transfers between devices: 61.5 us -> 55.9 us  [over_row(): return lax.ppermute(value, 'row', [(i, i ^ flip) for i in range(rows)])]
  transfers between devices with their start and end apart: 45 -> 46, of which waited for: 23 -> 31; matrix products, arithmetic and copies ran while one was open for 8% -> 16% of each run, Pallas kernels for 0% -> 0%
where the time goes in v2:
time: 177 us
  waiting for transfers between devices  85.8 us (48%)
  starting transfers between devices  46.8 us (26%)
  other arithmetic  15.3 us (9%)
  matrix products  13.1 us (7%)
  local copies, waits for them, and re-layouts  13 us (7%)
  between operations  2.63 us (1%)
    ppermute x28, waiting for transfers between devices, over_row(): return lax.ppermute(value, 'row', [(i, i ^ flip) for i in range(rows)])  55.9 us
    ppermute x28, starting transfers between devices, over_row(): return lax.ppermute(value, 'row', [(i, i ^ flip) for i in range(rows)])  30.1 us
    ppermute x12, waiting for transfers between devices, over_z(): return lax.ppermute(value, 'col', [(i, i ^ 2 * flip) for i in range(cols)])  26.5 us
    ppermute x12, starting transfers between devices, over_z(): return lax.ppermute(value, 'col', [(i, i ^ 2 * flip) for i in range(cols)])  16.3 us
    dynamic_slice x2, local copies, waits for them, and re-layouts, own_and_other(): other = lax.dynamic_slice_in_dim(weight, (1 - core) * width, width, 1)  7.49 us
    dot_general x4, matrix products, dot_t(): lax.dot_general(a, b, (((1,), (1,)), ((), ())), preferred_element_type=F32)  6.56 us
    dot_general x4, matrix products, dot(): return jnp.dot(a, b, preferred_element_type=F32)  6.56 us
  transfers between devices with their start and end apart: 46, of which 31 were waited for; matrix products, arithmetic and copies ran while one was open for 16% of the time, Pallas kernels for 0%

profile of v2, /device:TPU:0, one launch (start us, length us, event | category | flops | bytes accessed | tf_op | source)
XLA Modules:
  0.0 176.6 jit_solution(3212831903961418886)
XLA Ops:
  1.4 1.0 maximum_maximum_fusion
  2.4 5.1 %collective-permute-start.2 = (bf16[144,640]{1,0:T(8,128)(2,1)S(1)}, bf16[144,640]{1,0:T(8,128)(2,1)S(1)}, u32[]{:S(2)}, u32[]{:S(2)}) collective-permute-start(bf16[144,640]{1,0:T(8,128)(2,1)S(1)} %maximum_maximum_fusion), channel_id=1, source_target_pairs={{0,6},{1,7},{2,4},{3,5},{4,2},{5,3},{6,0},{7,1},{8,14},{9,15},{10,... | collective-permute-start | bytes 552968 | tf_op jit(solution)/shard_map/x_over_z/ppermute | solution.py:92
  9.0 1.3 fusion.92
  13.0 2.7 %dynamic-slice_bitcast_fusion = (bf16[1728,640]{1,0:T(8,128)(2,1)S(1)}, bf16[1728,640]{1,0:T(8,128)(2,1)S(1)}) fusion(bf16[1280,1728]{0,1:T(8,128)(2,1)} %param.9, s32[]{:T(128)S(6)} %select_n.53, s32[]{:T(128)S(6)} %select_n.52), kind=kLoop, calls=%fused_computation.2 | loop fusion | bytes 8847368 | tf_op jit(solution)/shard_map/dynamic_slice | solution.py:152
  15.8 7.4 %collective-permute-done.1 = bf16[144,640]{1,0:T(8,128)(2,1)S(1)} collective-permute-done((bf16[144,640]{1,0:T(8,128)(2,1)S(1)}, bf16[144,640]{1,0:T(8,128)(2,1)S(1)}, u32[]{:S(2)}, u32[]{:S(2)}) %collective-permute-start.1) | collective-permute-done | bytes 184352 | tf_op jit(solution)/shard_map/x_over_z/ppermute | solution.py:92
  23.9 1.2 pad_maximum_fusion.1
  27.2 2.5 %collective-permute-start.6 = (bf16[128,640]{1,0:T(8,128)(2,1)S(1)}, bf16[128,640]{1,0:T(8,128)(2,1)S(1)}, u32[]{:S(2)}, u32[]{:S(2)}) collective-permute-start(bf16[128,640]{1,0:T(8,128)(2,1)S(1)} %get-tuple-element.135), channel_id=1, source_target_pairs={{0,24},{8,16},{16,8},{24,0},{1,25},{9,17},{17,9},{25,1},{2,26},{10... | collective-permute-start | bytes 491528 | tf_op jit(solution)/shard_map/modulated_over_row/ppermute | solution.py:89
  31.2 4.8 %constant_dynamic-slice_fusion.16 = (bf16[1728,640]{1,0:T(8,128)(2,1)}, bf16[1728,640]{1,0:T(8,128)(2,1)}) fusion(bf16[1728,1280]{1,0:T(8,128)(2,1)} %param.10, s32[]{:T(128)S(6)} %select_n.53, s32[]{:T(128)S(6)} %select_n.52), kind=kLoop, calls=%fused_computation.165 | loop fusion | bytes 8847368 | tf_op jit(solution)/shard_map/dynamic_slice | solution.py:152
  36.0 1.9 %collective-permute-done.5 = bf16[128,640]{1,0:T(8,128)(2,1)S(1)} collective-permute-done((bf16[128,640]{1,0:T(8,128)(2,1)S(1)}, bf16[128,640]{1,0:T(8,128)(2,1)S(1)}, u32[]{:S(2)}, u32[]{:S(2)}) %collective-permute-start.5) | collective-permute-done | bytes 163872 | tf_op jit(solution)/shard_map/modulated_over_row/ppermute | solution.py:89
  38.2 2.1 %collective-permute-done.7 = bf16[512,640]{1,0:T(8,128)(2,1)S(1)} collective-permute-done((bf16[512,640]{1,0:T(8,128)(2,1)S(1)}, bf16[512,640]{1,0:T(8,128)(2,1)S(1)}, u32[]{:S(2)}, u32[]{:S(2)}) %collective-permute-start.7) | collective-permute-done | bytes 655392 | tf_op jit(solution)/shard_map/ppermute | solution.py:95
  40.3 1.6 fusion.93
  41.9 1.7 add_convert_fusion.1
  43.7 1.2 copy-done.5
  46.5 1.5 collective-permute-start.8
  48.0 1.2 collective-permute-start.9
  49.2 2.5 %collective-permute-start.18 = (bf16[128,640]{1,0:T(8,128)(2,1)S(1)}, bf16[128,640]{1,0:T(8,128)(2,1)S(1)}, u32[]{:S(2)}, u32[]{:S(2)}) collective-permute-start(bf16[128,640]{1,0:T(8,128)(2,1)S(1)} %get-tuple-element.44), channel_id=1, source_target_pairs={{0,6},{1,7},{2,4},{3,5},{4,2},{5,3},{6,0},{7,1},{8,14},{9,15},{10,... | collective-permute-start | bytes 491528 | tf_op jit(solution)/shard_map/z_grad_over_z/ppermute | solution.py:92
  51.7 1.9 %collective-permute-start.16 = (bf16[128,640]{1,0:T(8,128)(2,1)S(1)}, bf16[128,640]{1,0:T(8,128)(2,1)S(1)}, u32[]{:S(2)}, u32[]{:S(2)}) collective-permute-start(bf16[128,640]{1,0:T(8,128)(2,1)S(1)} %get-tuple-element.44), channel_id=1, source_target_pairs={{0,2},{1,3},{2,0},{3,1},{4,6},{5,7},{6,4},{7,5},{8,10},{9,11},{10,... | collective-permute-start | bytes 491528 | tf_op jit(solution)/shard_map/z_grad_over_z/ppermute | solution.py:92
  53.6 5.8 %collective-permute-done.8 = bf16[2,64,1728]{2,1,0:T(8,128)(2,1)} collective-permute-done((bf16[2,64,1728]{2,1,0:T(8,128)(2,1)}, bf16[2,64,1728]{2,1,0:T(8,128)(2,1)}, u32[]{:S(2)}, u32[]{:S(2)}) %collective-permute-start.8) | collective-permute-done | bytes 442400 | tf_op jit(solution)/shard_map/pre_act_scatter/ppermute | solution.py:89
  59.4 1.2 collective-permute-done.9
  60.6 1.4 add_convert_fusion.6
  62.0 1.3 collective-permute-start.10
  64.7 1.1 collective-permute-start.21
  65.8 1.2 collective-permute-start.20
  67.0 1.3 collective-permute-start.19
  68.3 3.1 %collective-permute-done.10 = bf16[1,64,1728]{2,1,0:T(8,128)(2,1)S(1)} collective-permute-done((bf16[1,64,1728]{2,1,0:T(8,128)(2,1)S(1)}, bf16[1,64,1728]{2,1,0:T(8,128)(2,1)S(1)}, u32[]{:S(2)}, u32[]{:S(2)}) %collective-permute-start.10) | collective-permute-done | bytes 221216 | tf_op jit(solution)/shard_map/pre_act_scatter/ppermute | solution.py:89
  71.8 1.4 add_bitcast_fusion.3
  75.2 1.4 collective-permute-done.20
  76.7 2.2 %collective-permute-done.19 = bf16[128,640]{1,0:T(8,128)(2,1)S(1)} collective-permute-done((bf16[128,640]{1,0:T(8,128)(2,1)S(1)}, bf16[128,640]{1,0:T(8,128)(2,1)S(1)}, u32[]{:S(2)}, u32[]{:S(2)}) %collective-permute-start.19) | collective-permute-done | bytes 163872 | tf_op jit(solution)/shard_map/z_grad_over_row/ppermute | solution.py:89
  79.0 2.4 %collective-permute-done.12 = bf16[1,64,1728]{2,1,0:T(8,128)(2,1)S(1)} collective-permute-done((bf16[1,64,1728]{2,1,0:T(8,128)(2,1)S(1)}, bf16[1,64,1728]{2,1,0:T(8,128)(2,1)S(1)}, u32[]{:S(2)}, u32[]{:S(2)}) %collective-permute-start.12) | collective-permute-done | bytes 221216 | tf_op jit(solution)/shard_map/activated_gather/ppermute | solution.py:89
  83.1 1.6 fusion.94
  84.7 1.6 add_convert_fusion
  86.5 1.5 collective-permute-start.24
  88.0 1.2 collective-permute-start.25
  89.2 5.8 %collective-permute-done.14 = bf16[2,64,1728]{2,1,0:T(8,128)(2,1)S(1)} collective-permute-done((bf16[2,64,1728]{2,1,0:T(8,128)(2,1)S(1)}, bf16[2,64,1728]{2,1,0:T(8,128)(2,1)S(1)}, u32[]{:S(2)}, u32[]{:S(2)}) %collective-permute-start.14) | collective-permute-done | bytes 442400 | tf_op jit(solution)/shard_map/activated_gather/ppermute | solution.py:89
  95.0 0.9 collective-permute-done.15
  96.0 1.6 fusion.95
  97.6 4.9 %collective-permute-done.24 = bf16[2,64,1728]{2,1,0:T(8,128)(2,1)S(1)} collective-permute-done((bf16[2,64,1728]{2,1,0:T(8,128)(2,1)S(1)}, bf16[2,64,1728]{2,1,0:T(8,128)(2,1)S(1)}, u32[]{:S(2)}, u32[]{:S(2)}) %collective-permute-start.24) | collective-permute-done | bytes 442400 | tf_op jit(solution)/shard_map/act_grad_scatter/ppermute | solution.py:89
  102.6 1.3 collective-permute-start.26
  104.6 1.8 %convolution_convert_fusion.1 = bf16[512,640]{1,0:T(8,128)(2,1)S(1)} fusion(bf16[512,1728]{1,0:T(8,128)(2,1)S(1)} %bitcast_dynamic-update-slice_fusion.6, bf16[1728,640]{1,0:T(8,128)(2,1)S(1)} %copy-done.3), kind=kOutput, calls=%fused_computation.9 | convolution fusion | flops 1132789760 | bytes 4636672 | tf_op jit(solution)/shard_map/dot_general | solution.py:24
  106.5 2.2 %collective-permute-done.26 = bf16[1,64,1728]{2,1,0:T(8,128)(2,1)S(1)} collective-permute-done((bf16[1,64,1728]{2,1,0:T(8,128)(2,1)S(1)}, bf16[1,64,1728]{2,1,0:T(8,128)(2,1)S(1)}, u32[]{:S(2)}, u32[]{:S(2)}) %collective-permute-start.26) | collective-permute-done | bytes 221216 | tf_op jit(solution)/shard_map/act_grad_scatter/ppermute | solution.py:89
  108.7 1.2 collective-permute-done.27
  112.7 2.0 %collective-permute-start.30 = (bf16[128,640]{1,0:T(8,128)(2,1)S(1)}, bf16[128,640]{1,0:T(8,128)(2,1)S(1)}, u32[]{:S(2)}, u32[]{:S(2)}) collective-permute-start(bf16[128,640]{1,0:T(8,128)(2,1)S(1)} %get-tuple-element.145), channel_id=1, source_target_pairs={{0,24},{8,16},{16,8},{24,0},{1,25},{9,17},{17,9},{25,1},{2,26},{10... | collective-permute-start | bytes 491528 | tf_op jit(solution)/shard_map/projected_home/ppermute | solution.py:89
  116.2 2.8 %collective-permute-done.33 = bf16[1,64,1728]{2,1,0:T(8,128)(2,1)S(1)} collective-permute-done((bf16[1,64,1728]{2,1,0:T(8,128)(2,1)S(1)}, bf16[1,64,1728]{2,1,0:T(8,128)(2,1)S(1)}, u32[]{:S(2)}, u32[]{:S(2)}) %collective-permute-start.33) | collective-permute-done | bytes 221216 | tf_op jit(solution)/shard_map/pre_grad_gather/ppermute | solution.py:89
  119.0 3.0 %collective-permute-done.34 = bf16[1,64,1728]{2,1,0:T(8,128)(2,1)S(1)} collective-permute-done((bf16[1,64,1728]{2,1,0:T(8,128)(2,1)S(1)}, bf16[1,64,1728]{2,1,0:T(8,128)(2,1)S(1)}, u32[]{:S(2)}, u32[]{:S(2)}) %collective-permute-start.34) | collective-permute-done | bytes 221216 | tf_op jit(solution)/shard_map/pre_grad_gather/ppermute | solution.py:89
  122.6 1.5 collective-permute-start.36
  124.1 9.2 %collective-permute-done.35 = bf16[2,64,1728]{2,1,0:T(8,128)(2,1)S(1)} collective-permute-done((bf16[2,64,1728]{2,1,0:T(8,128)(2,1)S(1)}, bf16[2,64,1728]{2,1,0:T(8,128)(2,1)S(1)}, u32[]{:S(2)}, u32[]{:S(2)}) %collective-permute-start.35) | collective-permute-done | bytes 442400 | tf_op jit(solution)/shard_map/pre_grad_gather/ppermute | solution.py:89
  133.4 1.6 convolution_convert_fusion
  135.2 1.6 fusion.96
  137.3 1.1 collective-permute-start.40
  138.5 1.1 collective-permute-start.39
  139.6 1.3 collective-permute-start.38
  141.1 4.3 %collective-permute-done.40 = bf16[128,640]{1,0:T(8,128)(2,1)S(1)} collective-permute-done((bf16[128,640]{1,0:T(8,128)(2,1)S(1)}, bf16[128,640]{1,0:T(8,128)(2,1)S(1)}, u32[]{:S(2)}, u32[]{:S(2)}) %collective-permute-start.40) | collective-permute-done | bytes 163872 | tf_op jit(solution)/shard_map/in_grad_to_row/ppermute | solution.py:89
  145.4 2.6 %collective-permute-done.39 = bf16[128,640]{1,0:T(8,128)(2,1)S(1)} collective-permute-done((bf16[128,640]{1,0:T(8,128)(2,1)S(1)}, bf16[128,640]{1,0:T(8,128)(2,1)S(1)}, u32[]{:S(2)}, u32[]{:S(2)}) %collective-permute-start.39) | collective-permute-done | bytes 163872 | tf_op jit(solution)/shard_map/in_grad_to_row/ppermute | solution.py:89
  149.0 0.9 collective-permute-done.31
  150.0 1.4 collective-permute-start.32
  151.4 1.8 %collective-permute-start.43 = (f32[2,128]{1,0:T(2,128)S(1)}, f32[2,128]{1,0:T(2,128)S(1)}, u32[]{:S(2)}, u32[]{:S(2)}) collective-permute-start(f32[2,128]{1,0:T(2,128)S(1)} %fusion.87), channel_id=1, source_target_pairs={{0,2},{1,3},{2,0},{3,1},{4,6},{5,7},{6,4},{7,5},{8,10},{9,11},{10,... | collective-permute-start | bytes 3080 | tf_op jit(solution)/shard_map/norm_sums/ppermute | solution.py:92
  153.6 2.3 %collective-permute-done.43 = f32[2,128]{1,0:T(2,128)S(1)} collective-permute-done((f32[2,128]{1,0:T(2,128)S(1)}, f32[2,128]{1,0:T(2,128)S(1)}, u32[]{:S(2)}, u32[]{:S(2)}) %collective-permute-start.43) | collective-permute-done | bytes 1056 | tf_op jit(solution)/shard_map/norm_sums/ppermute | solution.py:92
  155.9 2.4 %collective-permute-start.44 = (f32[2,128]{1,0:T(2,128)S(1)}, f32[2,128]{1,0:T(2,128)S(1)}, u32[]{:S(2)}, u32[]{:S(2)}) collective-permute-start(f32[2,128]{1,0:T(2,128)S(1)} %fusion.113), channel_id=1, source_target_pairs={{0,4},{1,5},{2,6},{3,7},{4,0},{5,1},{6,2},{7,3},{8,12},{9,13},{10,... | collective-permute-start | bytes 3080 | tf_op jit(solution)/shard_map/norm_sums/ppermute | solution.py:92
  158.4 1.7 collective-permute-done.32
  160.1 1.3 collective-permute-done.44
  161.3 3.9 %collective-permute-done.41 = bf16[2,128,640]{2,1,0:T(8,128)(2,1)S(1)} collective-permute-done((bf16[2,128,640]{2,1,0:T(8,128)(2,1)S(1)}, bf16[2,128,640]{2,1,0:T(8,128)(2,1)S(1)}, u32[]{:S(2)}, u32[]{:S(2)}) %collective-permute-start.41) | collective-permute-done | bytes 327712 | tf_op jit(solution)/shard_map/in_grad_over_z/ppermute | solution.py:92
  165.4 8.5 %collective-permute-done.45 = bf16[1,128,640]{2,1,0:T(8,128)(2,1)S(1)} collective-permute-done((bf16[1,128,640]{2,1,0:T(8,128)(2,1)S(1)}, bf16[1,128,640]{2,1,0:T(8,128)(2,1)S(1)}, u32[]{:S(2)}, u32[]{:S(2)}) %collective-permute-start.45) | collective-permute-done | bytes 163872 | tf_op jit(solution)/shard_map/in_grad_over_z/ppermute | solution.py:92
  173.9 0.9 fusion.20
  174.9 1.0 multiply_reduce_fusion.3
  (141 shorter events, 24.7 us)
Async XLA Ops:
  2.4 13.4 %collective-permute-start.2 = (bf16[144,640]{1,0:T(8,128)(2,1)S(1)}, bf16[144,640]{1,0:T(8,128)(2,1)S(1)}, u32[]{:S(2)}, u32[]{:S(2)}) collective-permute-start(bf16[144,640]{1,0:T(8,128)(2,1)S(1)} %maximum_maximum_fusion), channel_id=1, source_target_pairs={{0,6},{1,7},{2,4},{3,5},{4,2},{5,3},{6,0},{7,1},{8,14},{9,15},{10,... | collective-permute-start | bytes 552968 | tf_op jit(solution)/shard_map/x_over_z/ppermute | solution.py:92
  7.6 15.6 %collective-permute-start.1 = (bf16[144,640]{1,0:T(8,128)(2,1)S(1)}, bf16[144,640]{1,0:T(8,128)(2,1)S(1)}, u32[]{:S(2)}, u32[]{:S(2)}) collective-permute-start(bf16[144,640]{1,0:T(8,128)(2,1)S(1)} %maximum_maximum_fusion), channel_id=1, source_target_pairs={{0,4},{1,5},{2,6},{3,7},{4,0},{5,1},{6,2},{7,3},{8,12},{9,13},{10,... | collective-permute-start | bytes 552968 | tf_op jit(solution)/shard_map/x_over_z/ppermute | solution.py:92
  7.6 15.6 %collective-permute-start = (bf16[144,640]{1,0:T(8,128)(2,1)S(1)}, bf16[144,640]{1,0:T(8,128)(2,1)S(1)}, u32[]{:S(2)}, u32[]{:S(2)}) collective-permute-start(bf16[144,640]{1,0:T(8,128)(2,1)S(1)} %maximum_maximum_fusion), channel_id=1, source_target_pairs={{0,2},{1,3},{2,0},{3,1},{4,6},{5,7},{6,4},{7,5},{8,10},{9,11},{10,... | collective-permute-start | bytes 552968 | tf_op jit(solution)/shard_map/x_over_z/ppermute | solution.py:92
  13.0 2.7 %copy-start = (bf16[128,640]{1,0:T(8,128)(2,1)S(1)}, bf16[128,640]{1,0:T(8,128)(2,1)}, u32[]{:S(2)}) copy-start(bf16[128,640]{1,0:T(8,128)(2,1)} %param.6) | copy-start | bytes 491524
  15.7 24.6 %copy-start.1 = (bf16[1728,640]{1,0:T(8,128)(2,1)}, bf16[1728,640]{1,0:T(8,128)(2,1)S(1)}, u32[]{:S(2)}) copy-start(bf16[1728,640]{1,0:T(8,128)(2,1)S(1)} %get-tuple-element.120) | copy-start | bytes 6635524
  23.2 0.7 copy-start.7
  23.2 0.7 copy-start.8
  23.9 5.8 %copy-start.6 = (bf16[128,640]{1,0:T(8,128)(2,1)S(1)}, bf16[128,640]{1,0:T(8,128)(2,1)}, u32[]{:S(2)}) copy-start(bf16[128,640]{1,0:T(8,128)(2,1)} %param.11) | copy-start | bytes 491524
  25.6 1.2 collective-permute-start.3
  27.2 8.8 %collective-permute-start.6 = (bf16[128,640]{1,0:T(8,128)(2,1)S(1)}, bf16[128,640]{1,0:T(8,128)(2,1)S(1)}, u32[]{:S(2)}, u32[]{:S(2)}) collective-permute-start(bf16[128,640]{1,0:T(8,128)(2,1)S(1)} %get-tuple-element.135), channel_id=1, source_target_pairs={{0,24},{8,16},{16,8},{24,0},{1,25},{9,17},{17,9},{25,1},{2,26},{10... | collective-permute-start | bytes 491528 | tf_op jit(solution)/shard_map/modulated_over_row/ppermute | solution.py:89
  30.1 7.8 %collective-permute-start.5 = (bf16[128,640]{1,0:T(8,128)(2,1)S(1)}, bf16[128,640]{1,0:T(8,128)(2,1)S(1)}, u32[]{:S(2)}, u32[]{:S(2)}) collective-permute-start(bf16[128,640]{1,0:T(8,128)(2,1)S(1)} %get-tuple-element.137), channel_id=1, source_target_pairs={{0,16},{8,24},{16,0},{24,8},{1,17},{9,25},{17,1},{25,9},{2,18},{10... | collective-permute-start | bytes 491528 | tf_op jit(solution)/shard_map/modulated_over_row/ppermute | solution.py:89
  30.7 7.3 %collective-permute-start.4 = (bf16[128,640]{1,0:T(8,128)(2,1)S(1)}, bf16[128,640]{1,0:T(8,128)(2,1)S(1)}, u32[]{:S(2)}, u32[]{:S(2)}) collective-permute-start(bf16[128,640]{1,0:T(8,128)(2,1)S(1)} %get-tuple-element.136), channel_id=1, source_target_pairs={{0,8},{8,0},{16,24},{24,16},{1,9},{9,1},{17,25},{25,17},{2,10},{10... | collective-permute-start | bytes 491528 | tf_op jit(solution)/shard_map/modulated_over_row/ppermute | solution.py:89
  38.1 2.2 %collective-permute-start.7 = (bf16[512,640]{1,0:T(8,128)(2,1)S(1)}, bf16[512,640]{1,0:T(8,128)(2,1)S(1)}, u32[]{:S(2)}, u32[]{:S(2)}) collective-permute-start(bf16[512,640]{1,0:T(8,128)(2,1)S(1)} %pad_maximum_fusion.2), channel_id=1, source_target_pairs={{0,1},{1,0},{2,3},{3,2},{4,5},{5,4},{6,7},{7,6},{8,9},{9,8},{10,11... | collective-permute-start | bytes 1966088 | tf_op jit(solution)/shard_map/ppermute | solution.py:95
  43.6 1.2 copy-start.5
  46.5 12.9 %collective-permute-start.8 = (bf16[2,64,1728]{2,1,0:T(8,128)(2,1)}, bf16[2,64,1728]{2,1,0:T(8,128)(2,1)}, u32[]{:S(2)}, u32[]{:S(2)}) collective-permute-start(bf16[2,64,1728]{2,1,0:T(8,128)(2,1)} %pad_maximum_fusion.7), channel_id=1, source_target_pairs={{0,8},{8,0},{16,24},{24,16},{1,9},{9,1},{17,25},{25,17},{2,10},{10... | collective-permute-start | bytes 1327112 | tf_op jit(solution)/shard_map/pre_act_scatter/ppermute | solution.py:89
  48.0 12.6 %collective-permute-start.9 = (bf16[2,64,1728]{2,1,0:T(8,128)(2,1)}, bf16[2,64,1728]{2,1,0:T(8,128)(2,1)}, u32[]{:S(2)}, u32[]{:S(2)}) collective-permute-start(bf16[2,64,1728]{2,1,0:T(8,128)(2,1)} %stack.209), channel_id=1, source_target_pairs={{0,16},{8,24},{16,0},{24,8},{1,17},{9,25},{17,1},{25,9},{2,18},{10... | collective-permute-start | bytes 1327112 | tf_op jit(solution)/shard_map/pre_act_scatter/ppermute | solution.py:89
  49.2 14.8 %collective-permute-start.18 = (bf16[128,640]{1,0:T(8,128)(2,1)S(1)}, bf16[128,640]{1,0:T(8,128)(2,1)S(1)}, u32[]{:S(2)}, u32[]{:S(2)}) collective-permute-start(bf16[128,640]{1,0:T(8,128)(2,1)S(1)} %get-tuple-element.44), channel_id=1, source_target_pairs={{0,6},{1,7},{2,4},{3,5},{4,2},{5,3},{6,0},{7,1},{8,14},{9,15},{10,... | collective-permute-start | bytes 491528 | tf_op jit(solution)/shard_map/z_grad_over_z/ppermute | solution.py:92
  51.7 12.8 %collective-permute-start.17 = (bf16[128,640]{1,0:T(8,128)(2,1)S(1)}, bf16[128,640]{1,0:T(8,128)(2,1)S(1)}, u32[]{:S(2)}, u32[]{:S(2)}) collective-permute-start(bf16[128,640]{1,0:T(8,128)(2,1)S(1)} %get-tuple-element.44), channel_id=1, source_target_pairs={{0,4},{1,5},{2,6},{3,7},{4,0},{5,1},{6,2},{7,3},{8,12},{9,13},{10,... | collective-permute-start | bytes 491528 | tf_op jit(solution)/shard_map/z_grad_over_z/ppermute | solution.py:92
  51.7 12.8 %collective-permute-start.16 = (bf16[128,640]{1,0:T(8,128)(2,1)S(1)}, bf16[128,640]{1,0:T(8,128)(2,1)S(1)}, u32[]{:S(2)}, u32[]{:S(2)}) collective-permute-start(bf16[128,640]{1,0:T(8,128)(2,1)S(1)} %get-tuple-element.44), channel_id=1, source_target_pairs={{0,2},{1,3},{2,0},{3,1},{4,6},{5,7},{6,4},{7,5},{8,10},{9,11},{10,... | collective-permute-start | bytes 491528 | tf_op jit(solution)/shard_map/z_grad_over_z/ppermute | solution.py:92
  62.0 9.4 %collective-permute-start.10 = (bf16[1,64,1728]{2,1,0:T(8,128)(2,1)S(1)}, bf16[1,64,1728]{2,1,0:T(8,128)(2,1)S(1)}, u32[]{:S(2)}, u32[]{:S(2)}) collective-permute-start(bf16[1,64,1728]{2,1,0:T(8,128)(2,1)S(1)} %get-tuple-element.131), channel_id=1, source_target_pairs={{0,16},{8,24},{16,0},{24,8},{1,17},{9,25},{17,1},{25,9},{2,18},{10... | collective-permute-start | bytes 663560 | tf_op jit(solution)/shard_map/pre_act_scatter/ppermute | solution.py:89
  63.3 8.5 %collective-permute-start.11 = (bf16[1,64,1728]{2,1,0:T(8,128)(2,1)S(1)}, bf16[1,64,1728]{2,1,0:T(8,128)(2,1)S(1)}, u32[]{:S(2)}, u32[]{:S(2)}) collective-permute-start(bf16[1,64,1728]{2,1,0:T(8,128)(2,1)S(1)} %get-tuple-element.130), channel_id=1, source_target_pairs={{0,8},{8,0},{16,24},{24,16},{1,9},{9,1},{17,25},{25,17},{2,10},{10... | collective-permute-start | bytes 663560 | tf_op jit(solution)/shard_map/pre_act_scatter/ppermute | solution.py:89
  64.7 10.5 %collective-permute-start.21 = (bf16[128,640]{1,0:T(8,128)(2,1)S(1)}, bf16[128,640]{1,0:T(8,128)(2,1)S(1)}, u32[]{:S(2)}, u32[]{:S(2)}) collective-permute-start(bf16[128,640]{1,0:T(8,128)(2,1)S(1)} %get-tuple-element.149), channel_id=1, source_target_pairs={{0,24},{8,16},{16,8},{24,0},{1,25},{9,17},{17,9},{25,1},{2,26},{10... | collective-permute-start | bytes 491528 | tf_op jit(solution)/shard_map/z_grad_over_row/ppermute | solution.py:89
  65.8 10.9 %collective-permute-start.20 = (bf16[128,640]{1,0:T(8,128)(2,1)S(1)}, bf16[128,640]{1,0:T(8,128)(2,1)S(1)}, u32[]{:S(2)}, u32[]{:S(2)}) collective-permute-start(bf16[128,640]{1,0:T(8,128)(2,1)S(1)} %get-tuple-element.150), channel_id=1, source_target_pairs={{0,16},{8,24},{16,0},{24,8},{1,17},{9,25},{17,1},{25,9},{2,18},{10... | collective-permute-start | bytes 491528 | tf_op jit(solution)/shard_map/z_grad_over_row/ppermute | solution.py:89
  67.0 11.8 %collective-permute-start.19 = (bf16[128,640]{1,0:T(8,128)(2,1)S(1)}, bf16[128,640]{1,0:T(8,128)(2,1)S(1)}, u32[]{:S(2)}, u32[]{:S(2)}) collective-permute-start(bf16[128,640]{1,0:T(8,128)(2,1)S(1)} %get-tuple-element.151), channel_id=1, source_target_pairs={{0,8},{8,0},{16,24},{24,16},{1,9},{9,1},{17,25},{25,17},{2,10},{10... | collective-permute-start | bytes 491528 | tf_op jit(solution)/shard_map/z_grad_over_row/ppermute | solution.py:89
  73.6 9.5 %copy-start.3 = (bf16[1728,640]{1,0:T(8,128)(2,1)S(1)}, bf16[1728,640]{1,0:T(8,128)(2,1)}, u32[]{:S(2)}) copy-start(bf16[1728,640]{1,0:T(8,128)(2,1)} %get-tuple-element.118) | copy-start | bytes 6635524
  73.6 7.8 %collective-permute-start.12 = (bf16[1,64,1728]{2,1,0:T(8,128)(2,1)S(1)}, bf16[1,64,1728]{2,1,0:T(8,128)(2,1)S(1)}, u32[]{:S(2)}, u32[]{:S(2)}) collective-permute-start(bf16[1,64,1728]{2,1,0:T(8,128)(2,1)S(1)} %get-tuple-element.156), channel_id=1, source_target_pairs={{0,8},{8,0},{16,24},{24,16},{1,9},{9,1},{17,25},{25,17},{2,10},{10... | collective-permute-start | bytes 663560 | tf_op jit(solution)/shard_map/activated_gather/ppermute | solution.py:89
  74.4 7.0 %collective-permute-start.13 = (bf16[1,64,1728]{2,1,0:T(8,128)(2,1)S(1)}, bf16[1,64,1728]{2,1,0:T(8,128)(2,1)S(1)}, u32[]{:S(2)}, u32[]{:S(2)}) collective-permute-start(bf16[1,64,1728]{2,1,0:T(8,128)(2,1)S(1)} %get-tuple-element.155), channel_id=1, source_target_pairs={{0,16},{8,24},{16,0},{24,8},{1,17},{9,25},{17,1},{25,9},{2,18},{10... | collective-permute-start | bytes 663560 | tf_op jit(solution)/shard_map/activated_gather/ppermute | solution.py:89
  78.9 4.2 %collective-permute-start.22 = (bf16[512,640]{1,0:T(8,128)(2,1)S(1)}, bf16[512,640]{1,0:T(8,128)(2,1)S(1)}, u32[]{:S(2)}, u32[]{:S(2)}) collective-permute-start(bf16[512,640]{1,0:T(8,128)(2,1)S(1)} %pad_maximum_fusion.4), channel_id=1, source_target_pairs={{0,1},{1,0},{2,3},{3,2},{4,5},{5,4},{6,7},{7,6},{8,9},{9,8},{10,11... | collective-permute-start | bytes 1966088 | tf_op jit(solution)/shard_map/ppermute | solution.py:95
  81.5 13.5 %collective-permute-start.14 = (bf16[2,64,1728]{2,1,0:T(8,128)(2,1)S(1)}, bf16[2,64,1728]{2,1,0:T(8,128)(2,1)S(1)}, u32[]{:S(2)}, u32[]{:S(2)}) collective-permute-start(bf16[2,64,1728]{2,1,0:T(8,128)(2,1)S(1)} %pad_maximum_fusion.8), channel_id=1, source_target_pairs={{0,16},{8,24},{16,0},{24,8},{1,17},{9,25},{17,1},{25,9},{2,18},{10... | collective-permute-start | bytes 1327112 | tf_op jit(solution)/shard_map/activated_gather/ppermute | solution.py:89
  82.4 13.5 %collective-permute-start.15 = (bf16[2,64,1728]{2,1,0:T(8,128)(2,1)S(1)}, bf16[2,64,1728]{2,1,0:T(8,128)(2,1)S(1)}, u32[]{:S(2)}, u32[]{:S(2)}) collective-permute-start(bf16[2,64,1728]{2,1,0:T(8,128)(2,1)S(1)} %pad_maximum_fusion.9), channel_id=1, source_target_pairs={{0,8},{8,0},{16,24},{24,16},{1,9},{9,1},{17,25},{25,17},{2,10},{10... | collective-permute-start | bytes 1327112 | tf_op jit(solution)/shard_map/activated_gather/ppermute | solution.py:89
  83.1 1.7 copy-start.4
  86.5 16.0 %collective-permute-start.24 = (bf16[2,64,1728]{2,1,0:T(8,128)(2,1)S(1)}, bf16[2,64,1728]{2,1,0:T(8,128)(2,1)S(1)}, u32[]{:S(2)}, u32[]{:S(2)}) collective-permute-start(bf16[2,64,1728]{2,1,0:T(8,128)(2,1)S(1)} %pad_maximum_fusion.10), channel_id=1, source_target_pairs={{0,8},{8,0},{16,24},{24,16},{1,9},{9,1},{17,25},{25,17},{2,10},{10... | collective-permute-start | bytes 1327112 | tf_op jit(solution)/shard_map/act_grad_scatter/ppermute | solution.py:89
  88.0 14.5 %collective-permute-start.25 = (bf16[2,64,1728]{2,1,0:T(8,128)(2,1)S(1)}, bf16[2,64,1728]{2,1,0:T(8,128)(2,1)S(1)}, u32[]{:S(2)}, u32[]{:S(2)}) collective-permute-start(bf16[2,64,1728]{2,1,0:T(8,128)(2,1)S(1)} %stack.210), channel_id=1, source_target_pairs={{0,16},{8,24},{16,0},{24,8},{1,17},{9,25},{17,1},{25,9},{2,18},{10... | collective-permute-start | bytes 1327112 | tf_op jit(solution)/shard_map/act_grad_scatter/ppermute | solution.py:89
  102.6 6.1 %collective-permute-start.26 = (bf16[1,64,1728]{2,1,0:T(8,128)(2,1)S(1)}, bf16[1,64,1728]{2,1,0:T(8,128)(2,1)S(1)}, u32[]{:S(2)}, u32[]{:S(2)}) collective-permute-start(bf16[1,64,1728]{2,1,0:T(8,128)(2,1)S(1)} %get-tuple-element.49), channel_id=1, source_target_pairs={{0,16},{8,24},{16,0},{24,8},{1,17},{9,25},{17,1},{25,9},{2,18},{10... | collective-permute-start | bytes 663560 | tf_op jit(solution)/shard_map/act_grad_scatter/ppermute | solution.py:89
  103.9 6.0 %collective-permute-start.27 = (bf16[1,64,1728]{2,1,0:T(8,128)(2,1)S(1)}, bf16[1,64,1728]{2,1,0:T(8,128)(2,1)S(1)}, u32[]{:S(2)}, u32[]{:S(2)}) collective-permute-start(bf16[1,64,1728]{2,1,0:T(8,128)(2,1)S(1)} %get-tuple-element.51), channel_id=1, source_target_pairs={{0,8},{8,0},{16,24},{24,16},{1,9},{9,1},{17,25},{25,17},{2,10},{10... | collective-permute-start | bytes 663560 | tf_op jit(solution)/shard_map/act_grad_scatter/ppermute | solution.py:89
  106.4 6.0 %collective-permute-start.23 = (bf16[512,640]{1,0:T(8,128)(2,1)S(1)}, bf16[512,640]{1,0:T(8,128)(2,1)S(1)}, u32[]{:S(2)}, u32[]{:S(2)}) collective-permute-start(bf16[512,640]{1,0:T(8,128)(2,1)S(1)} %convolution_convert_fusion.1), channel_id=1, source_target_pairs={{0,1},{1,0},{2,3},{3,2},{4,5},{5,4},{6,7},{7,6},{8,9},{9,8},{10,11... | collective-permute-start | bytes 1966088 | tf_op jit(solution)/shard_map/ppermute | solution.py:95
  110.7 8.3 %collective-permute-start.33 = (bf16[1,64,1728]{2,1,0:T(8,128)(2,1)S(1)}, bf16[1,64,1728]{2,1,0:T(8,128)(2,1)S(1)}, u32[]{:S(2)}, u32[]{:S(2)}) collective-permute-start(bf16[1,64,1728]{2,1,0:T(8,128)(2,1)S(1)} %get-tuple-element.154), channel_id=1, source_target_pairs={{0,8},{8,0},{16,24},{24,16},{1,9},{9,1},{17,25},{25,17},{2,10},{10... | collective-permute-start | bytes 663560 | tf_op jit(solution)/shard_map/pre_grad_gather/ppermute | solution.py:89
  111.5 10.5 %collective-permute-start.34 = (bf16[1,64,1728]{2,1,0:T(8,128)(2,1)S(1)}, bf16[1,64,1728]{2,1,0:T(8,128)(2,1)S(1)}, u32[]{:S(2)}, u32[]{:S(2)}) collective-permute-start(bf16[1,64,1728]{2,1,0:T(8,128)(2,1)S(1)} %get-tuple-element.153), channel_id=1, source_target_pairs={{0,16},{8,24},{16,0},{24,8},{1,17},{9,25},{17,1},{25,9},{2,18},{10... | collective-permute-start | bytes 663560 | tf_op jit(solution)/shard_map/pre_grad_gather/ppermute | solution.py:89
  112.7 22.4 %collective-permute-start.30 = (bf16[128,640]{1,0:T(8,128)(2,1)S(1)}, bf16[128,640]{1,0:T(8,128)(2,1)S(1)}, u32[]{:S(2)}, u32[]{:S(2)}) collective-permute-start(bf16[128,640]{1,0:T(8,128)(2,1)S(1)} %get-tuple-element.145), channel_id=1, source_target_pairs={{0,24},{8,16},{16,8},{24,0},{1,25},{9,17},{17,9},{25,1},{2,26},{10... | collective-permute-start | bytes 491528 | tf_op jit(solution)/shard_map/projected_home/ppermute | solution.py:89
  114.6 20.4 %collective-permute-start.29 = (bf16[128,640]{1,0:T(8,128)(2,1)S(1)}, bf16[128,640]{1,0:T(8,128)(2,1)S(1)}, u32[]{:S(2)}, u32[]{:S(2)}) collective-permute-start(bf16[128,640]{1,0:T(8,128)(2,1)S(1)} %get-tuple-element.146), channel_id=1, source_target_pairs={{0,16},{8,24},{16,0},{24,8},{1,17},{9,25},{17,1},{25,9},{2,18},{10... | collective-permute-start | bytes 491528 | tf_op jit(solution)/shard_map/projected_home/ppermute | solution.py:89
  115.5 19.6 %collective-permute-start.28 = (bf16[128,640]{1,0:T(8,128)(2,1)S(1)}, bf16[128,640]{1,0:T(8,128)(2,1)S(1)}, u32[]{:S(2)}, u32[]{:S(2)}) collective-permute-start(bf16[128,640]{1,0:T(8,128)(2,1)S(1)} %get-tuple-element.147), channel_id=1, source_target_pairs={{0,8},{8,0},{16,24},{24,16},{1,9},{9,1},{17,25},{25,17},{2,10},{10... | collective-permute-start | bytes 491528 | tf_op jit(solution)/shard_map/projected_home/ppermute | solution.py:89
  122.1 11.3 %copy-start.2 = (bf16[1728,640]{1,0:T(8,128)(2,1)S(1)}, bf16[1728,640]{1,0:T(8,128)(2,1)}, u32[]{:S(2)}) copy-start(bf16[1728,640]{1,0:T(8,128)(2,1)} %copy-done.1) | copy-start | bytes 6635524
  122.1 11.1 %collective-permute-start.35 = (bf16[2,64,1728]{2,1,0:T(8,128)(2,1)S(1)}, bf16[2,64,1728]{2,1,0:T(8,128)(2,1)S(1)}, u32[]{:S(2)}, u32[]{:S(2)}) collective-permute-start(bf16[2,64,1728]{2,1,0:T(8,128)(2,1)S(1)} %get-tuple-element.57), channel_id=1, source_target_pairs={{0,16},{8,24},{16,0},{24,8},{1,17},{9,25},{17,1},{25,9},{2,18},{10... | collective-permute-start | bytes 1327112 | tf_op jit(solution)/shard_map/pre_grad_gather/ppermute | solution.py:89
  122.6 10.7 %collective-permute-start.36 = (bf16[2,64,1728]{2,1,0:T(8,128)(2,1)S(1)}, bf16[2,64,1728]{2,1,0:T(8,128)(2,1)S(1)}, u32[]{:S(2)}, u32[]{:S(2)}) collective-permute-start(bf16[2,64,1728]{2,1,0:T(8,128)(2,1)S(1)} %get-tuple-element.59), channel_id=1, source_target_pairs={{0,8},{8,0},{16,24},{24,16},{1,9},{9,1},{17,25},{25,17},{2,10},{10... | collective-permute-start | bytes 1327112 | tf_op jit(solution)/shard_map/pre_grad_gather/ppermute | solution.py:89
  135.0 2.2 %collective-permute-start.37 = (bf16[512,640]{1,0:T(8,128)(2,1)S(1)}, bf16[512,640]{1,0:T(8,128)(2,1)S(1)}, u32[]{:S(2)}, u32[]{:S(2)}) collective-permute-start(bf16[512,640]{1,0:T(8,128)(2,1)S(1)} %convolution_convert_fusion), channel_id=1, source_target_pairs={{0,1},{1,0},{2,3},{3,2},{4,5},{5,4},{6,7},{7,6},{8,9},{9,8},{10,11... | collective-permute-start | bytes 1966088 | tf_op jit(solution)/shard_map/ppermute | solution.py:95
  137.3 8.1 %collective-permute-start.40 = (bf16[128,640]{1,0:T(8,128)(2,1)S(1)}, bf16[128,640]{1,0:T(8,128)(2,1)S(1)}, u32[]{:S(2)}, u32[]{:S(2)}) collective-permute-start(bf16[128,640]{1,0:T(8,128)(2,1)S(1)} %get-tuple-element.139), channel_id=1, source_target_pairs={{0,24},{8,16},{16,8},{24,0},{1,25},{9,17},{17,9},{25,1},{2,26},{10... | collective-permute-start | bytes 491528 | tf_op jit(solution)/shard_map/in_grad_to_row/ppermute | solution.py:89
  138.5 9.5 %collective-permute-start.39 = (bf16[128,640]{1,0:T(8,128)(2,1)S(1)}, bf16[128,640]{1,0:T(8,128)(2,1)S(1)}, u32[]{:S(2)}, u32[]{:S(2)}) collective-permute-start(bf16[128,640]{1,0:T(8,128)(2,1)S(1)} %get-tuple-element.140), channel_id=1, source_target_pairs={{0,16},{8,24},{16,0},{24,8},{1,17},{9,25},{17,1},{25,9},{2,18},{10... | collective-permute-start | bytes 491528 | tf_op jit(solution)/shard_map/in_grad_to_row/ppermute | solution.py:89
  139.6 8.4 %collective-permute-start.38 = (bf16[128,640]{1,0:T(8,128)(2,1)S(1)}, bf16[128,640]{1,0:T(8,128)(2,1)S(1)}, u32[]{:S(2)}, u32[]{:S(2)}) collective-permute-start(bf16[128,640]{1,0:T(8,128)(2,1)S(1)} %get-tuple-element.141), channel_id=1, source_target_pairs={{0,8},{8,0},{16,24},{24,16},{1,9},{9,1},{17,25},{25,17},{2,10},{10... | collective-permute-start | bytes 491528 | tf_op jit(solution)/shard_map/in_grad_to_row/ppermute | solution.py:89
  141.0 9.0 %collective-permute-start.31 = (bf16[2,128,640]{2,1,0:T(8,128)(2,1)S(1)}, bf16[2,128,640]{2,1,0:T(8,128)(2,1)S(1)}, u32[]{:S(2)}, u32[]{:S(2)}) collective-permute-start(bf16[2,128,640]{2,1,0:T(8,128)(2,1)S(1)} %pad_maximum_fusion.13), channel_id=1, source_target_pairs={{0,2},{1,3},{2,0},{3,1},{4,6},{5,7},{6,4},{7,5},{8,10},{9,11},{10,... | collective-permute-start | bytes 983048 | tf_op jit(solution)/shard_map/projected_home/ppermute | solution.py:92
  148.9 2.5 %collective-permute-start.42 = (f32[2,128]{1,0:T(2,128)S(1)}, f32[2,128]{1,0:T(2,128)S(1)}, u32[]{:S(2)}, u32[]{:S(2)}) collective-permute-start(f32[2,128]{1,0:T(2,128)S(1)} %pad_maximum_fusion.17), channel_id=1, source_target_pairs={{0,1},{1,0},{2,3},{3,2},{4,5},{5,4},{6,7},{7,6},{8,9},{9,8},{10,11... | collective-permute-start | bytes 3080 | tf_op jit(solution)/shard_map/norm_sums/ppermute | solution.py:95
  150.0 10.0 %collective-permute-start.32 = (bf16[1,128,640]{2,1,0:T(8,128)(2,1)S(1)}, bf16[1,128,640]{2,1,0:T(8,128)(2,1)S(1)}, u32[]{:S(2)}, u32[]{:S(2)}) collective-permute-start(bf16[1,128,640]{2,1,0:T(8,128)(2,1)S(1)} %add_convert_fusion.8), channel_id=1, source_target_pairs={{0,4},{1,5},{2,6},{3,7},{4,0},{5,1},{6,2},{7,3},{8,12},{9,13},{10,... | collective-permute-start | bytes 491528 | tf_op jit(solution)/shard_map/projected_home/ppermute | solution.py:92
  151.4 4.5 %collective-permute-start.43 = (f32[2,128]{1,0:T(2,128)S(1)}, f32[2,128]{1,0:T(2,128)S(1)}, u32[]{:S(2)}, u32[]{:S(2)}) collective-permute-start(f32[2,128]{1,0:T(2,128)S(1)} %fusion.87), channel_id=1, source_target_pairs={{0,2},{1,3},{2,0},{3,1},{4,6},{5,7},{6,4},{7,5},{8,10},{9,11},{10,... | collective-permute-start | bytes 3080 | tf_op jit(solution)/shard_map/norm_sums/ppermute | solution.py:92
  153.3 12.0 %collective-permute-start.41 = (bf16[2,128,640]{2,1,0:T(8,128)(2,1)S(1)}, bf16[2,128,640]{2,1,0:T(8,128)(2,1)S(1)}, u32[]{:S(2)}, u32[]{:S(2)}) collective-permute-start(bf16[2,128,640]{2,1,0:T(8,128)(2,1)S(1)} %pad_maximum_fusion.14), channel_id=1, source_target_pairs={{0,2},{1,3},{2,0},{3,1},{4,6},{5,7},{6,4},{7,5},{8,10},{9,11},{10,... | collective-permute-start | bytes 983048 | tf_op jit(solution)/shard_map/in_grad_over_z/ppermute | solution.py:92
  155.9 5.4 %collective-permute-start.44 = (f32[2,128]{1,0:T(2,128)S(1)}, f32[2,128]{1,0:T(2,128)S(1)}, u32[]{:S(2)}, u32[]{:S(2)}) collective-permute-start(f32[2,128]{1,0:T(2,128)S(1)} %fusion.113), channel_id=1, source_target_pairs={{0,4},{1,5},{2,6},{3,7},{4,0},{5,1},{6,2},{7,3},{8,12},{9,13},{10,... | collective-permute-start | bytes 3080 | tf_op jit(solution)/shard_map/norm_sums/ppermute | solution.py:92
  165.3 8.6 %collective-permute-start.45 = (bf16[1,128,640]{2,1,0:T(8,128)(2,1)S(1)}, bf16[1,128,640]{2,1,0:T(8,128)(2,1)S(1)}, u32[]{:S(2)}, u32[]{:S(2)}) collective-permute-start(bf16[1,128,640]{2,1,0:T(8,128)(2,1)S(1)} %fusion.16), channel_id=1, source_target_pairs={{0,4},{1,5},{2,6},{3,7},{4,0},{5,1},{6,2},{7,3},{8,12},{9,13},{10,... | collective-permute-start | bytes 491528 | tf_op jit(solution)/shard_map/in_grad_over_z/ppermute | solution.py:92

commit v3 on v2

--- a/solution.py
+++ b/solution.py
@@ -232,10 +232,11 @@
         out_both = core_sum(dot(act_all, second_other), dot(act_all, second_own))
         out_both = out_both.astype(BF)
         with jax.named_scope("projected_home"):
-            projected, depth_marks = to_depth(groups_of(to_rows(after(out_both, *act_marks[-1]))))
+            out_groups = groups_of(to_rows(after(out_both, *act_marks[-1])))
+            projected, depth_marks = to_depth(out_groups)
         with jax.named_scope("pre_grad_gather"):
             pre_grad_all, _ = gather_rows(pre_grad, lambda marks: (out_both,))
-        in_both = core_sum(dot(pre_grad_all, first_other), dot(pre_grad_all, first_own))
+        in_both = core_sum(dot(pre_grad_all, first_other), dot(after(pre_grad_all, *depth_marks[0]), first_own))
         with jax.named_scope("in_grad_to_row"):
             in_groups = groups_of(to_rows(in_both))
         first_sum = jnp.zeros((tok_rows,), F32)
@@ -251,14 +252,17 @@
         sums = jnp.stack([first_sum, second_sum * inverse[:, 0]])
         with jax.named_scope("norm_sums"):
             sums = sums + over_core(sums)
-            for flip in up:
-                sums = sums + over_z(sums, flip)
+        whole = after(sums, *depth_marks[1])
+        with jax.named_scope("norm_sums"):
+            whole = whole + sum(over_z(whole, i) for i in range(1, depth))
         with jax.named_scope("in_grad_over_z"):
-            mod_in_grad, _ = to_depth([after(in_groups[0], *depth_marks[0]), *in_groups[1:]], lambda marks: (sums,))
+            mod_in_grad, _ = to_depth(
+                [after(in_groups[0], *depth_marks[0]), *in_groups[1:]], lambda marks: (whole,)
+            )
         projected = after(projected, mod_in_grad)
         norm_grad = mod_in_grad * (1.0 + scale_here)
-        first_mean = (sums[0] / full_width)[:, None]
-        second_mean = (sums[1] / full_width)[:, None]
+        first_mean = (whole[0] / full_width)[:, None]
+        second_mean = (whole[1] / full_width)[:, None]
         input_grad = (
             live * (g_here + inverse * (norm_grad - first_mean - normed * second_mean))
         ).astype(BF)

time: 177 us -> 173 us (0.977)
  waiting for transfers between devices: 85.8 us -> 82.8 us
    ppermute x12 -> x13, waiting for transfers between devices: 26.5 us -> 22.7 us  [over_z(): return lax.ppermute(value, 'col', [(i, i ^ 2 * flip) for i in range(cols)])]
    ppermute x12 -> x13, starting transfers between devices: 16.3 us -> 15.4 us  [over_z(): return lax.ppermute(value, 'col', [(i, i ^ 2 * flip) for i in range(cols)])]
  transfers between devices with their start and end apart: 46 -> 47, of which waited for: 31 -> 31; matrix products, arithmetic and copies ran while one was open for 16% -> 16% of each run, Pallas kernels for 0% -> 0%
where the time goes in v3:
time: 173 us
  waiting for transfers between devices  82.8 us (48%)
  starting transfers between devices  45.9 us (27%)
  other arithmetic  15.3 us (9%)
  matrix products  13.1 us (8%)
  local copies, waits for them, and re-layouts  13 us (8%)
  between operations  2.64 us (2%)
    ppermute x28, waiting for transfers between devices, over_row(): return lax.ppermute(value, 'row', [(i, i ^ flip) for i in range(rows)])  55.6 us
    ppermute x28, starting transfers between devices, over_row(): return lax.ppermute(value, 'row', [(i, i ^ flip) for i in range(rows)])  30.1 us
    ppermute x13, waiting for transfers between devices, over_z(): return lax.ppermute(value, 'col', [(i, i ^ 2 * flip) for i in range(cols)])  22.7 us
    ppermute x13, starting transfers between devices, over_z(): return lax.ppermute(value, 'col', [(i, i ^ 2 * flip) for i in range(cols)])  15.4 us
    dynamic_slice x2, local copies, waits for them, and re-layouts, own_and_other(): other = lax.dynamic_slice_in_dim(weight, (1 - core) * width, width, 1)  7.49 us
    dot_general x4, matrix products, dot(): return jnp.dot(a, b, preferred_element_type=F32)  6.57 us
    dot_general x4, matrix products, dot_t(): lax.dot_general(a, b, (((1,), (1,)), ((), ())), preferred_element_type=F32)  6.56 us
    ppermute x6, waiting for transfers between devices, over_core(): return lax.ppermute(value, 'col', [(i, i ^ 1) for i in range(cols)])  4.46 us
  transfers between devices with their start and end apart: 47, of which 31 were waited for; matrix products, arithmetic and copies ran while one was open for 16% of the time, Pallas kernels for 0%

profile of v3, /device:TPU:0, one launch (start us, length us, event | category | flops | bytes accessed | tf_op | source)
XLA Modules:
  0.0 172.9 jit_solution(5500822288322838384)
XLA Ops:
  1.4 1.0 maximum_maximum_fusion
  2.4 5.1 %collective-permute-start.2 = (bf16[144,640]{1,0:T(8,128)(2,1)S(1)}, bf16[144,640]{1,0:T(8,128)(2,1)S(1)}, u32[]{:S(2)}, u32[]{:S(2)}) collective-permute-start(bf16[144,640]{1,0:T(8,128)(2,1)S(1)} %maximum_maximum_fusion), channel_id=1, source_target_pairs={{0,6},{1,7},{2,4},{3,5},{4,2},{5,3},{6,0},{7,1},{8,14},{9,15},{10,... | collective-permute-start | bytes 552968 | tf_op jit(solution)/shard_map/x_over_z/ppermute | solution.py:92
  9.0 1.3 fusion.92
  13.0 2.7 %dynamic-slice_bitcast_fusion = (bf16[1728,640]{1,0:T(8,128)(2,1)S(1)}, bf16[1728,640]{1,0:T(8,128)(2,1)S(1)}) fusion(bf16[1280,1728]{0,1:T(8,128)(2,1)} %param.9, s32[]{:T(128)S(6)} %select_n.53, s32[]{:T(128)S(6)} %select_n.52), kind=kLoop, calls=%fused_computation.2 | loop fusion | bytes 8847368 | tf_op jit(solution)/shard_map/dynamic_slice | solution.py:152
  15.8 7.4 %collective-permute-done.1 = bf16[144,640]{1,0:T(8,128)(2,1)S(1)} collective-permute-done((bf16[144,640]{1,0:T(8,128)(2,1)S(1)}, bf16[144,640]{1,0:T(8,128)(2,1)S(1)}, u32[]{:S(2)}, u32[]{:S(2)}) %collective-permute-start.1) | collective-permute-done | bytes 184352 | tf_op jit(solution)/shard_map/x_over_z/ppermute | solution.py:92
  23.9 1.2 pad_maximum_fusion.1
  25.9 0.9 collective-permute-done.3
  27.2 2.5 %collective-permute-start.6 = (bf16[128,640]{1,0:T(8,128)(2,1)S(1)}, bf16[128,640]{1,0:T(8,128)(2,1)S(1)}, u32[]{:S(2)}, u32[]{:S(2)}) collective-permute-start(bf16[128,640]{1,0:T(8,128)(2,1)S(1)} %get-tuple-element.139), channel_id=1, source_target_pairs={{0,24},{8,16},{16,8},{24,0},{1,25},{9,17},{17,9},{25,1},{2,26},{10... | collective-permute-start | bytes 491528 | tf_op jit(solution)/shard_map/modulated_over_row/ppermute | solution.py:89
  31.2 4.8 %constant_dynamic-slice_fusion.16 = (bf16[1728,640]{1,0:T(8,128)(2,1)}, bf16[1728,640]{1,0:T(8,128)(2,1)}) fusion(bf16[1728,1280]{1,0:T(8,128)(2,1)} %param.10, s32[]{:T(128)S(6)} %select_n.53, s32[]{:T(128)S(6)} %select_n.52), kind=kLoop, calls=%fused_computation.165 | loop fusion | bytes 8847368 | tf_op jit(solution)/shard_map/dynamic_slice | solution.py:152
  36.0 1.9 %collective-permute-done.5 = bf16[128,640]{1,0:T(8,128)(2,1)S(1)} collective-permute-done((bf16[128,640]{1,0:T(8,128)(2,1)S(1)}, bf16[128,640]{1,0:T(8,128)(2,1)S(1)}, u32[]{:S(2)}, u32[]{:S(2)}) %collective-permute-start.5) | collective-permute-done | bytes 163872 | tf_op jit(solution)/shard_map/modulated_over_row/ppermute | solution.py:89
  38.2 2.1 %collective-permute-done.7 = bf16[512,640]{1,0:T(8,128)(2,1)S(1)} collective-permute-done((bf16[512,640]{1,0:T(8,128)(2,1)S(1)}, bf16[512,640]{1,0:T(8,128)(2,1)S(1)}, u32[]{:S(2)}, u32[]{:S(2)}) %collective-permute-start.7) | collective-permute-done | bytes 655392 | tf_op jit(solution)/shard_map/ppermute | solution.py:95
  40.3 1.6 fusion.93
  41.9 1.7 add_convert_fusion.1
  43.7 1.2 copy-done.5
  46.5 1.5 collective-permute-start.8
  48.0 1.2 collective-permute-start.9
  49.2 2.5 %collective-permute-start.18 = (bf16[128,640]{1,0:T(8,128)(2,1)S(1)}, bf16[128,640]{1,0:T(8,128)(2,1)S(1)}, u32[]{:S(2)}, u32[]{:S(2)}) collective-permute-start(bf16[128,640]{1,0:T(8,128)(2,1)S(1)} %get-tuple-element.46), channel_id=1, source_target_pairs={{0,6},{1,7},{2,4},{3,5},{4,2},{5,3},{6,0},{7,1},{8,14},{9,15},{10,... | collective-permute-start | bytes 491528 | tf_op jit(solution)/shard_map/z_grad_over_z/ppermute | solution.py:92
  51.7 1.9 %collective-permute-start.16 = (bf16[128,640]{1,0:T(8,128)(2,1)S(1)}, bf16[128,640]{1,0:T(8,128)(2,1)S(1)}, u32[]{:S(2)}, u32[]{:S(2)}) collective-permute-start(bf16[128,640]{1,0:T(8,128)(2,1)S(1)} %get-tuple-element.46), channel_id=1, source_target_pairs={{0,2},{1,3},{2,0},{3,1},{4,6},{5,7},{6,4},{7,5},{8,10},{9,11},{10,... | collective-permute-start | bytes 491528 | tf_op jit(solution)/shard_map/z_grad_over_z/ppermute | solution.py:92
  53.6 5.8 %collective-permute-done.8 = bf16[2,64,1728]{2,1,0:T(8,128)(2,1)} collective-permute-done((bf16[2,64,1728]{2,1,0:T(8,128)(2,1)}, bf16[2,64,1728]{2,1,0:T(8,128)(2,1)}, u32[]{:S(2)}, u32[]{:S(2)}) %collective-permute-start.8) | collective-permute-done | bytes 442400 | tf_op jit(solution)/shard_map/pre_act_scatter/ppermute | solution.py:89
  59.4 1.2 collective-permute-done.9
  60.6 1.4 add_convert_fusion.6
  62.0 1.3 collective-permute-start.10
  64.7 1.1 collective-permute-start.21
  65.8 1.2 collective-permute-start.20
  67.0 1.3 collective-permute-start.19
  68.3 3.1 %collective-permute-done.10 = bf16[1,64,1728]{2,1,0:T(8,128)(2,1)S(1)} collective-permute-done((bf16[1,64,1728]{2,1,0:T(8,128)(2,1)S(1)}, bf16[1,64,1728]{2,1,0:T(8,128)(2,1)S(1)}, u32[]{:S(2)}, u32[]{:S(2)}) %collective-permute-start.10) | collective-permute-done | bytes 221216 | tf_op jit(solution)/shard_map/pre_act_scatter/ppermute | solution.py:89
  71.8 1.4 add_bitcast_fusion.3
  75.2 1.4 collective-permute-done.20
  76.7 2.2 %collective-permute-done.19 = bf16[128,640]{1,0:T(8,128)(2,1)S(1)} collective-permute-done((bf16[128,640]{1,0:T(8,128)(2,1)S(1)}, bf16[128,640]{1,0:T(8,128)(2,1)S(1)}, u32[]{:S(2)}, u32[]{:S(2)}) %collective-permute-start.19) | collective-permute-done | bytes 163872 | tf_op jit(solution)/shard_map/z_grad_over_row/ppermute | solution.py:89
  79.0 2.4 %collective-permute-done.12 = bf16[1,64,1728]{2,1,0:T(8,128)(2,1)S(1)} collective-permute-done((bf16[1,64,1728]{2,1,0:T(8,128)(2,1)S(1)}, bf16[1,64,1728]{2,1,0:T(8,128)(2,1)S(1)}, u32[]{:S(2)}, u32[]{:S(2)}) %collective-permute-start.12) | collective-permute-done | bytes 221216 | tf_op jit(solution)/shard_map/activated_gather/ppermute | solution.py:89
  81.5 0.9 collective-permute-start.14
  83.1 1.6 fusion.94
  84.7 1.6 add_convert_fusion
  86.5 1.5 collective-permute-start.24
  88.0 1.2 collective-permute-start.25
  89.2 5.8 %collective-permute-done.14 = bf16[2,64,1728]{2,1,0:T(8,128)(2,1)S(1)} collective-permute-done((bf16[2,64,1728]{2,1,0:T(8,128)(2,1)S(1)}, bf16[2,64,1728]{2,1,0:T(8,128)(2,1)S(1)}, u32[]{:S(2)}, u32[]{:S(2)}) %collective-permute-start.14) | collective-permute-done | bytes 442400 | tf_op jit(solution)/shard_map/activated_gather/ppermute | solution.py:89
  95.0 0.9 collective-permute-done.15
  96.0 1.6 fusion.95
  97.6 4.9 %collective-permute-done.24 = bf16[2,64,1728]{2,1,0:T(8,128)(2,1)S(1)} collective-permute-done((bf16[2,64,1728]{2,1,0:T(8,128)(2,1)S(1)}, bf16[2,64,1728]{2,1,0:T(8,128)(2,1)S(1)}, u32[]{:S(2)}, u32[]{:S(2)}) %collective-permute-start.24) | collective-permute-done | bytes 442400 | tf_op jit(solution)/shard_map/act_grad_scatter/ppermute | solution.py:89
  102.6 1.3 collective-permute-start.26
  104.6 1.8 %convolution_convert_fusion.1 = bf16[512,640]{1,0:T(8,128)(2,1)S(1)} fusion(bf16[512,1728]{1,0:T(8,128)(2,1)S(1)} %bitcast_dynamic-update-slice_fusion.6, bf16[1728,640]{1,0:T(8,128)(2,1)S(1)} %copy-done.3), kind=kOutput, calls=%fused_computation.9 | convolution fusion | flops 1132789760 | bytes 4636672 | tf_op jit(solution)/shard_map/dot_general | solution.py:24
  106.5 2.2 %collective-permute-done.26 = bf16[1,64,1728]{2,1,0:T(8,128)(2,1)S(1)} collective-permute-done((bf16[1,64,1728]{2,1,0:T(8,128)(2,1)S(1)}, bf16[1,64,1728]{2,1,0:T(8,128)(2,1)S(1)}, u32[]{:S(2)}, u32[]{:S(2)}) %collective-permute-start.26) | collective-permute-done | bytes 221216 | tf_op jit(solution)/shard_map/act_grad_scatter/ppermute | solution.py:89
  108.7 1.2 collective-permute-done.27
  111.5 0.9 collective-permute-start.34
  112.7 2.0 %collective-permute-start.30 = (bf16[128,640]{1,0:T(8,128)(2,1)S(1)}, bf16[128,640]{1,0:T(8,128)(2,1)S(1)}, u32[]{:S(2)}, u32[]{:S(2)}) collective-permute-start(bf16[128,640]{1,0:T(8,128)(2,1)S(1)} %get-tuple-element.149), channel_id=1, source_target_pairs={{0,24},{8,16},{16,8},{24,0},{1,25},{9,17},{17,9},{25,1},{2,26},{10... | collective-permute-start | bytes 491528 | tf_op jit(solution)/shard_map/projected_home/ppermute | solution.py:89
  116.2 2.8 %collective-permute-done.33 = bf16[1,64,1728]{2,1,0:T(8,128)(2,1)S(1)} collective-permute-done((bf16[1,64,1728]{2,1,0:T(8,128)(2,1)S(1)}, bf16[1,64,1728]{2,1,0:T(8,128)(2,1)S(1)}, u32[]{:S(2)}, u32[]{:S(2)}) %collective-permute-start.33) | collective-permute-done | bytes 221216 | tf_op jit(solution)/shard_map/pre_grad_gather/ppermute | solution.py:89
  119.0 3.0 %collective-permute-done.34 = bf16[1,64,1728]{2,1,0:T(8,128)(2,1)S(1)} collective-permute-done((bf16[1,64,1728]{2,1,0:T(8,128)(2,1)S(1)}, bf16[1,64,1728]{2,1,0:T(8,128)(2,1)S(1)}, u32[]{:S(2)}, u32[]{:S(2)}) %collective-permute-start.34) | collective-permute-done | bytes 221216 | tf_op jit(solution)/shard_map/pre_grad_gather/ppermute | solution.py:89
  122.6 1.5 collective-permute-start.36
  124.0 1.5 collective-permute-done.29
  126.1 7.2 %collective-permute-done.35 = bf16[2,64,1728]{2,1,0:T(8,128)(2,1)S(1)} collective-permute-done((bf16[2,64,1728]{2,1,0:T(8,128)(2,1)S(1)}, bf16[2,64,1728]{2,1,0:T(8,128)(2,1)S(1)}, u32[]{:S(2)}, u32[]{:S(2)}) %collective-permute-start.35) | collective-permute-done | bytes 442400 | tf_op jit(solution)/shard_map/pre_grad_gather/ppermute | solution.py:89
  133.4 1.6 convolution_convert_fusion
  135.1 1.6 fusion.96
  137.3 1.1 collective-permute-start.40
  138.5 1.1 collective-permute-start.39
  139.6 1.3 collective-permute-start.38
  141.0 4.4 %collective-permute-done.40 = bf16[128,640]{1,0:T(8,128)(2,1)S(1)} collective-permute-done((bf16[128,640]{1,0:T(8,128)(2,1)S(1)}, bf16[128,640]{1,0:T(8,128)(2,1)S(1)}, u32[]{:S(2)}, u32[]{:S(2)}) %collective-permute-start.40) | collective-permute-done | bytes 163872 | tf_op jit(solution)/shard_map/in_grad_to_row/ppermute | solution.py:89
  145.4 2.6 %collective-permute-done.39 = bf16[128,640]{1,0:T(8,128)(2,1)S(1)} collective-permute-done((bf16[128,640]{1,0:T(8,128)(2,1)S(1)}, bf16[128,640]{1,0:T(8,128)(2,1)S(1)}, u32[]{:S(2)}, u32[]{:S(2)}) %collective-permute-start.39) | collective-permute-done | bytes 163872 | tf_op jit(solution)/shard_map/in_grad_to_row/ppermute | solution.py:89
  149.1 1.0 collective-permute-done.42
  150.7 1.9 %collective-permute-start.45 = (f32[2,128]{1,0:T(2,128)S(1)}, f32[2,128]{1,0:T(2,128)S(1)}, u32[]{:S(2)}, u32[]{:S(2)}) collective-permute-start(f32[2,128]{1,0:T(2,128)S(1)} %fusion.87), channel_id=1, source_target_pairs={{0,6},{1,7},{2,4},{3,5},{4,2},{5,3},{6,0},{7,1},{8,14},{9,15},{10,... | collective-permute-start | bytes 3080 | tf_op jit(solution)/shard_map/norm_sums/ppermute | solution.py:92
  152.7 2.3 %collective-permute-start.44 = (f32[2,128]{1,0:T(2,128)S(1)}, f32[2,128]{1,0:T(2,128)S(1)}, u32[]{:S(2)}, u32[]{:S(2)}) collective-permute-start(f32[2,128]{1,0:T(2,128)S(1)} %fusion.87), channel_id=1, source_target_pairs={{0,4},{1,5},{2,6},{3,7},{4,0},{5,1},{6,2},{7,3},{8,12},{9,13},{10,... | collective-permute-start | bytes 3080 | tf_op jit(solution)/shard_map/norm_sums/ppermute | solution.py:92
  155.1 4.8 %collective-permute-done.45 = f32[2,128]{1,0:T(2,128)S(1)} collective-permute-done((f32[2,128]{1,0:T(2,128)S(1)}, f32[2,128]{1,0:T(2,128)S(1)}, u32[]{:S(2)}, u32[]{:S(2)}) %collective-permute-start.45) | collective-permute-done | bytes 1056 | tf_op jit(solution)/shard_map/norm_sums/ppermute | solution.py:92
  160.7 9.5 %collective-permute-done.46 = bf16[1,128,640]{2,1,0:T(8,128)(2,1)S(1)} collective-permute-done((bf16[1,128,640]{2,1,0:T(8,128)(2,1)S(1)}, bf16[1,128,640]{2,1,0:T(8,128)(2,1)S(1)}, u32[]{:S(2)}, u32[]{:S(2)}) %collective-permute-start.46) | collective-permute-done | bytes 163872 | tf_op jit(solution)/shard_map/in_grad_over_z/ppermute | solution.py:92
  170.2 0.9 fusion.20
  171.1 1.0 multiply_reduce_fusion.3
  (142 shorter events, 23.5 us)
Async XLA Ops:
  2.4 13.4 %collective-permute-start.2 = (bf16[144,640]{1,0:T(8,128)(2,1)S(1)}, bf16[144,640]{1,0:T(8,128)(2,1)S(1)}, u32[]{:S(2)}, u32[]{:S(2)}) collective-permute-start(bf16[144,640]{1,0:T(8,128)(2,1)S(1)} %maximum_maximum_fusion), channel_id=1, source_target_pairs={{0,6},{1,7},{2,4},{3,5},{4,2},{5,3},{6,0},{7,1},{8,14},{9,15},{10,... | collective-permute-start | bytes 552968 | tf_op jit(solution)/shard_map/x_over_z/ppermute | solution.py:92
  7.6 15.6 %collective-permute-start.1 = (bf16[144,640]{1,0:T(8,128)(2,1)S(1)}, bf16[144,640]{1,0:T(8,128)(2,1)S(1)}, u32[]{:S(2)}, u32[]{:S(2)}) collective-permute-start(bf16[144,640]{1,0:T(8,128)(2,1)S(1)} %maximum_maximum_fusion), channel_id=1, source_target_pairs={{0,4},{1,5},{2,6},{3,7},{4,0},{5,1},{6,2},{7,3},{8,12},{9,13},{10,... | collective-permute-start | bytes 552968 | tf_op jit(solution)/shard_map/x_over_z/ppermute | solution.py:92
  7.6 15.6 %collective-permute-start = (bf16[144,640]{1,0:T(8,128)(2,1)S(1)}, bf16[144,640]{1,0:T(8,128)(2,1)S(1)}, u32[]{:S(2)}, u32[]{:S(2)}) collective-permute-start(bf16[144,640]{1,0:T(8,128)(2,1)S(1)} %maximum_maximum_fusion), channel_id=1, source_target_pairs={{0,2},{1,3},{2,0},{3,1},{4,6},{5,7},{6,4},{7,5},{8,10},{9,11},{10,... | collective-permute-start | bytes 552968 | tf_op jit(solution)/shard_map/x_over_z/ppermute | solution.py:92
  13.0 2.7 %copy-start = (bf16[128,640]{1,0:T(8,128)(2,1)S(1)}, bf16[128,640]{1,0:T(8,128)(2,1)}, u32[]{:S(2)}) copy-start(bf16[128,640]{1,0:T(8,128)(2,1)} %param.6) | copy-start | bytes 491524
  15.7 24.6 %copy-start.1 = (bf16[1728,640]{1,0:T(8,128)(2,1)}, bf16[1728,640]{1,0:T(8,128)(2,1)S(1)}, u32[]{:S(2)}) copy-start(bf16[1728,640]{1,0:T(8,128)(2,1)S(1)} %get-tuple-element.124) | copy-start | bytes 6635524
  23.2 0.7 copy-start.7
  23.2 0.7 copy-start.8
  23.9 5.8 %copy-start.6 = (bf16[128,640]{1,0:T(8,128)(2,1)S(1)}, bf16[128,640]{1,0:T(8,128)(2,1)}, u32[]{:S(2)}) copy-start(bf16[128,640]{1,0:T(8,128)(2,1)} %param.11) | copy-start | bytes 491524
  25.6 1.2 collective-permute-start.3
  27.2 8.8 %collective-permute-start.6 = (bf16[128,640]{1,0:T(8,128)(2,1)S(1)}, bf16[128,640]{1,0:T(8,128)(2,1)S(1)}, u32[]{:S(2)}, u32[]{:S(2)}) collective-permute-start(bf16[128,640]{1,0:T(8,128)(2,1)S(1)} %get-tuple-element.139), channel_id=1, source_target_pairs={{0,24},{8,16},{16,8},{24,0},{1,25},{9,17},{17,9},{25,1},{2,26},{10... | collective-permute-start | bytes 491528 | tf_op jit(solution)/shard_map/modulated_over_row/ppermute | solution.py:89
  30.1 7.8 %collective-permute-start.5 = (bf16[128,640]{1,0:T(8,128)(2,1)S(1)}, bf16[128,640]{1,0:T(8,128)(2,1)S(1)}, u32[]{:S(2)}, u32[]{:S(2)}) collective-permute-start(bf16[128,640]{1,0:T(8,128)(2,1)S(1)} %get-tuple-element.141), channel_id=1, source_target_pairs={{0,16},{8,24},{16,0},{24,8},{1,17},{9,25},{17,1},{25,9},{2,18},{10... | collective-permute-start | bytes 491528 | tf_op jit(solution)/shard_map/modulated_over_row/ppermute | solution.py:89
  30.7 7.3 %collective-permute-start.4 = (bf16[128,640]{1,0:T(8,128)(2,1)S(1)}, bf16[128,640]{1,0:T(8,128)(2,1)S(1)}, u32[]{:S(2)}, u32[]{:S(2)}) collective-permute-start(bf16[128,640]{1,0:T(8,128)(2,1)S(1)} %get-tuple-element.140), channel_id=1, source_target_pairs={{0,8},{8,0},{16,24},{24,16},{1,9},{9,1},{17,25},{25,17},{2,10},{10... | collective-permute-start | bytes 491528 | tf_op jit(solution)/shard_map/modulated_over_row/ppermute | solution.py:89
  38.1 2.2 %collective-permute-start.7 = (bf16[512,640]{1,0:T(8,128)(2,1)S(1)}, bf16[512,640]{1,0:T(8,128)(2,1)S(1)}, u32[]{:S(2)}, u32[]{:S(2)}) collective-permute-start(bf16[512,640]{1,0:T(8,128)(2,1)S(1)} %pad_maximum_fusion.2), channel_id=1, source_target_pairs={{0,1},{1,0},{2,3},{3,2},{4,5},{5,4},{6,7},{7,6},{8,9},{9,8},{10,11... | collective-permute-start | bytes 1966088 | tf_op jit(solution)/shard_map/ppermute | solution.py:95
  43.6 1.2 copy-start.5
  46.5 12.9 %collective-permute-start.8 = (bf16[2,64,1728]{2,1,0:T(8,128)(2,1)}, bf16[2,64,1728]{2,1,0:T(8,128)(2,1)}, u32[]{:S(2)}, u32[]{:S(2)}) collective-permute-start(bf16[2,64,1728]{2,1,0:T(8,128)(2,1)} %pad_maximum_fusion.7), channel_id=1, source_target_pairs={{0,8},{8,0},{16,24},{24,16},{1,9},{9,1},{17,25},{25,17},{2,10},{10... | collective-permute-start | bytes 1327112 | tf_op jit(solution)/shard_map/pre_act_scatter/ppermute | solution.py:89
  48.0 12.6 %collective-permute-start.9 = (bf16[2,64,1728]{2,1,0:T(8,128)(2,1)}, bf16[2,64,1728]{2,1,0:T(8,128)(2,1)}, u32[]{:S(2)}, u32[]{:S(2)}) collective-permute-start(bf16[2,64,1728]{2,1,0:T(8,128)(2,1)} %stack.209), channel_id=1, source_target_pairs={{0,16},{8,24},{16,0},{24,8},{1,17},{9,25},{17,1},{25,9},{2,18},{10... | collective-permute-start | bytes 1327112 | tf_op jit(solution)/shard_map/pre_act_scatter/ppermute | solution.py:89
  49.2 14.8 %collective-permute-start.18 = (bf16[128,640]{1,0:T(8,128)(2,1)S(1)}, bf16[128,640]{1,0:T(8,128)(2,1)S(1)}, u32[]{:S(2)}, u32[]{:S(2)}) collective-permute-start(bf16[128,640]{1,0:T(8,128)(2,1)S(1)} %get-tuple-element.46), channel_id=1, source_target_pairs={{0,6},{1,7},{2,4},{3,5},{4,2},{5,3},{6,0},{7,1},{8,14},{9,15},{10,... | collective-permute-start | bytes 491528 | tf_op jit(solution)/shard_map/z_grad_over_z/ppermute | solution.py:92
  51.7 12.8 %collective-permute-start.17 = (bf16[128,640]{1,0:T(8,128)(2,1)S(1)}, bf16[128,640]{1,0:T(8,128)(2,1)S(1)}, u32[]{:S(2)}, u32[]{:S(2)}) collective-permute-start(bf16[128,640]{1,0:T(8,128)(2,1)S(1)} %get-tuple-element.46), channel_id=1, source_target_pairs={{0,4},{1,5},{2,6},{3,7},{4,0},{5,1},{6,2},{7,3},{8,12},{9,13},{10,... | collective-permute-start | bytes 491528 | tf_op jit(solution)/shard_map/z_grad_over_z/ppermute | solution.py:92
  51.7 12.8 %collective-permute-start.16 = (bf16[128,640]{1,0:T(8,128)(2,1)S(1)}, bf16[128,640]{1,0:T(8,128)(2,1)S(1)}, u32[]{:S(2)}, u32[]{:S(2)}) collective-permute-start(bf16[128,640]{1,0:T(8,128)(2,1)S(1)} %get-tuple-element.46), channel_id=1, source_target_pairs={{0,2},{1,3},{2,0},{3,1},{4,6},{5,7},{6,4},{7,5},{8,10},{9,11},{10,... | collective-permute-start | bytes 491528 | tf_op jit(solution)/shard_map/z_grad_over_z/ppermute | solution.py:92
  62.0 9.4 %collective-permute-start.10 = (bf16[1,64,1728]{2,1,0:T(8,128)(2,1)S(1)}, bf16[1,64,1728]{2,1,0:T(8,128)(2,1)S(1)}, u32[]{:S(2)}, u32[]{:S(2)}) collective-permute-start(bf16[1,64,1728]{2,1,0:T(8,128)(2,1)S(1)} %get-tuple-element.135), channel_id=1, source_target_pairs={{0,16},{8,24},{16,0},{24,8},{1,17},{9,25},{17,1},{25,9},{2,18},{10... | collective-permute-start | bytes 663560 | tf_op jit(solution)/shard_map/pre_act_scatter/ppermute | solution.py:89
  63.3 8.5 %collective-permute-start.11 = (bf16[1,64,1728]{2,1,0:T(8,128)(2,1)S(1)}, bf16[1,64,1728]{2,1,0:T(8,128)(2,1)S(1)}, u32[]{:S(2)}, u32[]{:S(2)}) collective-permute-start(bf16[1,64,1728]{2,1,0:T(8,128)(2,1)S(1)} %get-tuple-element.134), channel_id=1, source_target_pairs={{0,8},{8,0},{16,24},{24,16},{1,9},{9,1},{17,25},{25,17},{2,10},{10... | collective-permute-start | bytes 663560 | tf_op jit(solution)/shard_map/pre_act_scatter/ppermute | solution.py:89
  64.7 10.5 %collective-permute-start.21 = (bf16[128,640]{1,0:T(8,128)(2,1)S(1)}, bf16[128,640]{1,0:T(8,128)(2,1)S(1)}, u32[]{:S(2)}, u32[]{:S(2)}) collective-permute-start(bf16[128,640]{1,0:T(8,128)(2,1)S(1)} %get-tuple-element.153), channel_id=1, source_target_pairs={{0,24},{8,16},{16,8},{24,0},{1,25},{9,17},{17,9},{25,1},{2,26},{10... | collective-permute-start | bytes 491528 | tf_op jit(solution)/shard_map/z_grad_over_row/ppermute | solution.py:89
  65.8 10.9 %collective-permute-start.20 = (bf16[128,640]{1,0:T(8,128)(2,1)S(1)}, bf16[128,640]{1,0:T(8,128)(2,1)S(1)}, u32[]{:S(2)}, u32[]{:S(2)}) collective-permute-start(bf16[128,640]{1,0:T(8,128)(2,1)S(1)} %get-tuple-element.154), channel_id=1, source_target_pairs={{0,16},{8,24},{16,0},{24,8},{1,17},{9,25},{17,1},{25,9},{2,18},{10... | collective-permute-start | bytes 491528 | tf_op jit(solution)/shard_map/z_grad_over_row/ppermute | solution.py:89
  67.0 11.8 %collective-permute-start.19 = (bf16[128,640]{1,0:T(8,128)(2,1)S(1)}, bf16[128,640]{1,0:T(8,128)(2,1)S(1)}, u32[]{:S(2)}, u32[]{:S(2)}) collective-permute-start(bf16[128,640]{1,0:T(8,128)(2,1)S(1)} %get-tuple-element.155), channel_id=1, source_target_pairs={{0,8},{8,0},{16,24},{24,16},{1,9},{9,1},{17,25},{25,17},{2,10},{10... | collective-permute-start | bytes 491528 | tf_op jit(solution)/shard_map/z_grad_over_row/ppermute | solution.py:89
  73.6 9.5 %copy-start.3 = (bf16[1728,640]{1,0:T(8,128)(2,1)S(1)}, bf16[1728,640]{1,0:T(8,128)(2,1)}, u32[]{:S(2)}) copy-start(bf16[1728,640]{1,0:T(8,128)(2,1)} %get-tuple-element.122) | copy-start | bytes 6635524
  73.6 7.8 %collective-permute-start.12 = (bf16[1,64,1728]{2,1,0:T(8,128)(2,1)S(1)}, bf16[1,64,1728]{2,1,0:T(8,128)(2,1)S(1)}, u32[]{:S(2)}, u32[]{:S(2)}) collective-permute-start(bf16[1,64,1728]{2,1,0:T(8,128)(2,1)S(1)} %get-tuple-element.160), channel_id=1, source_target_pairs={{0,8},{8,0},{16,24},{24,16},{1,9},{9,1},{17,25},{25,17},{2,10},{10... | collective-permute-start | bytes 663560 | tf_op jit(solution)/shard_map/activated_gather/ppermute | solution.py:89
  74.4 7.0 %collective-permute-start.13 = (bf16[1,64,1728]{2,1,0:T(8,128)(2,1)S(1)}, bf16[1,64,1728]{2,1,0:T(8,128)(2,1)S(1)}, u32[]{:S(2)}, u32[]{:S(2)}) collective-permute-start(bf16[1,64,1728]{2,1,0:T(8,128)(2,1)S(1)} %get-tuple-element.159), channel_id=1, source_target_pairs={{0,16},{8,24},{16,0},{24,8},{1,17},{9,25},{17,1},{25,9},{2,18},{10... | collective-permute-start | bytes 663560 | tf_op jit(solution)/shard_map/activated_gather/ppermute | solution.py:89
  78.9 4.2 %collective-permute-start.22 = (bf16[512,640]{1,0:T(8,128)(2,1)S(1)}, bf16[512,640]{1,0:T(8,128)(2,1)S(1)}, u32[]{:S(2)}, u32[]{:S(2)}) collective-permute-start(bf16[512,640]{1,0:T(8,128)(2,1)S(1)} %pad_maximum_fusion.4), channel_id=1, source_target_pairs={{0,1},{1,0},{2,3},{3,2},{4,5},{5,4},{6,7},{7,6},{8,9},{9,8},{10,11... | collective-permute-start | bytes 1966088 | tf_op jit(solution)/shard_map/ppermute | solution.py:95
  81.5 13.5 %collective-permute-start.14 = (bf16[2,64,1728]{2,1,0:T(8,128)(2,1)S(1)}, bf16[2,64,1728]{2,1,0:T(8,128)(2,1)S(1)}, u32[]{:S(2)}, u32[]{:S(2)}) collective-permute-start(bf16[2,64,1728]{2,1,0:T(8,128)(2,1)S(1)} %pad_maximum_fusion.8), channel_id=1, source_target_pairs={{0,16},{8,24},{16,0},{24,8},{1,17},{9,25},{17,1},{25,9},{2,18},{10... | collective-permute-start | bytes 1327112 | tf_op jit(solution)/shard_map/activated_gather/ppermute | solution.py:89
  82.4 13.5 %collective-permute-start.15 = (bf16[2,64,1728]{2,1,0:T(8,128)(2,1)S(1)}, bf16[2,64,1728]{2,1,0:T(8,128)(2,1)S(1)}, u32[]{:S(2)}, u32[]{:S(2)}) collective-permute-start(bf16[2,64,1728]{2,1,0:T(8,128)(2,1)S(1)} %pad_maximum_fusion.9), channel_id=1, source_target_pairs={{0,8},{8,0},{16,24},{24,16},{1,9},{9,1},{17,25},{25,17},{2,10},{10... | collective-permute-start | bytes 1327112 | tf_op jit(solution)/shard_map/activated_gather/ppermute | solution.py:89
  83.1 1.7 copy-start.4
  86.5 16.0 %collective-permute-start.24 = (bf16[2,64,1728]{2,1,0:T(8,128)(2,1)S(1)}, bf16[2,64,1728]{2,1,0:T(8,128)(2,1)S(1)}, u32[]{:S(2)}, u32[]{:S(2)}) collective-permute-start(bf16[2,64,1728]{2,1,0:T(8,128)(2,1)S(1)} %pad_maximum_fusion.10), channel_id=1, source_target_pairs={{0,8},{8,0},{16,24},{24,16},{1,9},{9,1},{17,25},{25,17},{2,10},{10... | collective-permute-start | bytes 1327112 | tf_op jit(solution)/shard_map/act_grad_scatter/ppermute | solution.py:89
  88.0 14.5 %collective-permute-start.25 = (bf16[2,64,1728]{2,1,0:T(8,128)(2,1)S(1)}, bf16[2,64,1728]{2,1,0:T(8,128)(2,1)S(1)}, u32[]{:S(2)}, u32[]{:S(2)}) collective-permute-start(bf16[2,64,1728]{2,1,0:T(8,128)(2,1)S(1)} %stack.210), channel_id=1, source_target_pairs={{0,16},{8,24},{16,0},{24,8},{1,17},{9,25},{17,1},{25,9},{2,18},{10... | collective-permute-start | bytes 1327112 | tf_op jit(solution)/shard_map/act_grad_scatter/ppermute | solution.py:89
  102.6 6.1 %collective-permute-start.26 = (bf16[1,64,1728]{2,1,0:T(8,128)(2,1)S(1)}, bf16[1,64,1728]{2,1,0:T(8,128)(2,1)S(1)}, u32[]{:S(2)}, u32[]{:S(2)}) collective-permute-start(bf16[1,64,1728]{2,1,0:T(8,128)(2,1)S(1)} %get-tuple-element.51), channel_id=1, source_target_pairs={{0,16},{8,24},{16,0},{24,8},{1,17},{9,25},{17,1},{25,9},{2,18},{10... | collective-permute-start | bytes 663560 | tf_op jit(solution)/shard_map/act_grad_scatter/ppermute | solution.py:89
  103.9 6.0 %collective-permute-start.27 = (bf16[1,64,1728]{2,1,0:T(8,128)(2,1)S(1)}, bf16[1,64,1728]{2,1,0:T(8,128)(2,1)S(1)}, u32[]{:S(2)}, u32[]{:S(2)}) collective-permute-start(bf16[1,64,1728]{2,1,0:T(8,128)(2,1)S(1)} %get-tuple-element.53), channel_id=1, source_target_pairs={{0,8},{8,0},{16,24},{24,16},{1,9},{9,1},{17,25},{25,17},{2,10},{10... | collective-permute-start | bytes 663560 | tf_op jit(solution)/shard_map/act_grad_scatter/ppermute | solution.py:89
  106.4 6.0 %collective-permute-start.23 = (bf16[512,640]{1,0:T(8,128)(2,1)S(1)}, bf16[512,640]{1,0:T(8,128)(2,1)S(1)}, u32[]{:S(2)}, u32[]{:S(2)}) collective-permute-start(bf16[512,640]{1,0:T(8,128)(2,1)S(1)} %convolution_convert_fusion.1), channel_id=1, source_target_pairs={{0,1},{1,0},{2,3},{3,2},{4,5},{5,4},{6,7},{7,6},{8,9},{9,8},{10,11... | collective-permute-start | bytes 1966088 | tf_op jit(solution)/shard_map/ppermute | solution.py:95
  110.7 8.3 %collective-permute-start.33 = (bf16[1,64,1728]{2,1,0:T(8,128)(2,1)S(1)}, bf16[1,64,1728]{2,1,0:T(8,128)(2,1)S(1)}, u32[]{:S(2)}, u32[]{:S(2)}) collective-permute-start(bf16[1,64,1728]{2,1,0:T(8,128)(2,1)S(1)} %get-tuple-element.158), channel_id=1, source_target_pairs={{0,8},{8,0},{16,24},{24,16},{1,9},{9,1},{17,25},{25,17},{2,10},{10... | collective-permute-start | bytes 663560 | tf_op jit(solution)/shard_map/pre_grad_gather/ppermute | solution.py:89
  111.5 10.5 %collective-permute-start.34 = (bf16[1,64,1728]{2,1,0:T(8,128)(2,1)S(1)}, bf16[1,64,1728]{2,1,0:T(8,128)(2,1)S(1)}, u32[]{:S(2)}, u32[]{:S(2)}) collective-permute-start(bf16[1,64,1728]{2,1,0:T(8,128)(2,1)S(1)} %get-tuple-element.157), channel_id=1, source_target_pairs={{0,16},{8,24},{16,0},{24,8},{1,17},{9,25},{17,1},{25,9},{2,18},{10... | collective-permute-start | bytes 663560 | tf_op jit(solution)/shard_map/pre_grad_gather/ppermute | solution.py:89
  112.7 11.4 %collective-permute-start.30 = (bf16[128,640]{1,0:T(8,128)(2,1)S(1)}, bf16[128,640]{1,0:T(8,128)(2,1)S(1)}, u32[]{:S(2)}, u32[]{:S(2)}) collective-permute-start(bf16[128,640]{1,0:T(8,128)(2,1)S(1)} %get-tuple-element.149), channel_id=1, source_target_pairs={{0,24},{8,16},{16,8},{24,0},{1,25},{9,17},{17,9},{25,1},{2,26},{10... | collective-permute-start | bytes 491528 | tf_op jit(solution)/shard_map/projected_home/ppermute | solution.py:89
  114.6 10.9 %collective-permute-start.29 = (bf16[128,640]{1,0:T(8,128)(2,1)S(1)}, bf16[128,640]{1,0:T(8,128)(2,1)S(1)}, u32[]{:S(2)}, u32[]{:S(2)}) collective-permute-start(bf16[128,640]{1,0:T(8,128)(2,1)S(1)} %get-tuple-element.150), channel_id=1, source_target_pairs={{0,16},{8,24},{16,0},{24,8},{1,17},{9,25},{17,1},{25,9},{2,18},{10... | collective-permute-start | bytes 491528 | tf_op jit(solution)/shard_map/projected_home/ppermute | solution.py:89
  115.5 10.3 %collective-permute-start.28 = (bf16[128,640]{1,0:T(8,128)(2,1)S(1)}, bf16[128,640]{1,0:T(8,128)(2,1)S(1)}, u32[]{:S(2)}, u32[]{:S(2)}) collective-permute-start(bf16[128,640]{1,0:T(8,128)(2,1)S(1)} %get-tuple-element.151), channel_id=1, source_target_pairs={{0,8},{8,0},{16,24},{24,16},{1,9},{9,1},{17,25},{25,17},{2,10},{10... | collective-permute-start | bytes 491528 | tf_op jit(solution)/shard_map/projected_home/ppermute | solution.py:89
  122.1 11.1 %collective-permute-start.35 = (bf16[2,64,1728]{2,1,0:T(8,128)(2,1)S(1)}, bf16[2,64,1728]{2,1,0:T(8,128)(2,1)S(1)}, u32[]{:S(2)}, u32[]{:S(2)}) collective-permute-start(bf16[2,64,1728]{2,1,0:T(8,128)(2,1)S(1)} %get-tuple-element.59), channel_id=1, source_target_pairs={{0,16},{8,24},{16,0},{24,8},{1,17},{9,25},{17,1},{25,9},{2,18},{10... | collective-permute-start | bytes 1327112 | tf_op jit(solution)/shard_map/pre_grad_gather/ppermute | solution.py:89
  122.6 10.7 %collective-permute-start.36 = (bf16[2,64,1728]{2,1,0:T(8,128)(2,1)S(1)}, bf16[2,64,1728]{2,1,0:T(8,128)(2,1)S(1)}, u32[]{:S(2)}, u32[]{:S(2)}) collective-permute-start(bf16[2,64,1728]{2,1,0:T(8,128)(2,1)S(1)} %get-tuple-element.61), channel_id=1, source_target_pairs={{0,8},{8,0},{16,24},{24,16},{1,9},{9,1},{17,25},{25,17},{2,10},{10... | collective-permute-start | bytes 1327112 | tf_op jit(solution)/shard_map/pre_grad_gather/ppermute | solution.py:89
  125.9 7.5 %copy-start.2 = (bf16[1728,640]{1,0:T(8,128)(2,1)S(1)}, bf16[1728,640]{1,0:T(8,128)(2,1)}, u32[]{:S(2)}) copy-start(bf16[1728,640]{1,0:T(8,128)(2,1)} %copy-done.1) | copy-start | bytes 6635524
  126.0 9.1 %collective-permute-start.31 = (bf16[2,128,640]{2,1,0:T(8,128)(2,1)S(1)}, bf16[2,128,640]{2,1,0:T(8,128)(2,1)S(1)}, u32[]{:S(2)}, u32[]{:S(2)}) collective-permute-start(bf16[2,128,640]{2,1,0:T(8,128)(2,1)S(1)} %pad_maximum_fusion.13), channel_id=1, source_target_pairs={{0,2},{1,3},{2,0},{3,1},{4,6},{5,7},{6,4},{7,5},{8,10},{9,11},{10,... | collective-permute-start | bytes 983048 | tf_op jit(solution)/shard_map/projected_home/ppermute | solution.py:92
  135.0 2.2 %collective-permute-start.37 = (bf16[512,640]{1,0:T(8,128)(2,1)S(1)}, bf16[512,640]{1,0:T(8,128)(2,1)S(1)}, u32[]{:S(2)}, u32[]{:S(2)}) collective-permute-start(bf16[512,640]{1,0:T(8,128)(2,1)S(1)} %convolution_convert_fusion), channel_id=1, source_target_pairs={{0,1},{1,0},{2,3},{3,2},{4,5},{5,4},{6,7},{7,6},{8,9},{9,8},{10,11... | collective-permute-start | bytes 1966088 | tf_op jit(solution)/shard_map/ppermute | solution.py:95
  137.3 8.1 %collective-permute-start.40 = (bf16[128,640]{1,0:T(8,128)(2,1)S(1)}, bf16[128,640]{1,0:T(8,128)(2,1)S(1)}, u32[]{:S(2)}, u32[]{:S(2)}) collective-permute-start(bf16[128,640]{1,0:T(8,128)(2,1)S(1)} %get-tuple-element.143), channel_id=1, source_target_pairs={{0,24},{8,16},{16,8},{24,0},{1,25},{9,17},{17,9},{25,1},{2,26},{10... | collective-permute-start | bytes 491528 | tf_op jit(solution)/shard_map/in_grad_to_row/ppermute | solution.py:89
  138.5 9.5 %collective-permute-start.39 = (bf16[128,640]{1,0:T(8,128)(2,1)S(1)}, bf16[128,640]{1,0:T(8,128)(2,1)S(1)}, u32[]{:S(2)}, u32[]{:S(2)}) collective-permute-start(bf16[128,640]{1,0:T(8,128)(2,1)S(1)} %get-tuple-element.144), channel_id=1, source_target_pairs={{0,16},{8,24},{16,0},{24,8},{1,17},{9,25},{17,1},{25,9},{2,18},{10... | collective-permute-start | bytes 491528 | tf_op jit(solution)/shard_map/in_grad_to_row/ppermute | solution.py:89
  139.6 8.4 %collective-permute-start.38 = (bf16[128,640]{1,0:T(8,128)(2,1)S(1)}, bf16[128,640]{1,0:T(8,128)(2,1)S(1)}, u32[]{:S(2)}, u32[]{:S(2)}) collective-permute-start(bf16[128,640]{1,0:T(8,128)(2,1)S(1)} %get-tuple-element.145), channel_id=1, source_target_pairs={{0,8},{8,0},{16,24},{24,16},{1,9},{9,1},{17,25},{25,17},{2,10},{10... | collective-permute-start | bytes 491528 | tf_op jit(solution)/shard_map/in_grad_to_row/ppermute | solution.py:89
  140.9 9.7 %collective-permute-start.32 = (bf16[1,128,640]{2,1,0:T(8,128)(2,1)S(1)}, bf16[1,128,640]{2,1,0:T(8,128)(2,1)S(1)}, u32[]{:S(2)}, u32[]{:S(2)}) collective-permute-start(bf16[1,128,640]{2,1,0:T(8,128)(2,1)S(1)} %add_convert_fusion.8), channel_id=1, source_target_pairs={{0,4},{1,5},{2,6},{3,7},{4,0},{5,1},{6,2},{7,3},{8,12},{9,13},{10,... | collective-permute-start | bytes 491528 | tf_op jit(solution)/shard_map/projected_home/ppermute | solution.py:92
  148.9 1.2 collective-permute-start.42
  149.1 10.9 %collective-permute-start.41 = (bf16[2,128,640]{2,1,0:T(8,128)(2,1)S(1)}, bf16[2,128,640]{2,1,0:T(8,128)(2,1)S(1)}, u32[]{:S(2)}, u32[]{:S(2)}) collective-permute-start(bf16[2,128,640]{2,1,0:T(8,128)(2,1)S(1)} %pad_maximum_fusion.14), channel_id=1, source_target_pairs={{0,2},{1,3},{2,0},{3,1},{4,6},{5,7},{6,4},{7,5},{8,10},{9,11},{10,... | collective-permute-start | bytes 983048 | tf_op jit(solution)/shard_map/in_grad_over_z/ppermute | solution.py:92
  150.7 9.2 %collective-permute-start.45 = (f32[2,128]{1,0:T(2,128)S(1)}, f32[2,128]{1,0:T(2,128)S(1)}, u32[]{:S(2)}, u32[]{:S(2)}) collective-permute-start(f32[2,128]{1,0:T(2,128)S(1)} %fusion.87), channel_id=1, source_target_pairs={{0,6},{1,7},{2,4},{3,5},{4,2},{5,3},{6,0},{7,1},{8,14},{9,15},{10,... | collective-permute-start | bytes 3080 | tf_op jit(solution)/shard_map/norm_sums/ppermute | solution.py:92
  152.6 7.3 %collective-permute-start.43 = (f32[2,128]{1,0:T(2,128)S(1)}, f32[2,128]{1,0:T(2,128)S(1)}, u32[]{:S(2)}, u32[]{:S(2)}) collective-permute-start(f32[2,128]{1,0:T(2,128)S(1)} %fusion.87), channel_id=1, source_target_pairs={{0,2},{1,3},{2,0},{3,1},{4,6},{5,7},{6,4},{7,5},{8,10},{9,11},{10,... | collective-permute-start | bytes 3080 | tf_op jit(solution)/shard_map/norm_sums/ppermute | solution.py:92
  152.7 7.2 %collective-permute-start.44 = (f32[2,128]{1,0:T(2,128)S(1)}, f32[2,128]{1,0:T(2,128)S(1)}, u32[]{:S(2)}, u32[]{:S(2)}) collective-permute-start(f32[2,128]{1,0:T(2,128)S(1)} %fusion.87), channel_id=1, source_target_pairs={{0,4},{1,5},{2,6},{3,7},{4,0},{5,1},{6,2},{7,3},{8,12},{9,13},{10,... | collective-permute-start | bytes 3080 | tf_op jit(solution)/shard_map/norm_sums/ppermute | solution.py:92
  160.0 10.2 %collective-permute-start.46 = (bf16[1,128,640]{2,1,0:T(8,128)(2,1)S(1)}, bf16[1,128,640]{2,1,0:T(8,128)(2,1)S(1)}, u32[]{:S(2)}, u32[]{:S(2)}) collective-permute-start(bf16[1,128,640]{2,1,0:T(8,128)(2,1)S(1)} %fusion.16), channel_id=1, source_target_pairs={{0,4},{1,5},{2,6},{3,7},{4,0},{5,1},{6,2},{7,3},{8,12},{9,13},{10,... | collective-permute-start | bytes 491528 | tf_op jit(solution)/shard_map/in_grad_over_z/ppermute | solution.py:92

commit v4 on v3

--- a/solution.py
+++ b/solution.py
@@ -257,7 +257,7 @@
             whole = whole + sum(over_z(whole, i) for i in range(1, depth))
         with jax.named_scope("in_grad_over_z"):
             mod_in_grad, _ = to_depth(
-                [after(in_groups[0], *depth_marks[0]), *in_groups[1:]], lambda marks: (whole,)
+                [in_groups[0], *in_groups[1:]], lambda marks: (whole,)
             )
         projected = after(projected, mod_in_grad)
         norm_grad = mod_in_grad * (1.0 + scale_here)

time: 173 us -> 173 us (level)
  transfers between devices with their start and end apart: 47 -> 47, of which waited for: 31 -> 29; matrix products, arithmetic and copies ran while one was open for 16% -> 16% of each run, Pallas kernels for 0% -> 0%
where the time goes in v4:
time: 173 us
  waiting for transfers between devices  81.9 us (47%)
  starting transfers between devices  46.6 us (27%)
  other arithmetic  15.3 us (9%)
  matrix products  13.1 us (8%)
  local copies, waits for them, and re-layouts  13 us (8%)
  between operations  2.64 us (2%)
    ppermute x28, waiting for transfers between devices, over_row(): return lax.ppermute(value, 'row', [(i, i ^ flip) for i in range(rows)])  55.2 us
    ppermute x28, starting transfers between devices, over_row(): return lax.ppermute(value, 'row', [(i, i ^ flip) for i in range(rows)])  30.8 us
    ppermute x13, waiting for transfers between devices, over_z(): return lax.ppermute(value, 'col', [(i, i ^ 2 * flip) for i in range(cols)])  22.2 us
    ppermute x13, starting transfers between devices, over_z(): return lax.ppermute(value, 'col', [(i, i ^ 2 * flip) for i in range(cols)])  15.4 us
    dynamic_slice x2, local copies, waits for them, and re-layouts, own_and_other(): other = lax.dynamic_slice_in_dim(weight, (1 - core) * width, width, 1)  7.49 us
    dot_general x4, matrix products, dot(): return jnp.dot(a, b, preferred_element_type=F32)  6.56 us
    dot_general x4, matrix products, dot_t(): lax.dot_general(a, b, (((1,), (1,)), ((), ())), preferred_element_type=F32)  6.56 us
    ppermute x6, waiting for transfers between devices, over_core(): return lax.ppermute(value, 'col', [(i, i ^ 1) for i in range(cols)])  4.47 us
  transfers between devices with their start and end apart: 47, of which 29 were waited for; matrix products, arithmetic and copies ran while one was open for 16% of the time, Pallas kernels for 0%

profile of v4, /device:TPU:0, one launch (start us, length us, event | category | flops | bytes accessed | tf_op | source)
XLA Modules:
  0.0 172.6 jit_solution(7099268219768048896)
XLA Ops:
  1.4 1.0 maximum_maximum_fusion
  2.4 5.1 %collective-permute-start.2 = (bf16[144,640]{1,0:T(8,128)(2,1)S(1)}, bf16[144,640]{1,0:T(8,128)(2,1)S(1)}, u32[]{:S(2)}, u32[]{:S(2)}) collective-permute-start(bf16[144,640]{1,0:T(8,128)(2,1)S(1)} %maximum_maximum_fusion), channel_id=1, source_target_pairs={{0,6},{1,7},{2,4},{3,5},{4,2},{5,3},{6,0},{7,1},{8,14},{9,15},{10,... | collective-permute-start | bytes 552968 | tf_op jit(solution)/shard_map/x_over_z/ppermute | solution.py:92
  9.0 1.3 fusion.94
  13.0 2.7 %dynamic-slice_bitcast_fusion = (bf16[1728,640]{1,0:T(8,128)(2,1)S(1)}, bf16[1728,640]{1,0:T(8,128)(2,1)S(1)}) fusion(bf16[1280,1728]{0,1:T(8,128)(2,1)} %param.9, s32[]{:T(128)S(6)} %select_n.53, s32[]{:T(128)S(6)} %select_n.52), kind=kLoop, calls=%fused_computation.2 | loop fusion | bytes 8847368 | tf_op jit(solution)/shard_map/dynamic_slice | solution.py:152
  15.8 7.4 %collective-permute-done.1 = bf16[144,640]{1,0:T(8,128)(2,1)S(1)} collective-permute-done((bf16[144,640]{1,0:T(8,128)(2,1)S(1)}, bf16[144,640]{1,0:T(8,128)(2,1)S(1)}, u32[]{:S(2)}, u32[]{:S(2)}) %collective-permute-start.1) | collective-permute-done | bytes 184352 | tf_op jit(solution)/shard_map/x_over_z/ppermute | solution.py:92
  23.9 1.1 pad_maximum_fusion.1
  25.9 0.9 collective-permute-done.3
  27.2 2.5 %collective-permute-start.6 = (bf16[128,640]{1,0:T(8,128)(2,1)S(1)}, bf16[128,640]{1,0:T(8,128)(2,1)S(1)}, u32[]{:S(2)}, u32[]{:S(2)}) collective-permute-start(bf16[128,640]{1,0:T(8,128)(2,1)S(1)} %get-tuple-element.138), channel_id=1, source_target_pairs={{0,24},{8,16},{16,8},{24,0},{1,25},{9,17},{17,9},{25,1},{2,26},{10... | collective-permute-start | bytes 491528 | tf_op jit(solution)/shard_map/modulated_over_row/ppermute | solution.py:89
  31.2 4.8 %constant_dynamic-slice_fusion.16 = (bf16[1728,640]{1,0:T(8,128)(2,1)}, bf16[1728,640]{1,0:T(8,128)(2,1)}) fusion(bf16[1728,1280]{1,0:T(8,128)(2,1)} %param.10, s32[]{:T(128)S(6)} %select_n.53, s32[]{:T(128)S(6)} %select_n.52), kind=kLoop, calls=%fused_computation.164 | loop fusion | bytes 8847368 | tf_op jit(solution)/shard_map/dynamic_slice | solution.py:152
  36.0 2.0 %collective-permute-done.5 = bf16[128,640]{1,0:T(8,128)(2,1)S(1)} collective-permute-done((bf16[128,640]{1,0:T(8,128)(2,1)S(1)}, bf16[128,640]{1,0:T(8,128)(2,1)S(1)}, u32[]{:S(2)}, u32[]{:S(2)}) %collective-permute-start.5) | collective-permute-done | bytes 163872 | tf_op jit(solution)/shard_map/modulated_over_row/ppermute | solution.py:89
  38.2 2.1 %collective-permute-done.7 = bf16[512,640]{1,0:T(8,128)(2,1)S(1)} collective-permute-done((bf16[512,640]{1,0:T(8,128)(2,1)S(1)}, bf16[512,640]{1,0:T(8,128)(2,1)S(1)}, u32[]{:S(2)}, u32[]{:S(2)}) %collective-permute-start.7) | collective-permute-done | bytes 655392 | tf_op jit(solution)/shard_map/ppermute | solution.py:95
  40.3 1.6 fusion.95
  42.0 1.7 add_convert_fusion.1
  43.7 1.2 copy-done.5
  46.5 1.5 collective-permute-start.8
  48.8 2.5 %collective-permute-start.18 = (bf16[128,640]{1,0:T(8,128)(2,1)S(1)}, bf16[128,640]{1,0:T(8,128)(2,1)S(1)}, u32[]{:S(2)}, u32[]{:S(2)}) collective-permute-start(bf16[128,640]{1,0:T(8,128)(2,1)S(1)} %get-tuple-element.45), channel_id=1, source_target_pairs={{0,6},{1,7},{2,4},{3,5},{4,2},{5,3},{6,0},{7,1},{8,14},{9,15},{10,... | collective-permute-start | bytes 491528 | tf_op jit(solution)/shard_map/z_grad_over_z/ppermute | solution.py:92
  51.2 1.9 %collective-permute-start.16 = (bf16[128,640]{1,0:T(8,128)(2,1)S(1)}, bf16[128,640]{1,0:T(8,128)(2,1)S(1)}, u32[]{:S(2)}, u32[]{:S(2)}) collective-permute-start(bf16[128,640]{1,0:T(8,128)(2,1)S(1)} %get-tuple-element.45), channel_id=1, source_target_pairs={{0,2},{1,3},{2,0},{3,1},{4,6},{5,7},{6,4},{7,5},{8,10},{9,11},{10,... | collective-permute-start | bytes 491528 | tf_op jit(solution)/shard_map/z_grad_over_z/ppermute | solution.py:92
  53.2 6.3 %collective-permute-done.8 = bf16[2,64,1728]{2,1,0:T(8,128)(2,1)} collective-permute-done((bf16[2,64,1728]{2,1,0:T(8,128)(2,1)}, bf16[2,64,1728]{2,1,0:T(8,128)(2,1)}, u32[]{:S(2)}, u32[]{:S(2)}) %collective-permute-start.8) | collective-permute-done | bytes 442400 | tf_op jit(solution)/shard_map/pre_act_scatter/ppermute | solution.py:89
  59.4 1.2 collective-permute-done.9
  60.6 1.4 add_convert_fusion.6
  62.8 1.2 collective-permute-start.11
  64.3 1.6 collective-permute-start.21
  65.8 1.2 collective-permute-start.20
  67.8 3.6 %collective-permute-done.10 = bf16[1,64,1728]{2,1,0:T(8,128)(2,1)S(1)} collective-permute-done((bf16[1,64,1728]{2,1,0:T(8,128)(2,1)S(1)}, bf16[1,64,1728]{2,1,0:T(8,128)(2,1)S(1)}, u32[]{:S(2)}, u32[]{:S(2)}) %collective-permute-start.10) | collective-permute-done | bytes 221216 | tf_op jit(solution)/shard_map/pre_act_scatter/ppermute | solution.py:89
  71.4 1.4 add_bitcast_fusion.3
  73.2 1.2 collective-permute-start.12
  75.6 1.1 collective-permute-done.20
  76.7 1.3 collective-permute-done.19
  78.1 2.8 %collective-permute-done.12 = bf16[1,64,1728]{2,1,0:T(8,128)(2,1)S(1)} collective-permute-done((bf16[1,64,1728]{2,1,0:T(8,128)(2,1)S(1)}, bf16[1,64,1728]{2,1,0:T(8,128)(2,1)S(1)}, u32[]{:S(2)}, u32[]{:S(2)}) %collective-permute-start.12) | collective-permute-done | bytes 221216 | tf_op jit(solution)/shard_map/activated_gather/ppermute | solution.py:89
  81.0 1.4 collective-permute-start.14
  83.1 1.6 fusion.96
  84.8 1.6 add_convert_fusion
  86.5 1.5 collective-permute-start.24
  88.7 5.8 %collective-permute-done.14 = bf16[2,64,1728]{2,1,0:T(8,128)(2,1)S(1)} collective-permute-done((bf16[2,64,1728]{2,1,0:T(8,128)(2,1)S(1)}, bf16[2,64,1728]{2,1,0:T(8,128)(2,1)S(1)}, u32[]{:S(2)}, u32[]{:S(2)}) %collective-permute-start.14) | collective-permute-done | bytes 442400 | tf_op jit(solution)/shard_map/activated_gather/ppermute | solution.py:89
  94.5 1.4 collective-permute-done.15
  96.1 1.6 fusion.97
  97.7 4.9 %collective-permute-done.24 = bf16[2,64,1728]{2,1,0:T(8,128)(2,1)S(1)} collective-permute-done((bf16[2,64,1728]{2,1,0:T(8,128)(2,1)S(1)}, bf16[2,64,1728]{2,1,0:T(8,128)(2,1)S(1)}, u32[]{:S(2)}, u32[]{:S(2)}) %collective-permute-start.24) | collective-permute-done | bytes 442400 | tf_op jit(solution)/shard_map/act_grad_scatter/ppermute | solution.py:89
  102.6 0.9 collective-permute-start.26
  103.6 1.1 collective-permute-start.27
  104.7 1.8 %convolution_convert_fusion.1 = bf16[512,640]{1,0:T(8,128)(2,1)S(1)} fusion(bf16[512,1728]{1,0:T(8,128)(2,1)S(1)} %bitcast_dynamic-update-slice_fusion.6, bf16[1728,640]{1,0:T(8,128)(2,1)S(1)} %copy-done.3), kind=kOutput, calls=%fused_computation.9 | convolution fusion | flops 1132789760 | bytes 4636672 | tf_op jit(solution)/shard_map/dot_general | solution.py:24
  106.6 2.2 %collective-permute-done.26 = bf16[1,64,1728]{2,1,0:T(8,128)(2,1)S(1)} collective-permute-done((bf16[1,64,1728]{2,1,0:T(8,128)(2,1)S(1)}, bf16[1,64,1728]{2,1,0:T(8,128)(2,1)S(1)}, u32[]{:S(2)}, u32[]{:S(2)}) %collective-permute-start.26) | collective-permute-done | bytes 221216 | tf_op jit(solution)/shard_map/act_grad_scatter/ppermute | solution.py:89
  110.4 1.2 collective-permute-start.33
  111.6 0.9 collective-permute-start.34
  112.7 1.6 collective-permute-start.30
  114.3 1.2 collective-permute-start.29
  116.3 2.7 %collective-permute-done.33 = bf16[1,64,1728]{2,1,0:T(8,128)(2,1)S(1)} collective-permute-done((bf16[1,64,1728]{2,1,0:T(8,128)(2,1)S(1)}, bf16[1,64,1728]{2,1,0:T(8,128)(2,1)S(1)}, u32[]{:S(2)}, u32[]{:S(2)}) %collective-permute-start.33) | collective-permute-done | bytes 221216 | tf_op jit(solution)/shard_map/pre_grad_gather/ppermute | solution.py:89
  119.0 2.3 %collective-permute-done.34 = bf16[1,64,1728]{2,1,0:T(8,128)(2,1)S(1)} collective-permute-done((bf16[1,64,1728]{2,1,0:T(8,128)(2,1)S(1)}, bf16[1,64,1728]{2,1,0:T(8,128)(2,1)S(1)}, u32[]{:S(2)}, u32[]{:S(2)}) %collective-permute-start.34) | collective-permute-done | bytes 221216 | tf_op jit(solution)/shard_map/pre_grad_gather/ppermute | solution.py:89
  121.4 1.2 collective-permute-start.35
  123.4 2.2 %collective-permute-done.29 = bf16[128,640]{1,0:T(8,128)(2,1)S(1)} collective-permute-done((bf16[128,640]{1,0:T(8,128)(2,1)S(1)}, bf16[128,640]{1,0:T(8,128)(2,1)S(1)}, u32[]{:S(2)}, u32[]{:S(2)}) %collective-permute-start.29) | collective-permute-done | bytes 163872 | tf_op jit(solution)/shard_map/projected_home/ppermute | solution.py:89
  126.3 6.6 %collective-permute-done.35 = bf16[2,64,1728]{2,1,0:T(8,128)(2,1)S(1)} collective-permute-done((bf16[2,64,1728]{2,1,0:T(8,128)(2,1)S(1)}, bf16[2,64,1728]{2,1,0:T(8,128)(2,1)S(1)}, u32[]{:S(2)}, u32[]{:S(2)}) %collective-permute-start.35) | collective-permute-done | bytes 442400 | tf_op jit(solution)/shard_map/pre_grad_gather/ppermute | solution.py:89
  133.0 1.6 convolution_convert_fusion
  134.7 1.6 fusion.98
  137.0 1.5 collective-permute-start.40
  138.5 1.2 collective-permute-start.39
  139.7 0.9 collective-permute-start.38
  140.7 4.4 %collective-permute-done.40 = bf16[128,640]{1,0:T(8,128)(2,1)S(1)} collective-permute-done((bf16[128,640]{1,0:T(8,128)(2,1)S(1)}, bf16[128,640]{1,0:T(8,128)(2,1)S(1)}, u32[]{:S(2)}, u32[]{:S(2)}) %collective-permute-start.40) | collective-permute-done | bytes 163872 | tf_op jit(solution)/shard_map/in_grad_to_row/ppermute | solution.py:89
  145.0 2.7 %collective-permute-done.39 = bf16[128,640]{1,0:T(8,128)(2,1)S(1)} collective-permute-done((bf16[128,640]{1,0:T(8,128)(2,1)S(1)}, bf16[128,640]{1,0:T(8,128)(2,1)S(1)}, u32[]{:S(2)}, u32[]{:S(2)}) %collective-permute-start.39) | collective-permute-done | bytes 163872 | tf_op jit(solution)/shard_map/in_grad_to_row/ppermute | solution.py:89
  148.9 1.0 collective-permute-done.42
  150.1 2.2 %collective-permute-start.45 = (f32[2,128]{1,0:T(2,128)S(1)}, f32[2,128]{1,0:T(2,128)S(1)}, u32[]{:S(2)}, u32[]{:S(2)}) collective-permute-start(f32[2,128]{1,0:T(2,128)S(1)} %fusion.88), channel_id=1, source_target_pairs={{0,6},{1,7},{2,4},{3,5},{4,2},{5,3},{6,0},{7,1},{8,14},{9,15},{10,... | collective-permute-start | bytes 3080 | tf_op jit(solution)/shard_map/norm_sums/ppermute | solution.py:92
  152.5 2.0 %collective-permute-start.44 = (f32[2,128]{1,0:T(2,128)S(1)}, f32[2,128]{1,0:T(2,128)S(1)}, u32[]{:S(2)}, u32[]{:S(2)}) collective-permute-start(f32[2,128]{1,0:T(2,128)S(1)} %fusion.88), channel_id=1, source_target_pairs={{0,4},{1,5},{2,6},{3,7},{4,0},{5,1},{6,2},{7,3},{8,12},{9,13},{10,... | collective-permute-start | bytes 3080 | tf_op jit(solution)/shard_map/norm_sums/ppermute | solution.py:92
  154.6 5.1 %collective-permute-done.45 = f32[2,128]{1,0:T(2,128)S(1)} collective-permute-done((f32[2,128]{1,0:T(2,128)S(1)}, f32[2,128]{1,0:T(2,128)S(1)}, u32[]{:S(2)}, u32[]{:S(2)}) %collective-permute-start.45) | collective-permute-done | bytes 1056 | tf_op jit(solution)/shard_map/norm_sums/ppermute | solution.py:92
  160.4 9.5 %collective-permute-done.46 = bf16[1,128,640]{2,1,0:T(8,128)(2,1)S(1)} collective-permute-done((bf16[1,128,640]{2,1,0:T(8,128)(2,1)S(1)}, bf16[1,128,640]{2,1,0:T(8,128)(2,1)S(1)}, u32[]{:S(2)}, u32[]{:S(2)}) %collective-permute-start.46) | collective-permute-done | bytes 163872 | tf_op jit(solution)/shard_map/in_grad_over_z/ppermute | solution.py:92
  169.9 0.9 fusion.21
  170.9 1.0 multiply_reduce_fusion.3
  (142 shorter events, 23.1 us)
Async XLA Ops:
  2.4 13.4 %collective-permute-start.2 = (bf16[144,640]{1,0:T(8,128)(2,1)S(1)}, bf16[144,640]{1,0:T(8,128)(2,1)S(1)}, u32[]{:S(2)}, u32[]{:S(2)}) collective-permute-start(bf16[144,640]{1,0:T(8,128)(2,1)S(1)} %maximum_maximum_fusion), channel_id=1, source_target_pairs={{0,6},{1,7},{2,4},{3,5},{4,2},{5,3},{6,0},{7,1},{8,14},{9,15},{10,... | collective-permute-start | bytes 552968 | tf_op jit(solution)/shard_map/x_over_z/ppermute | solution.py:92
  7.6 15.6 %collective-permute-start.1 = (bf16[144,640]{1,0:T(8,128)(2,1)S(1)}, bf16[144,640]{1,0:T(8,128)(2,1)S(1)}, u32[]{:S(2)}, u32[]{:S(2)}) collective-permute-start(bf16[144,640]{1,0:T(8,128)(2,1)S(1)} %maximum_maximum_fusion), channel_id=1, source_target_pairs={{0,4},{1,5},{2,6},{3,7},{4,0},{5,1},{6,2},{7,3},{8,12},{9,13},{10,... | collective-permute-start | bytes 552968 | tf_op jit(solution)/shard_map/x_over_z/ppermute | solution.py:92
  7.6 15.6 %collective-permute-start = (bf16[144,640]{1,0:T(8,128)(2,1)S(1)}, bf16[144,640]{1,0:T(8,128)(2,1)S(1)}, u32[]{:S(2)}, u32[]{:S(2)}) collective-permute-start(bf16[144,640]{1,0:T(8,128)(2,1)S(1)} %maximum_maximum_fusion), channel_id=1, source_target_pairs={{0,2},{1,3},{2,0},{3,1},{4,6},{5,7},{6,4},{7,5},{8,10},{9,11},{10,... | collective-permute-start | bytes 552968 | tf_op jit(solution)/shard_map/x_over_z/ppermute | solution.py:92
  13.0 2.7 %copy-start = (bf16[128,640]{1,0:T(8,128)(2,1)S(1)}, bf16[128,640]{1,0:T(8,128)(2,1)}, u32[]{:S(2)}) copy-start(bf16[128,640]{1,0:T(8,128)(2,1)} %param.6) | copy-start | bytes 491524
  15.7 24.6 %copy-start.1 = (bf16[1728,640]{1,0:T(8,128)(2,1)}, bf16[1728,640]{1,0:T(8,128)(2,1)S(1)}, u32[]{:S(2)}) copy-start(bf16[1728,640]{1,0:T(8,128)(2,1)S(1)} %get-tuple-element.121) | copy-start | bytes 6635524
  15.7 11.1 %copy-start.6 = (bf16[128,640]{1,0:T(8,128)(2,1)S(1)}, bf16[128,640]{1,0:T(8,128)(2,1)}, u32[]{:S(2)}) copy-start(bf16[128,640]{1,0:T(8,128)(2,1)} %param.11) | copy-start | bytes 491524
  23.2 0.7 copy-start.7
  23.2 0.7 copy-start.8
  25.6 1.2 collective-permute-start.3
  27.2 8.8 %collective-permute-start.6 = (bf16[128,640]{1,0:T(8,128)(2,1)S(1)}, bf16[128,640]{1,0:T(8,128)(2,1)S(1)}, u32[]{:S(2)}, u32[]{:S(2)}) collective-permute-start(bf16[128,640]{1,0:T(8,128)(2,1)S(1)} %get-tuple-element.138), channel_id=1, source_target_pairs={{0,24},{8,16},{16,8},{24,0},{1,25},{9,17},{17,9},{25,1},{2,26},{10... | collective-permute-start | bytes 491528 | tf_op jit(solution)/shard_map/modulated_over_row/ppermute | solution.py:89
  29.7 8.3 %collective-permute-start.5 = (bf16[128,640]{1,0:T(8,128)(2,1)S(1)}, bf16[128,640]{1,0:T(8,128)(2,1)S(1)}, u32[]{:S(2)}, u32[]{:S(2)}) collective-permute-start(bf16[128,640]{1,0:T(8,128)(2,1)S(1)} %get-tuple-element.137), channel_id=1, source_target_pairs={{0,16},{8,24},{16,0},{24,8},{1,17},{9,25},{17,1},{25,9},{2,18},{10... | collective-permute-start | bytes 491528 | tf_op jit(solution)/shard_map/modulated_over_row/ppermute | solution.py:89
  30.6 7.5 %collective-permute-start.4 = (bf16[128,640]{1,0:T(8,128)(2,1)S(1)}, bf16[128,640]{1,0:T(8,128)(2,1)S(1)}, u32[]{:S(2)}, u32[]{:S(2)}) collective-permute-start(bf16[128,640]{1,0:T(8,128)(2,1)S(1)} %get-tuple-element.136), channel_id=1, source_target_pairs={{0,8},{8,0},{16,24},{24,16},{1,9},{9,1},{17,25},{25,17},{2,10},{10... | collective-permute-start | bytes 491528 | tf_op jit(solution)/shard_map/modulated_over_row/ppermute | solution.py:89
  38.2 2.2 %collective-permute-start.7 = (bf16[512,640]{1,0:T(8,128)(2,1)S(1)}, bf16[512,640]{1,0:T(8,128)(2,1)S(1)}, u32[]{:S(2)}, u32[]{:S(2)}) collective-permute-start(bf16[512,640]{1,0:T(8,128)(2,1)S(1)} %pad_maximum_fusion.2), channel_id=1, source_target_pairs={{0,1},{1,0},{2,3},{3,2},{4,5},{5,4},{6,7},{7,6},{8,9},{9,8},{10,11... | collective-permute-start | bytes 1966088 | tf_op jit(solution)/shard_map/ppermute | solution.py:95
  43.6 1.2 copy-start.5
  46.5 12.9 %collective-permute-start.8 = (bf16[2,64,1728]{2,1,0:T(8,128)(2,1)}, bf16[2,64,1728]{2,1,0:T(8,128)(2,1)}, u32[]{:S(2)}, u32[]{:S(2)}) collective-permute-start(bf16[2,64,1728]{2,1,0:T(8,128)(2,1)} %pad_maximum_fusion.7), channel_id=1, source_target_pairs={{0,8},{8,0},{16,24},{24,16},{1,9},{9,1},{17,25},{25,17},{2,10},{10... | collective-permute-start | bytes 1327112 | tf_op jit(solution)/shard_map/pre_act_scatter/ppermute | solution.py:89
  48.0 12.6 %collective-permute-start.9 = (bf16[2,64,1728]{2,1,0:T(8,128)(2,1)}, bf16[2,64,1728]{2,1,0:T(8,128)(2,1)}, u32[]{:S(2)}, u32[]{:S(2)}) collective-permute-start(bf16[2,64,1728]{2,1,0:T(8,128)(2,1)} %stack.209), channel_id=1, source_target_pairs={{0,16},{8,24},{16,0},{24,8},{1,17},{9,25},{17,1},{25,9},{2,18},{10... | collective-permute-start | bytes 1327112 | tf_op jit(solution)/shard_map/pre_act_scatter/ppermute | solution.py:89
  48.8 15.3 %collective-permute-start.18 = (bf16[128,640]{1,0:T(8,128)(2,1)S(1)}, bf16[128,640]{1,0:T(8,128)(2,1)S(1)}, u32[]{:S(2)}, u32[]{:S(2)}) collective-permute-start(bf16[128,640]{1,0:T(8,128)(2,1)S(1)} %get-tuple-element.45), channel_id=1, source_target_pairs={{0,6},{1,7},{2,4},{3,5},{4,2},{5,3},{6,0},{7,1},{8,14},{9,15},{10,... | collective-permute-start | bytes 491528 | tf_op jit(solution)/shard_map/z_grad_over_z/ppermute | solution.py:92
  51.2 12.8 %collective-permute-start.17 = (bf16[128,640]{1,0:T(8,128)(2,1)S(1)}, bf16[128,640]{1,0:T(8,128)(2,1)S(1)}, u32[]{:S(2)}, u32[]{:S(2)}) collective-permute-start(bf16[128,640]{1,0:T(8,128)(2,1)S(1)} %get-tuple-element.45), channel_id=1, source_target_pairs={{0,4},{1,5},{2,6},{3,7},{4,0},{5,1},{6,2},{7,3},{8,12},{9,13},{10,... | collective-permute-start | bytes 491528 | tf_op jit(solution)/shard_map/z_grad_over_z/ppermute | solution.py:92
  51.2 12.8 %collective-permute-start.16 = (bf16[128,640]{1,0:T(8,128)(2,1)S(1)}, bf16[128,640]{1,0:T(8,128)(2,1)S(1)}, u32[]{:S(2)}, u32[]{:S(2)}) collective-permute-start(bf16[128,640]{1,0:T(8,128)(2,1)S(1)} %get-tuple-element.45), channel_id=1, source_target_pairs={{0,2},{1,3},{2,0},{3,1},{4,6},{5,7},{6,4},{7,5},{8,10},{9,11},{10,... | collective-permute-start | bytes 491528 | tf_op jit(solution)/shard_map/z_grad_over_z/ppermute | solution.py:92
  62.0 9.4 %collective-permute-start.10 = (bf16[1,64,1728]{2,1,0:T(8,128)(2,1)S(1)}, bf16[1,64,1728]{2,1,0:T(8,128)(2,1)S(1)}, u32[]{:S(2)}, u32[]{:S(2)}) collective-permute-start(bf16[1,64,1728]{2,1,0:T(8,128)(2,1)S(1)} %get-tuple-element.132), channel_id=1, source_target_pairs={{0,16},{8,24},{16,0},{24,8},{1,17},{9,25},{17,1},{25,9},{2,18},{10... | collective-permute-start | bytes 663560 | tf_op jit(solution)/shard_map/pre_act_scatter/ppermute | solution.py:89
  62.8 8.6 %collective-permute-start.11 = (bf16[1,64,1728]{2,1,0:T(8,128)(2,1)S(1)}, bf16[1,64,1728]{2,1,0:T(8,128)(2,1)S(1)}, u32[]{:S(2)}, u32[]{:S(2)}) collective-permute-start(bf16[1,64,1728]{2,1,0:T(8,128)(2,1)S(1)} %get-tuple-element.131), channel_id=1, source_target_pairs={{0,8},{8,0},{16,24},{24,16},{1,9},{9,1},{17,25},{25,17},{2,10},{10... | collective-permute-start | bytes 663560 | tf_op jit(solution)/shard_map/pre_act_scatter/ppermute | solution.py:89
  64.3 11.3 %collective-permute-start.21 = (bf16[128,640]{1,0:T(8,128)(2,1)S(1)}, bf16[128,640]{1,0:T(8,128)(2,1)S(1)}, u32[]{:S(2)}, u32[]{:S(2)}) collective-permute-start(bf16[128,640]{1,0:T(8,128)(2,1)S(1)} %get-tuple-element.150), channel_id=1, source_target_pairs={{0,24},{8,16},{16,8},{24,0},{1,25},{9,17},{17,9},{25,1},{2,26},{10... | collective-permute-start | bytes 491528 | tf_op jit(solution)/shard_map/z_grad_over_row/ppermute | solution.py:89
  65.8 10.9 %collective-permute-start.20 = (bf16[128,640]{1,0:T(8,128)(2,1)S(1)}, bf16[128,640]{1,0:T(8,128)(2,1)S(1)}, u32[]{:S(2)}, u32[]{:S(2)}) collective-permute-start(bf16[128,640]{1,0:T(8,128)(2,1)S(1)} %get-tuple-element.151), channel_id=1, source_target_pairs={{0,16},{8,24},{16,0},{24,8},{1,17},{9,25},{17,1},{25,9},{2,18},{10... | collective-permute-start | bytes 491528 | tf_op jit(solution)/shard_map/z_grad_over_row/ppermute | solution.py:89
  67.0 10.9 %collective-permute-start.19 = (bf16[128,640]{1,0:T(8,128)(2,1)S(1)}, bf16[128,640]{1,0:T(8,128)(2,1)S(1)}, u32[]{:S(2)}, u32[]{:S(2)}) collective-permute-start(bf16[128,640]{1,0:T(8,128)(2,1)S(1)} %get-tuple-element.152), channel_id=1, source_target_pairs={{0,8},{8,0},{16,24},{24,16},{1,9},{9,1},{17,25},{25,17},{2,10},{10... | collective-permute-start | bytes 491528 | tf_op jit(solution)/shard_map/z_grad_over_row/ppermute | solution.py:89
  73.2 9.9 %copy-start.3 = (bf16[1728,640]{1,0:T(8,128)(2,1)S(1)}, bf16[1728,640]{1,0:T(8,128)(2,1)}, u32[]{:S(2)}) copy-start(bf16[1728,640]{1,0:T(8,128)(2,1)} %get-tuple-element.119) | copy-start | bytes 6635524
  73.2 7.7 %collective-permute-start.12 = (bf16[1,64,1728]{2,1,0:T(8,128)(2,1)S(1)}, bf16[1,64,1728]{2,1,0:T(8,128)(2,1)S(1)}, u32[]{:S(2)}, u32[]{:S(2)}) collective-permute-start(bf16[1,64,1728]{2,1,0:T(8,128)(2,1)S(1)} %get-tuple-element.157), channel_id=1, source_target_pairs={{0,8},{8,0},{16,24},{24,16},{1,9},{9,1},{17,25},{25,17},{2,10},{10... | collective-permute-start | bytes 663560 | tf_op jit(solution)/shard_map/activated_gather/ppermute | solution.py:89
  74.4 6.5 %collective-permute-start.13 = (bf16[1,64,1728]{2,1,0:T(8,128)(2,1)S(1)}, bf16[1,64,1728]{2,1,0:T(8,128)(2,1)S(1)}, u32[]{:S(2)}, u32[]{:S(2)}) collective-permute-start(bf16[1,64,1728]{2,1,0:T(8,128)(2,1)S(1)} %get-tuple-element.156), channel_id=1, source_target_pairs={{0,16},{8,24},{16,0},{24,8},{1,17},{9,25},{17,1},{25,9},{2,18},{10... | collective-permute-start | bytes 663560 | tf_op jit(solution)/shard_map/activated_gather/ppermute | solution.py:89
  78.0 5.1 %collective-permute-start.22 = (bf16[512,640]{1,0:T(8,128)(2,1)S(1)}, bf16[512,640]{1,0:T(8,128)(2,1)S(1)}, u32[]{:S(2)}, u32[]{:S(2)}) collective-permute-start(bf16[512,640]{1,0:T(8,128)(2,1)S(1)} %pad_maximum_fusion.4), channel_id=1, source_target_pairs={{0,1},{1,0},{2,3},{3,2},{4,5},{5,4},{6,7},{7,6},{8,9},{9,8},{10,11... | collective-permute-start | bytes 1966088 | tf_op jit(solution)/shard_map/ppermute | solution.py:95
  81.0 13.5 %collective-permute-start.14 = (bf16[2,64,1728]{2,1,0:T(8,128)(2,1)S(1)}, bf16[2,64,1728]{2,1,0:T(8,128)(2,1)S(1)}, u32[]{:S(2)}, u32[]{:S(2)}) collective-permute-start(bf16[2,64,1728]{2,1,0:T(8,128)(2,1)S(1)} %pad_maximum_fusion.8), channel_id=1, source_target_pairs={{0,16},{8,24},{16,0},{24,8},{1,17},{9,25},{17,1},{25,9},{2,18},{10... | collective-permute-start | bytes 1327112 | tf_op jit(solution)/shard_map/activated_gather/ppermute | solution.py:89
  82.4 13.5 %collective-permute-start.15 = (bf16[2,64,1728]{2,1,0:T(8,128)(2,1)S(1)}, bf16[2,64,1728]{2,1,0:T(8,128)(2,1)S(1)}, u32[]{:S(2)}, u32[]{:S(2)}) collective-permute-start(bf16[2,64,1728]{2,1,0:T(8,128)(2,1)S(1)} %pad_maximum_fusion.9), channel_id=1, source_target_pairs={{0,8},{8,0},{16,24},{24,16},{1,9},{9,1},{17,25},{25,17},{2,10},{10... | collective-permute-start | bytes 1327112 | tf_op jit(solution)/shard_map/activated_gather/ppermute | solution.py:89
  83.1 1.7 copy-start.4
  86.5 16.0 %collective-permute-start.24 = (bf16[2,64,1728]{2,1,0:T(8,128)(2,1)S(1)}, bf16[2,64,1728]{2,1,0:T(8,128)(2,1)S(1)}, u32[]{:S(2)}, u32[]{:S(2)}) collective-permute-start(bf16[2,64,1728]{2,1,0:T(8,128)(2,1)S(1)} %pad_maximum_fusion.10), channel_id=1, source_target_pairs={{0,8},{8,0},{16,24},{24,16},{1,9},{9,1},{17,25},{25,17},{2,10},{10... | collective-permute-start | bytes 1327112 | tf_op jit(solution)/shard_map/act_grad_scatter/ppermute | solution.py:89
  88.0 14.5 %collective-permute-start.25 = (bf16[2,64,1728]{2,1,0:T(8,128)(2,1)S(1)}, bf16[2,64,1728]{2,1,0:T(8,128)(2,1)S(1)}, u32[]{:S(2)}, u32[]{:S(2)}) collective-permute-start(bf16[2,64,1728]{2,1,0:T(8,128)(2,1)S(1)} %stack.210), channel_id=1, source_target_pairs={{0,16},{8,24},{16,0},{24,8},{1,17},{9,25},{17,1},{25,9},{2,18},{10... | collective-permute-start | bytes 1327112 | tf_op jit(solution)/shard_map/act_grad_scatter/ppermute | solution.py:89
  102.6 6.1 %collective-permute-start.26 = (bf16[1,64,1728]{2,1,0:T(8,128)(2,1)S(1)}, bf16[1,64,1728]{2,1,0:T(8,128)(2,1)S(1)}, u32[]{:S(2)}, u32[]{:S(2)}) collective-permute-start(bf16[1,64,1728]{2,1,0:T(8,128)(2,1)S(1)} %get-tuple-element.50), channel_id=1, source_target_pairs={{0,16},{8,24},{16,0},{24,8},{1,17},{9,25},{17,1},{25,9},{2,18},{10... | collective-permute-start | bytes 663560 | tf_op jit(solution)/shard_map/act_grad_scatter/ppermute | solution.py:89
  103.6 6.0 %collective-permute-start.27 = (bf16[1,64,1728]{2,1,0:T(8,128)(2,1)S(1)}, bf16[1,64,1728]{2,1,0:T(8,128)(2,1)S(1)}, u32[]{:S(2)}, u32[]{:S(2)}) collective-permute-start(bf16[1,64,1728]{2,1,0:T(8,128)(2,1)S(1)} %get-tuple-element.52), channel_id=1, source_target_pairs={{0,8},{8,0},{16,24},{24,16},{1,9},{9,1},{17,25},{25,17},{2,10},{10... | collective-permute-start | bytes 663560 | tf_op jit(solution)/shard_map/act_grad_scatter/ppermute | solution.py:89
  106.5 6.0 %collective-permute-start.23 = (bf16[512,640]{1,0:T(8,128)(2,1)S(1)}, bf16[512,640]{1,0:T(8,128)(2,1)S(1)}, u32[]{:S(2)}, u32[]{:S(2)}) collective-permute-start(bf16[512,640]{1,0:T(8,128)(2,1)S(1)} %convolution_convert_fusion.1), channel_id=1, source_target_pairs={{0,1},{1,0},{2,3},{3,2},{4,5},{5,4},{6,7},{7,6},{8,9},{9,8},{10,11... | collective-permute-start | bytes 1966088 | tf_op jit(solution)/shard_map/ppermute | solution.py:95
  110.4 8.6 %collective-permute-start.33 = (bf16[1,64,1728]{2,1,0:T(8,128)(2,1)S(1)}, bf16[1,64,1728]{2,1,0:T(8,128)(2,1)S(1)}, u32[]{:S(2)}, u32[]{:S(2)}) collective-permute-start(bf16[1,64,1728]{2,1,0:T(8,128)(2,1)S(1)} %get-tuple-element.155), channel_id=1, source_target_pairs={{0,8},{8,0},{16,24},{24,16},{1,9},{9,1},{17,25},{25,17},{2,10},{10... | collective-permute-start | bytes 663560 | tf_op jit(solution)/shard_map/pre_grad_gather/ppermute | solution.py:89
  111.6 9.7 %collective-permute-start.34 = (bf16[1,64,1728]{2,1,0:T(8,128)(2,1)S(1)}, bf16[1,64,1728]{2,1,0:T(8,128)(2,1)S(1)}, u32[]{:S(2)}, u32[]{:S(2)}) collective-permute-start(bf16[1,64,1728]{2,1,0:T(8,128)(2,1)S(1)} %get-tuple-element.154), channel_id=1, source_target_pairs={{0,16},{8,24},{16,0},{24,8},{1,17},{9,25},{17,1},{25,9},{2,18},{10... | collective-permute-start | bytes 663560 | tf_op jit(solution)/shard_map/pre_grad_gather/ppermute | solution.py:89
  112.7 10.6 %collective-permute-start.30 = (bf16[128,640]{1,0:T(8,128)(2,1)S(1)}, bf16[128,640]{1,0:T(8,128)(2,1)S(1)}, u32[]{:S(2)}, u32[]{:S(2)}) collective-permute-start(bf16[128,640]{1,0:T(8,128)(2,1)S(1)} %get-tuple-element.146), channel_id=1, source_target_pairs={{0,24},{8,16},{16,8},{24,0},{1,25},{9,17},{17,9},{25,1},{2,26},{10... | collective-permute-start | bytes 491528 | tf_op jit(solution)/shard_map/projected_home/ppermute | solution.py:89
  114.3 11.3 %collective-permute-start.29 = (bf16[128,640]{1,0:T(8,128)(2,1)S(1)}, bf16[128,640]{1,0:T(8,128)(2,1)S(1)}, u32[]{:S(2)}, u32[]{:S(2)}) collective-permute-start(bf16[128,640]{1,0:T(8,128)(2,1)S(1)} %get-tuple-element.147), channel_id=1, source_target_pairs={{0,16},{8,24},{16,0},{24,8},{1,17},{9,25},{17,1},{25,9},{2,18},{10... | collective-permute-start | bytes 491528 | tf_op jit(solution)/shard_map/projected_home/ppermute | solution.py:89
  115.5 10.6 %collective-permute-start.28 = (bf16[128,640]{1,0:T(8,128)(2,1)S(1)}, bf16[128,640]{1,0:T(8,128)(2,1)S(1)}, u32[]{:S(2)}, u32[]{:S(2)}) collective-permute-start(bf16[128,640]{1,0:T(8,128)(2,1)S(1)} %get-tuple-element.148), channel_id=1, source_target_pairs={{0,8},{8,0},{16,24},{24,16},{1,9},{9,1},{17,25},{25,17},{2,10},{10... | collective-permute-start | bytes 491528 | tf_op jit(solution)/shard_map/projected_home/ppermute | solution.py:89
  121.4 11.5 %collective-permute-start.35 = (bf16[2,64,1728]{2,1,0:T(8,128)(2,1)S(1)}, bf16[2,64,1728]{2,1,0:T(8,128)(2,1)S(1)}, u32[]{:S(2)}, u32[]{:S(2)}) collective-permute-start(bf16[2,64,1728]{2,1,0:T(8,128)(2,1)S(1)} %get-tuple-element.58), channel_id=1, source_target_pairs={{0,16},{8,24},{16,0},{24,8},{1,17},{9,25},{17,1},{25,9},{2,18},{10... | collective-permute-start | bytes 1327112 | tf_op jit(solution)/shard_map/pre_grad_gather/ppermute | solution.py:89
  122.6 10.3 %collective-permute-start.36 = (bf16[2,64,1728]{2,1,0:T(8,128)(2,1)S(1)}, bf16[2,64,1728]{2,1,0:T(8,128)(2,1)S(1)}, u32[]{:S(2)}, u32[]{:S(2)}) collective-permute-start(bf16[2,64,1728]{2,1,0:T(8,128)(2,1)S(1)} %get-tuple-element.60), channel_id=1, source_target_pairs={{0,8},{8,0},{16,24},{24,16},{1,9},{9,1},{17,25},{25,17},{2,10},{10... | collective-permute-start | bytes 1327112 | tf_op jit(solution)/shard_map/pre_grad_gather/ppermute | solution.py:89
  126.2 6.9 %copy-start.2 = (bf16[1728,640]{1,0:T(8,128)(2,1)S(1)}, bf16[1728,640]{1,0:T(8,128)(2,1)}, u32[]{:S(2)}) copy-start(bf16[1728,640]{1,0:T(8,128)(2,1)} %copy-done.1) | copy-start | bytes 6635524
  126.2 8.5 %collective-permute-start.31 = (bf16[2,128,640]{2,1,0:T(8,128)(2,1)S(1)}, bf16[2,128,640]{2,1,0:T(8,128)(2,1)S(1)}, u32[]{:S(2)}, u32[]{:S(2)}) collective-permute-start(bf16[2,128,640]{2,1,0:T(8,128)(2,1)S(1)} %pad_maximum_fusion.13), channel_id=1, source_target_pairs={{0,2},{1,3},{2,0},{3,1},{4,6},{5,7},{6,4},{7,5},{8,10},{9,11},{10,... | collective-permute-start | bytes 983048 | tf_op jit(solution)/shard_map/projected_home/ppermute | solution.py:92
  134.6 2.2 %collective-permute-start.37 = (bf16[512,640]{1,0:T(8,128)(2,1)S(1)}, bf16[512,640]{1,0:T(8,128)(2,1)S(1)}, u32[]{:S(2)}, u32[]{:S(2)}) collective-permute-start(bf16[512,640]{1,0:T(8,128)(2,1)S(1)} %convolution_convert_fusion), channel_id=1, source_target_pairs={{0,1},{1,0},{2,3},{3,2},{4,5},{5,4},{6,7},{7,6},{8,9},{9,8},{10,11... | collective-permute-start | bytes 1966088 | tf_op jit(solution)/shard_map/ppermute | solution.py:95
  137.0 8.1 %collective-permute-start.40 = (bf16[128,640]{1,0:T(8,128)(2,1)S(1)}, bf16[128,640]{1,0:T(8,128)(2,1)S(1)}, u32[]{:S(2)}, u32[]{:S(2)}) collective-permute-start(bf16[128,640]{1,0:T(8,128)(2,1)S(1)} %get-tuple-element.140), channel_id=1, source_target_pairs={{0,24},{8,16},{16,8},{24,0},{1,25},{9,17},{17,9},{25,1},{2,26},{10... | collective-permute-start | bytes 491528 | tf_op jit(solution)/shard_map/in_grad_to_row/ppermute | solution.py:89
  138.5 9.2 %collective-permute-start.39 = (bf16[128,640]{1,0:T(8,128)(2,1)S(1)}, bf16[128,640]{1,0:T(8,128)(2,1)S(1)}, u32[]{:S(2)}, u32[]{:S(2)}) collective-permute-start(bf16[128,640]{1,0:T(8,128)(2,1)S(1)} %get-tuple-element.141), channel_id=1, source_target_pairs={{0,16},{8,24},{16,0},{24,8},{1,17},{9,25},{17,1},{25,9},{2,18},{10... | collective-permute-start | bytes 491528 | tf_op jit(solution)/shard_map/in_grad_to_row/ppermute | solution.py:89
  139.7 8.1 %collective-permute-start.38 = (bf16[128,640]{1,0:T(8,128)(2,1)S(1)}, bf16[128,640]{1,0:T(8,128)(2,1)S(1)}, u32[]{:S(2)}, u32[]{:S(2)}) collective-permute-start(bf16[128,640]{1,0:T(8,128)(2,1)S(1)} %get-tuple-element.142), channel_id=1, source_target_pairs={{0,8},{8,0},{16,24},{24,16},{1,9},{9,1},{17,25},{25,17},{2,10},{10... | collective-permute-start | bytes 491528 | tf_op jit(solution)/shard_map/in_grad_to_row/ppermute | solution.py:89
  140.6 9.5 %collective-permute-start.32 = (bf16[1,128,640]{2,1,0:T(8,128)(2,1)S(1)}, bf16[1,128,640]{2,1,0:T(8,128)(2,1)S(1)}, u32[]{:S(2)}, u32[]{:S(2)}) collective-permute-start(bf16[1,128,640]{2,1,0:T(8,128)(2,1)S(1)} %add_convert_fusion.8), channel_id=1, source_target_pairs={{0,4},{1,5},{2,6},{3,7},{4,0},{5,1},{6,2},{7,3},{8,12},{9,13},{10,... | collective-permute-start | bytes 491528 | tf_op jit(solution)/shard_map/projected_home/ppermute | solution.py:92
  148.7 1.2 collective-permute-start.42
  148.8 10.8 %collective-permute-start.41 = (bf16[2,128,640]{2,1,0:T(8,128)(2,1)S(1)}, bf16[2,128,640]{2,1,0:T(8,128)(2,1)S(1)}, u32[]{:S(2)}, u32[]{:S(2)}) collective-permute-start(bf16[2,128,640]{2,1,0:T(8,128)(2,1)S(1)} %pad_maximum_fusion.14), channel_id=1, source_target_pairs={{0,2},{1,3},{2,0},{3,1},{4,6},{5,7},{6,4},{7,5},{8,10},{9,11},{10,... | collective-permute-start | bytes 983048 | tf_op jit(solution)/shard_map/in_grad_over_z/ppermute | solution.py:92
  150.1 9.5 %collective-permute-start.45 = (f32[2,128]{1,0:T(2,128)S(1)}, f32[2,128]{1,0:T(2,128)S(1)}, u32[]{:S(2)}, u32[]{:S(2)}) collective-permute-start(f32[2,128]{1,0:T(2,128)S(1)} %fusion.88), channel_id=1, source_target_pairs={{0,6},{1,7},{2,4},{3,5},{4,2},{5,3},{6,0},{7,1},{8,14},{9,15},{10,... | collective-permute-start | bytes 3080 | tf_op jit(solution)/shard_map/norm_sums/ppermute | solution.py:92
  152.4 7.3 %collective-permute-start.43 = (f32[2,128]{1,0:T(2,128)S(1)}, f32[2,128]{1,0:T(2,128)S(1)}, u32[]{:S(2)}, u32[]{:S(2)}) collective-permute-start(f32[2,128]{1,0:T(2,128)S(1)} %fusion.88), channel_id=1, source_target_pairs={{0,2},{1,3},{2,0},{3,1},{4,6},{5,7},{6,4},{7,5},{8,10},{9,11},{10,... | collective-permute-start | bytes 3080 | tf_op jit(solution)/shard_map/norm_sums/ppermute | solution.py:92
  152.5 7.2 %collective-permute-start.44 = (f32[2,128]{1,0:T(2,128)S(1)}, f32[2,128]{1,0:T(2,128)S(1)}, u32[]{:S(2)}, u32[]{:S(2)}) collective-permute-start(f32[2,128]{1,0:T(2,128)S(1)} %fusion.88), channel_id=1, source_target_pairs={{0,4},{1,5},{2,6},{3,7},{4,0},{5,1},{6,2},{7,3},{8,12},{9,13},{10,... | collective-permute-start | bytes 3080 | tf_op jit(solution)/shard_map/norm_sums/ppermute | solution.py:92
  159.7 10.2 %collective-permute-start.46 = (bf16[1,128,640]{2,1,0:T(8,128)(2,1)S(1)}, bf16[1,128,640]{2,1,0:T(8,128)(2,1)S(1)}, u32[]{:S(2)}, u32[]{:S(2)}) collective-permute-start(bf16[1,128,640]{2,1,0:T(8,128)(2,1)S(1)} %fusion.16), channel_id=1, source_target_pairs={{0,4},{1,5},{2,6},{3,7},{4,0},{5,1},{6,2},{7,3},{8,12},{9,13},{10,... | collective-permute-start | bytes 491528 | tf_op jit(solution)/shard_map/in_grad_over_z/ppermute | solution.py:92

commit v5 on v4

--- a/solution.py
+++ b/solution.py
@@ -252,7 +252,7 @@
         sums = jnp.stack([first_sum, second_sum * inverse[:, 0]])
         with jax.named_scope("norm_sums"):
             sums = sums + over_core(sums)
-        whole = after(sums, *depth_marks[1])
+        whole = after(sums, *depth_marks[0])
         with jax.named_scope("norm_sums"):
             whole = whole + sum(over_z(whole, i) for i in range(1, depth))
         with jax.named_scope("in_grad_over_z"):

time: 173 us -> 173 us (level)
  transfers between devices with their start and end apart: 47 -> 47, of which waited for: 29 -> 28; matrix products, arithmetic and copies ran while one was open for 16% -> 16% of each run, Pallas kernels for 0% -> 0%
where the time goes in v5:
time: 173 us
  waiting for transfers between devices  81.8 us (47%)
  starting transfers between devices  46.7 us (27%)
  other arithmetic  15.3 us (9%)
  matrix products  13.1 us (8%)
  local copies, waits for them, and re-layouts  13 us (8%)
  between operations  2.65 us (2%)
    ppermute x28, waiting for transfers between devices, over_row(): return lax.ppermute(value, 'row', [(i, i ^ flip) for i in range(rows)])  55.2 us
    ppermute x28, starting transfers between devices, over_row(): return lax.ppermute(value, 'row', [(i, i ^ flip) for i in range(rows)])  30.8 us
    ppermute x13, waiting for transfers between devices, over_z(): return lax.ppermute(value, 'col', [(i, i ^ 2 * flip) for i in range(cols)])  22.1 us
    ppermute x13, starting transfers between devices, over_z(): return lax.ppermute(value, 'col', [(i, i ^ 2 * flip) for i in range(cols)])  15.5 us
    dynamic_slice x2, local copies, waits for them, and re-layouts, own_and_other(): other = lax.dynamic_slice_in_dim(weight, (1 - core) * width, width, 1)  7.49 us
    dot_general x4, matrix products, dot(): return jnp.dot(a, b, preferred_element_type=F32)  6.56 us
    dot_general x4, matrix products, dot_t(): lax.dot_general(a, b, (((1,), (1,)), ((), ())), preferred_element_type=F32)  6.56 us
    ppermute x6, waiting for transfers between devices, over_core(): return lax.ppermute(value, 'col', [(i, i ^ 1) for i in range(cols)])  4.47 us
  transfers between devices with their start and end apart: 47, of which 28 were waited for; matrix products, arithmetic and copies ran while one was open for 16% of the time, Pallas kernels for 0%

profile of v5, /device:TPU:0, one launch (start us, length us, event | category | flops | bytes accessed | tf_op | source)
XLA Modules:
  0.0 172.6 jit_solution(10035404217706520397)
XLA Ops:
  1.4 1.0 maximum_maximum_fusion
  2.4 5.1 %collective-permute-start.2 = (bf16[144,640]{1,0:T(8,128)(2,1)S(1)}, bf16[144,640]{1,0:T(8,128)(2,1)S(1)}, u32[]{:S(2)}, u32[]{:S(2)}) collective-permute-start(bf16[144,640]{1,0:T(8,128)(2,1)S(1)} %maximum_maximum_fusion), channel_id=1, source_target_pairs={{0,6},{1,7},{2,4},{3,5},{4,2},{5,3},{6,0},{7,1},{8,14},{9,15},{10,... | collective-permute-start | bytes 552968 | tf_op jit(solution)/shard_map/x_over_z/ppermute | solution.py:92
  9.0 1.3 fusion.94
  13.0 2.7 %dynamic-slice_bitcast_fusion = (bf16[1728,640]{1,0:T(8,128)(2,1)S(1)}, bf16[1728,640]{1,0:T(8,128)(2,1)S(1)}) fusion(bf16[1280,1728]{0,1:T(8,128)(2,1)} %param.9, s32[]{:T(128)S(6)} %select_n.53, s32[]{:T(128)S(6)} %select_n.52), kind=kLoop, calls=%fused_computation.2 | loop fusion | bytes 8847368 | tf_op jit(solution)/shard_map/dynamic_slice | solution.py:152
  15.8 7.4 %collective-permute-done.1 = bf16[144,640]{1,0:T(8,128)(2,1)S(1)} collective-permute-done((bf16[144,640]{1,0:T(8,128)(2,1)S(1)}, bf16[144,640]{1,0:T(8,128)(2,1)S(1)}, u32[]{:S(2)}, u32[]{:S(2)}) %collective-permute-start.1) | collective-permute-done | bytes 184352 | tf_op jit(solution)/shard_map/x_over_z/ppermute | solution.py:92
  23.9 1.1 pad_maximum_fusion.1
  25.9 0.9 collective-permute-done.3
  27.2 2.5 %collective-permute-start.6 = (bf16[128,640]{1,0:T(8,128)(2,1)S(1)}, bf16[128,640]{1,0:T(8,128)(2,1)S(1)}, u32[]{:S(2)}, u32[]{:S(2)}) collective-permute-start(bf16[128,640]{1,0:T(8,128)(2,1)S(1)} %get-tuple-element.138), channel_id=1, source_target_pairs={{0,24},{8,16},{16,8},{24,0},{1,25},{9,17},{17,9},{25,1},{2,26},{10... | collective-permute-start | bytes 491528 | tf_op jit(solution)/shard_map/modulated_over_row/ppermute | solution.py:89
  31.2 4.8 %constant_dynamic-slice_fusion.16 = (bf16[1728,640]{1,0:T(8,128)(2,1)}, bf16[1728,640]{1,0:T(8,128)(2,1)}) fusion(bf16[1728,1280]{1,0:T(8,128)(2,1)} %param.10, s32[]{:T(128)S(6)} %select_n.53, s32[]{:T(128)S(6)} %select_n.52), kind=kLoop, calls=%fused_computation.164 | loop fusion | bytes 8847368 | tf_op jit(solution)/shard_map/dynamic_slice | solution.py:152
  36.0 2.0 %collective-permute-done.5 = bf16[128,640]{1,0:T(8,128)(2,1)S(1)} collective-permute-done((bf16[128,640]{1,0:T(8,128)(2,1)S(1)}, bf16[128,640]{1,0:T(8,128)(2,1)S(1)}, u32[]{:S(2)}, u32[]{:S(2)}) %collective-permute-start.5) | collective-permute-done | bytes 163872 | tf_op jit(solution)/shard_map/modulated_over_row/ppermute | solution.py:89
  38.2 2.1 %collective-permute-done.7 = bf16[512,640]{1,0:T(8,128)(2,1)S(1)} collective-permute-done((bf16[512,640]{1,0:T(8,128)(2,1)S(1)}, bf16[512,640]{1,0:T(8,128)(2,1)S(1)}, u32[]{:S(2)}, u32[]{:S(2)}) %collective-permute-start.7) | collective-permute-done | bytes 655392 | tf_op jit(solution)/shard_map/ppermute | solution.py:95
  40.3 1.6 fusion.95
  42.0 1.7 add_convert_fusion.1
  43.7 1.2 copy-done.5
  46.5 1.5 collective-permute-start.8
  48.8 2.5 %collective-permute-start.18 = (bf16[128,640]{1,0:T(8,128)(2,1)S(1)}, bf16[128,640]{1,0:T(8,128)(2,1)S(1)}, u32[]{:S(2)}, u32[]{:S(2)}) collective-permute-start(bf16[128,640]{1,0:T(8,128)(2,1)S(1)} %get-tuple-element.45), channel_id=1, source_target_pairs={{0,6},{1,7},{2,4},{3,5},{4,2},{5,3},{6,0},{7,1},{8,14},{9,15},{10,... | collective-permute-start | bytes 491528 | tf_op jit(solution)/shard_map/z_grad_over_z/ppermute | solution.py:92
  51.2 1.9 %collective-permute-start.16 = (bf16[128,640]{1,0:T(8,128)(2,1)S(1)}, bf16[128,640]{1,0:T(8,128)(2,1)S(1)}, u32[]{:S(2)}, u32[]{:S(2)}) collective-permute-start(bf16[128,640]{1,0:T(8,128)(2,1)S(1)} %get-tuple-element.45), channel_id=1, source_target_pairs={{0,2},{1,3},{2,0},{3,1},{4,6},{5,7},{6,4},{7,5},{8,10},{9,11},{10,... | collective-permute-start | bytes 491528 | tf_op jit(solution)/shard_map/z_grad_over_z/ppermute | solution.py:92
  53.2 6.3 %collective-permute-done.8 = bf16[2,64,1728]{2,1,0:T(8,128)(2,1)} collective-permute-done((bf16[2,64,1728]{2,1,0:T(8,128)(2,1)}, bf16[2,64,1728]{2,1,0:T(8,128)(2,1)}, u32[]{:S(2)}, u32[]{:S(2)}) %collective-permute-start.8) | collective-permute-done | bytes 442400 | tf_op jit(solution)/shard_map/pre_act_scatter/ppermute | solution.py:89
  59.4 1.2 collective-permute-done.9
  60.6 1.4 add_convert_fusion.6
  62.8 1.2 collective-permute-start.11
  64.3 1.6 collective-permute-start.21
  65.8 1.2 collective-permute-start.20
  67.8 3.6 %collective-permute-done.10 = bf16[1,64,1728]{2,1,0:T(8,128)(2,1)S(1)} collective-permute-done((bf16[1,64,1728]{2,1,0:T(8,128)(2,1)S(1)}, bf16[1,64,1728]{2,1,0:T(8,128)(2,1)S(1)}, u32[]{:S(2)}, u32[]{:S(2)}) %collective-permute-start.10) | collective-permute-done | bytes 221216 | tf_op jit(solution)/shard_map/pre_act_scatter/ppermute | solution.py:89
  71.4 1.4 add_bitcast_fusion.3
  73.2 1.2 collective-permute-start.12
  75.6 1.1 collective-permute-done.20
  76.7 1.3 collective-permute-done.19
  78.1 2.8 %collective-permute-done.12 = bf16[1,64,1728]{2,1,0:T(8,128)(2,1)S(1)} collective-permute-done((bf16[1,64,1728]{2,1,0:T(8,128)(2,1)S(1)}, bf16[1,64,1728]{2,1,0:T(8,128)(2,1)S(1)}, u32[]{:S(2)}, u32[]{:S(2)}) %collective-permute-start.12) | collective-permute-done | bytes 221216 | tf_op jit(solution)/shard_map/activated_gather/ppermute | solution.py:89
  81.0 1.4 collective-permute-start.14
  83.1 1.6 fusion.96
  84.8 1.6 add_convert_fusion
  86.5 1.5 collective-permute-start.24
  88.7 5.8 %collective-permute-done.14 = bf16[2,64,1728]{2,1,0:T(8,128)(2,1)S(1)} collective-permute-done((bf16[2,64,1728]{2,1,0:T(8,128)(2,1)S(1)}, bf16[2,64,1728]{2,1,0:T(8,128)(2,1)S(1)}, u32[]{:S(2)}, u32[]{:S(2)}) %collective-permute-start.14) | collective-permute-done | bytes 442400 | tf_op jit(solution)/shard_map/activated_gather/ppermute | solution.py:89
  94.5 1.4 collective-permute-done.15
  96.1 1.6 fusion.97
  97.7 4.9 %collective-permute-done.24 = bf16[2,64,1728]{2,1,0:T(8,128)(2,1)S(1)} collective-permute-done((bf16[2,64,1728]{2,1,0:T(8,128)(2,1)S(1)}, bf16[2,64,1728]{2,1,0:T(8,128)(2,1)S(1)}, u32[]{:S(2)}, u32[]{:S(2)}) %collective-permute-start.24) | collective-permute-done | bytes 442400 | tf_op jit(solution)/shard_map/act_grad_scatter/ppermute | solution.py:89
  102.6 0.9 collective-permute-start.26
  103.6 1.1 collective-permute-start.27
  104.7 1.8 %convolution_convert_fusion.1 = bf16[512,640]{1,0:T(8,128)(2,1)S(1)} fusion(bf16[512,1728]{1,0:T(8,128)(2,1)S(1)} %bitcast_dynamic-update-slice_fusion.6, bf16[1728,640]{1,0:T(8,128)(2,1)S(1)} %copy-done.3), kind=kOutput, calls=%fused_computation.9 | convolution fusion | flops 1132789760 | bytes 4636672 | tf_op jit(solution)/shard_map/dot_general | solution.py:24
  106.6 2.2 %collective-permute-done.26 = bf16[1,64,1728]{2,1,0:T(8,128)(2,1)S(1)} collective-permute-done((bf16[1,64,1728]{2,1,0:T(8,128)(2,1)S(1)}, bf16[1,64,1728]{2,1,0:T(8,128)(2,1)S(1)}, u32[]{:S(2)}, u32[]{:S(2)}) %collective-permute-start.26) | collective-permute-done | bytes 221216 | tf_op jit(solution)/shard_map/act_grad_scatter/ppermute | solution.py:89
  110.4 1.2 collective-permute-start.33
  111.6 0.9 collective-permute-start.34
  112.7 1.6 collective-permute-start.30
  114.3 1.2 collective-permute-start.29
  116.3 2.7 %collective-permute-done.33 = bf16[1,64,1728]{2,1,0:T(8,128)(2,1)S(1)} collective-permute-done((bf16[1,64,1728]{2,1,0:T(8,128)(2,1)S(1)}, bf16[1,64,1728]{2,1,0:T(8,128)(2,1)S(1)}, u32[]{:S(2)}, u32[]{:S(2)}) %collective-permute-start.33) | collective-permute-done | bytes 221216 | tf_op jit(solution)/shard_map/pre_grad_gather/ppermute | solution.py:89
  119.0 2.3 %collective-permute-done.34 = bf16[1,64,1728]{2,1,0:T(8,128)(2,1)S(1)} collective-permute-done((bf16[1,64,1728]{2,1,0:T(8,128)(2,1)S(1)}, bf16[1,64,1728]{2,1,0:T(8,128)(2,1)S(1)}, u32[]{:S(2)}, u32[]{:S(2)}) %collective-permute-start.34) | collective-permute-done | bytes 221216 | tf_op jit(solution)/shard_map/pre_grad_gather/ppermute | solution.py:89
  121.4 1.2 collective-permute-start.35
  123.4 2.2 %collective-permute-done.29 = bf16[128,640]{1,0:T(8,128)(2,1)S(1)} collective-permute-done((bf16[128,640]{1,0:T(8,128)(2,1)S(1)}, bf16[128,640]{1,0:T(8,128)(2,1)S(1)}, u32[]{:S(2)}, u32[]{:S(2)}) %collective-permute-start.29) | collective-permute-done | bytes 163872 | tf_op jit(solution)/shard_map/projected_home/ppermute | solution.py:89
  126.3 6.6 %collective-permute-done.35 = bf16[2,64,1728]{2,1,0:T(8,128)(2,1)S(1)} collective-permute-done((bf16[2,64,1728]{2,1,0:T(8,128)(2,1)S(1)}, bf16[2,64,1728]{2,1,0:T(8,128)(2,1)S(1)}, u32[]{:S(2)}, u32[]{:S(2)}) %collective-permute-start.35) | collective-permute-done | bytes 442400 | tf_op jit(solution)/shard_map/pre_grad_gather/ppermute | solution.py:89
  133.0 1.6 convolution_convert_fusion
  134.7 1.6 fusion.98
  137.0 1.5 collective-permute-start.40
  138.5 1.2 collective-permute-start.39
  139.7 0.9 collective-permute-start.38
  140.7 4.4 %collective-permute-done.40 = bf16[128,640]{1,0:T(8,128)(2,1)S(1)} collective-permute-done((bf16[128,640]{1,0:T(8,128)(2,1)S(1)}, bf16[128,640]{1,0:T(8,128)(2,1)S(1)}, u32[]{:S(2)}, u32[]{:S(2)}) %collective-permute-start.40) | collective-permute-done | bytes 163872 | tf_op jit(solution)/shard_map/in_grad_to_row/ppermute | solution.py:89
  145.0 2.7 %collective-permute-done.39 = bf16[128,640]{1,0:T(8,128)(2,1)S(1)} collective-permute-done((bf16[128,640]{1,0:T(8,128)(2,1)S(1)}, bf16[128,640]{1,0:T(8,128)(2,1)S(1)}, u32[]{:S(2)}, u32[]{:S(2)}) %collective-permute-start.39) | collective-permute-done | bytes 163872 | tf_op jit(solution)/shard_map/in_grad_to_row/ppermute | solution.py:89
  148.9 1.0 collective-permute-done.42
  149.9 2.4 %collective-permute-start.45 = (f32[2,128]{1,0:T(2,128)S(1)}, f32[2,128]{1,0:T(2,128)S(1)}, u32[]{:S(2)}, u32[]{:S(2)}) collective-permute-start(f32[2,128]{1,0:T(2,128)S(1)} %fusion.88), channel_id=1, source_target_pairs={{0,6},{1,7},{2,4},{3,5},{4,2},{5,3},{6,0},{7,1},{8,14},{9,15},{10,... | collective-permute-start | bytes 3080 | tf_op jit(solution)/shard_map/norm_sums/ppermute | solution.py:92
  152.5 1.9 %collective-permute-start.44 = (f32[2,128]{1,0:T(2,128)S(1)}, f32[2,128]{1,0:T(2,128)S(1)}, u32[]{:S(2)}, u32[]{:S(2)}) collective-permute-start(f32[2,128]{1,0:T(2,128)S(1)} %fusion.88), channel_id=1, source_target_pairs={{0,4},{1,5},{2,6},{3,7},{4,0},{5,1},{6,2},{7,3},{8,12},{9,13},{10,... | collective-permute-start | bytes 3080 | tf_op jit(solution)/shard_map/norm_sums/ppermute | solution.py:92
  154.4 5.2 %collective-permute-done.45 = f32[2,128]{1,0:T(2,128)S(1)} collective-permute-done((f32[2,128]{1,0:T(2,128)S(1)}, f32[2,128]{1,0:T(2,128)S(1)}, u32[]{:S(2)}, u32[]{:S(2)}) %collective-permute-start.45) | collective-permute-done | bytes 1056 | tf_op jit(solution)/shard_map/norm_sums/ppermute | solution.py:92
  160.4 9.5 %collective-permute-done.46 = bf16[1,128,640]{2,1,0:T(8,128)(2,1)S(1)} collective-permute-done((bf16[1,128,640]{2,1,0:T(8,128)(2,1)S(1)}, bf16[1,128,640]{2,1,0:T(8,128)(2,1)S(1)}, u32[]{:S(2)}, u32[]{:S(2)}) %collective-permute-start.46) | collective-permute-done | bytes 163872 | tf_op jit(solution)/shard_map/in_grad_over_z/ppermute | solution.py:92
  169.9 0.9 fusion.21
  170.9 1.0 multiply_reduce_fusion.3
  (142 shorter events, 23.0 us)
Async XLA Ops:
  2.4 13.4 %collective-permute-start.2 = (bf16[144,640]{1,0:T(8,128)(2,1)S(1)}, bf16[144,640]{1,0:T(8,128)(2,1)S(1)}, u32[]{:S(2)}, u32[]{:S(2)}) collective-permute-start(bf16[144,640]{1,0:T(8,128)(2,1)S(1)} %maximum_maximum_fusion), channel_id=1, source_target_pairs={{0,6},{1,7},{2,4},{3,5},{4,2},{5,3},{6,0},{7,1},{8,14},{9,15},{10,... | collective-permute-start | bytes 552968 | tf_op jit(solution)/shard_map/x_over_z/ppermute | solution.py:92
  7.6 15.6 %collective-permute-start.1 = (bf16[144,640]{1,0:T(8,128)(2,1)S(1)}, bf16[144,640]{1,0:T(8,128)(2,1)S(1)}, u32[]{:S(2)}, u32[]{:S(2)}) collective-permute-start(bf16[144,640]{1,0:T(8,128)(2,1)S(1)} %maximum_maximum_fusion), channel_id=1, source_target_pairs={{0,4},{1,5},{2,6},{3,7},{4,0},{5,1},{6,2},{7,3},{8,12},{9,13},{10,... | collective-permute-start | bytes 552968 | tf_op jit(solution)/shard_map/x_over_z/ppermute | solution.py:92
  7.6 15.6 %collective-permute-start = (bf16[144,640]{1,0:T(8,128)(2,1)S(1)}, bf16[144,640]{1,0:T(8,128)(2,1)S(1)}, u32[]{:S(2)}, u32[]{:S(2)}) collective-permute-start(bf16[144,640]{1,0:T(8,128)(2,1)S(1)} %maximum_maximum_fusion), channel_id=1, source_target_pairs={{0,2},{1,3},{2,0},{3,1},{4,6},{5,7},{6,4},{7,5},{8,10},{9,11},{10,... | collective-permute-start | bytes 552968 | tf_op jit(solution)/shard_map/x_over_z/ppermute | solution.py:92
  13.0 2.7 %copy-start = (bf16[128,640]{1,0:T(8,128)(2,1)S(1)}, bf16[128,640]{1,0:T(8,128)(2,1)}, u32[]{:S(2)}) copy-start(bf16[128,640]{1,0:T(8,128)(2,1)} %param.6) | copy-start | bytes 491524
  15.7 24.6 %copy-start.1 = (bf16[1728,640]{1,0:T(8,128)(2,1)}, bf16[1728,640]{1,0:T(8,128)(2,1)S(1)}, u32[]{:S(2)}) copy-start(bf16[1728,640]{1,0:T(8,128)(2,1)S(1)} %get-tuple-element.121) | copy-start | bytes 6635524
  15.7 11.1 %copy-start.6 = (bf16[128,640]{1,0:T(8,128)(2,1)S(1)}, bf16[128,640]{1,0:T(8,128)(2,1)}, u32[]{:S(2)}) copy-start(bf16[128,640]{1,0:T(8,128)(2,1)} %param.11) | copy-start | bytes 491524
  23.2 0.7 copy-start.7
  23.2 0.7 copy-start.8
  25.6 1.2 collective-permute-start.3
  27.2 8.8 %collective-permute-start.6 = (bf16[128,640]{1,0:T(8,128)(2,1)S(1)}, bf16[128,640]{1,0:T(8,128)(2,1)S(1)}, u32[]{:S(2)}, u32[]{:S(2)}) collective-permute-start(bf16[128,640]{1,0:T(8,128)(2,1)S(1)} %get-tuple-element.138), channel_id=1, source_target_pairs={{0,24},{8,16},{16,8},{24,0},{1,25},{9,17},{17,9},{25,1},{2,26},{10... | collective-permute-start | bytes 491528 | tf_op jit(solution)/shard_map/modulated_over_row/ppermute | solution.py:89
  29.7 8.3 %collective-permute-start.5 = (bf16[128,640]{1,0:T(8,128)(2,1)S(1)}, bf16[128,640]{1,0:T(8,128)(2,1)S(1)}, u32[]{:S(2)}, u32[]{:S(2)}) collective-permute-start(bf16[128,640]{1,0:T(8,128)(2,1)S(1)} %get-tuple-element.137), channel_id=1, source_target_pairs={{0,16},{8,24},{16,0},{24,8},{1,17},{9,25},{17,1},{25,9},{2,18},{10... | collective-permute-start | bytes 491528 | tf_op jit(solution)/shard_map/modulated_over_row/ppermute | solution.py:89
  30.6 7.5 %collective-permute-start.4 = (bf16[128,640]{1,0:T(8,128)(2,1)S(1)}, bf16[128,640]{1,0:T(8,128)(2,1)S(1)}, u32[]{:S(2)}, u32[]{:S(2)}) collective-permute-start(bf16[128,640]{1,0:T(8,128)(2,1)S(1)} %get-tuple-element.136), channel_id=1, source_target_pairs={{0,8},{8,0},{16,24},{24,16},{1,9},{9,1},{17,25},{25,17},{2,10},{10... | collective-permute-start | bytes 491528 | tf_op jit(solution)/shard_map/modulated_over_row/ppermute | solution.py:89
  38.2 2.2 %collective-permute-start.7 = (bf16[512,640]{1,0:T(8,128)(2,1)S(1)}, bf16[512,640]{1,0:T(8,128)(2,1)S(1)}, u32[]{:S(2)}, u32[]{:S(2)}) collective-permute-start(bf16[512,640]{1,0:T(8,128)(2,1)S(1)} %pad_maximum_fusion.2), channel_id=1, source_target_pairs={{0,1},{1,0},{2,3},{3,2},{4,5},{5,4},{6,7},{7,6},{8,9},{9,8},{10,11... | collective-permute-start | bytes 1966088 | tf_op jit(solution)/shard_map/ppermute | solution.py:95
  43.6 1.2 copy-start.5
  46.5 12.9 %collective-permute-start.8 = (bf16[2,64,1728]{2,1,0:T(8,128)(2,1)}, bf16[2,64,1728]{2,1,0:T(8,128)(2,1)}, u32[]{:S(2)}, u32[]{:S(2)}) collective-permute-start(bf16[2,64,1728]{2,1,0:T(8,128)(2,1)} %pad_maximum_fusion.7), channel_id=1, source_target_pairs={{0,8},{8,0},{16,24},{24,16},{1,9},{9,1},{17,25},{25,17},{2,10},{10... | collective-permute-start | bytes 1327112 | tf_op jit(solution)/shard_map/pre_act_scatter/ppermute | solution.py:89
  48.0 12.6 %collective-permute-start.9 = (bf16[2,64,1728]{2,1,0:T(8,128)(2,1)}, bf16[2,64,1728]{2,1,0:T(8,128)(2,1)}, u32[]{:S(2)}, u32[]{:S(2)}) collective-permute-start(bf16[2,64,1728]{2,1,0:T(8,128)(2,1)} %stack.209), channel_id=1, source_target_pairs={{0,16},{8,24},{16,0},{24,8},{1,17},{9,25},{17,1},{25,9},{2,18},{10... | collective-permute-start | bytes 1327112 | tf_op jit(solution)/shard_map/pre_act_scatter/ppermute | solution.py:89
  48.8 15.3 %collective-permute-start.18 = (bf16[128,640]{1,0:T(8,128)(2,1)S(1)}, bf16[128,640]{1,0:T(8,128)(2,1)S(1)}, u32[]{:S(2)}, u32[]{:S(2)}) collective-permute-start(bf16[128,640]{1,0:T(8,128)(2,1)S(1)} %get-tuple-element.45), channel_id=1, source_target_pairs={{0,6},{1,7},{2,4},{3,5},{4,2},{5,3},{6,0},{7,1},{8,14},{9,15},{10,... | collective-permute-start | bytes 491528 | tf_op jit(solution)/shard_map/z_grad_over_z/ppermute | solution.py:92
  51.2 12.8 %collective-permute-start.17 = (bf16[128,640]{1,0:T(8,128)(2,1)S(1)}, bf16[128,640]{1,0:T(8,128)(2,1)S(1)}, u32[]{:S(2)}, u32[]{:S(2)}) collective-permute-start(bf16[128,640]{1,0:T(8,128)(2,1)S(1)} %get-tuple-element.45), channel_id=1, source_target_pairs={{0,4},{1,5},{2,6},{3,7},{4,0},{5,1},{6,2},{7,3},{8,12},{9,13},{10,... | collective-permute-start | bytes 491528 | tf_op jit(solution)/shard_map/z_grad_over_z/ppermute | solution.py:92
  51.2 12.8 %collective-permute-start.16 = (bf16[128,640]{1,0:T(8,128)(2,1)S(1)}, bf16[128,640]{1,0:T(8,128)(2,1)S(1)}, u32[]{:S(2)}, u32[]{:S(2)}) collective-permute-start(bf16[128,640]{1,0:T(8,128)(2,1)S(1)} %get-tuple-element.45), channel_id=1, source_target_pairs={{0,2},{1,3},{2,0},{3,1},{4,6},{5,7},{6,4},{7,5},{8,10},{9,11},{10,... | collective-permute-start | bytes 491528 | tf_op jit(solution)/shard_map/z_grad_over_z/ppermute | solution.py:92
  62.0 9.4 %collective-permute-start.10 = (bf16[1,64,1728]{2,1,0:T(8,128)(2,1)S(1)}, bf16[1,64,1728]{2,1,0:T(8,128)(2,1)S(1)}, u32[]{:S(2)}, u32[]{:S(2)}) collective-permute-start(bf16[1,64,1728]{2,1,0:T(8,128)(2,1)S(1)} %get-tuple-element.132), channel_id=1, source_target_pairs={{0,16},{8,24},{16,0},{24,8},{1,17},{9,25},{17,1},{25,9},{2,18},{10... | collective-permute-start | bytes 663560 | tf_op jit(solution)/shard_map/pre_act_scatter/ppermute | solution.py:89
  62.8 8.6 %collective-permute-start.11 = (bf16[1,64,1728]{2,1,0:T(8,128)(2,1)S(1)}, bf16[1,64,1728]{2,1,0:T(8,128)(2,1)S(1)}, u32[]{:S(2)}, u32[]{:S(2)}) collective-permute-start(bf16[1,64,1728]{2,1,0:T(8,128)(2,1)S(1)} %get-tuple-element.131), channel_id=1, source_target_pairs={{0,8},{8,0},{16,24},{24,16},{1,9},{9,1},{17,25},{25,17},{2,10},{10... | collective-permute-start | bytes 663560 | tf_op jit(solution)/shard_map/pre_act_scatter/ppermute | solution.py:89
  64.3 11.3 %collective-permute-start.21 = (bf16[128,640]{1,0:T(8,128)(2,1)S(1)}, bf16[128,640]{1,0:T(8,128)(2,1)S(1)}, u32[]{:S(2)}, u32[]{:S(2)}) collective-permute-start(bf16[128,640]{1,0:T(8,128)(2,1)S(1)} %get-tuple-element.150), channel_id=1, source_target_pairs={{0,24},{8,16},{16,8},{24,0},{1,25},{9,17},{17,9},{25,1},{2,26},{10... | collective-permute-start | bytes 491528 | tf_op jit(solution)/shard_map/z_grad_over_row/ppermute | solution.py:89
  65.8 10.9 %collective-permute-start.20 = (bf16[128,640]{1,0:T(8,128)(2,1)S(1)}, bf16[128,640]{1,0:T(8,128)(2,1)S(1)}, u32[]{:S(2)}, u32[]{:S(2)}) collective-permute-start(bf16[128,640]{1,0:T(8,128)(2,1)S(1)} %get-tuple-element.151), channel_id=1, source_target_pairs={{0,16},{8,24},{16,0},{24,8},{1,17},{9,25},{17,1},{25,9},{2,18},{10... | collective-permute-start | bytes 491528 | tf_op jit(solution)/shard_map/z_grad_over_row/ppermute | solution.py:89
  67.0 10.9 %collective-permute-start.19 = (bf16[128,640]{1,0:T(8,128)(2,1)S(1)}, bf16[128,640]{1,0:T(8,128)(2,1)S(1)}, u32[]{:S(2)}, u32[]{:S(2)}) collective-permute-start(bf16[128,640]{1,0:T(8,128)(2,1)S(1)} %get-tuple-element.152), channel_id=1, source_target_pairs={{0,8},{8,0},{16,24},{24,16},{1,9},{9,1},{17,25},{25,17},{2,10},{10... | collective-permute-start | bytes 491528 | tf_op jit(solution)/shard_map/z_grad_over_row/ppermute | solution.py:89
  73.2 9.9 %copy-start.3 = (bf16[1728,640]{1,0:T(8,128)(2,1)S(1)}, bf16[1728,640]{1,0:T(8,128)(2,1)}, u32[]{:S(2)}) copy-start(bf16[1728,640]{1,0:T(8,128)(2,1)} %get-tuple-element.119) | copy-start | bytes 6635524
  73.2 7.7 %collective-permute-start.12 = (bf16[1,64,1728]{2,1,0:T(8,128)(2,1)S(1)}, bf16[1,64,1728]{2,1,0:T(8,128)(2,1)S(1)}, u32[]{:S(2)}, u32[]{:S(2)}) collective-permute-start(bf16[1,64,1728]{2,1,0:T(8,128)(2,1)S(1)} %get-tuple-element.157), channel_id=1, source_target_pairs={{0,8},{8,0},{16,24},{24,16},{1,9},{9,1},{17,25},{25,17},{2,10},{10... | collective-permute-start | bytes 663560 | tf_op jit(solution)/shard_map/activated_gather/ppermute | solution.py:89
  74.4 6.5 %collective-permute-start.13 = (bf16[1,64,1728]{2,1,0:T(8,128)(2,1)S(1)}, bf16[1,64,1728]{2,1,0:T(8,128)(2,1)S(1)}, u32[]{:S(2)}, u32[]{:S(2)}) collective-permute-start(bf16[1,64,1728]{2,1,0:T(8,128)(2,1)S(1)} %get-tuple-element.156), channel_id=1, source_target_pairs={{0,16},{8,24},{16,0},{24,8},{1,17},{9,25},{17,1},{25,9},{2,18},{10... | collective-permute-start | bytes 663560 | tf_op jit(solution)/shard_map/activated_gather/ppermute | solution.py:89
  78.0 5.1 %collective-permute-start.22 = (bf16[512,640]{1,0:T(8,128)(2,1)S(1)}, bf16[512,640]{1,0:T(8,128)(2,1)S(1)}, u32[]{:S(2)}, u32[]{:S(2)}) collective-permute-start(bf16[512,640]{1,0:T(8,128)(2,1)S(1)} %pad_maximum_fusion.4), channel_id=1, source_target_pairs={{0,1},{1,0},{2,3},{3,2},{4,5},{5,4},{6,7},{7,6},{8,9},{9,8},{10,11... | collective-permute-start | bytes 1966088 | tf_op jit(solution)/shard_map/ppermute | solution.py:95
  81.0 13.5 %collective-permute-start.14 = (bf16[2,64,1728]{2,1,0:T(8,128)(2,1)S(1)}, bf16[2,64,1728]{2,1,0:T(8,128)(2,1)S(1)}, u32[]{:S(2)}, u32[]{:S(2)}) collective-permute-start(bf16[2,64,1728]{2,1,0:T(8,128)(2,1)S(1)} %pad_maximum_fusion.8), channel_id=1, source_target_pairs={{0,16},{8,24},{16,0},{24,8},{1,17},{9,25},{17,1},{25,9},{2,18},{10... | collective-permute-start | bytes 1327112 | tf_op jit(solution)/shard_map/activated_gather/ppermute | solution.py:89
  82.4 13.5 %collective-permute-start.15 = (bf16[2,64,1728]{2,1,0:T(8,128)(2,1)S(1)}, bf16[2,64,1728]{2,1,0:T(8,128)(2,1)S(1)}, u32[]{:S(2)}, u32[]{:S(2)}) collective-permute-start(bf16[2,64,1728]{2,1,0:T(8,128)(2,1)S(1)} %pad_maximum_fusion.9), channel_id=1, source_target_pairs={{0,8},{8,0},{16,24},{24,16},{1,9},{9,1},{17,25},{25,17},{2,10},{10... | collective-permute-start | bytes 1327112 | tf_op jit(solution)/shard_map/activated_gather/ppermute | solution.py:89
  83.1 1.7 copy-start.4
  86.5 16.0 %collective-permute-start.24 = (bf16[2,64,1728]{2,1,0:T(8,128)(2,1)S(1)}, bf16[2,64,1728]{2,1,0:T(8,128)(2,1)S(1)}, u32[]{:S(2)}, u32[]{:S(2)}) collective-permute-start(bf16[2,64,1728]{2,1,0:T(8,128)(2,1)S(1)} %pad_maximum_fusion.10), channel_id=1, source_target_pairs={{0,8},{8,0},{16,24},{24,16},{1,9},{9,1},{17,25},{25,17},{2,10},{10... | collective-permute-start | bytes 1327112 | tf_op jit(solution)/shard_map/act_grad_scatter/ppermute | solution.py:89
  88.0 14.5 %collective-permute-start.25 = (bf16[2,64,1728]{2,1,0:T(8,128)(2,1)S(1)}, bf16[2,64,1728]{2,1,0:T(8,128)(2,1)S(1)}, u32[]{:S(2)}, u32[]{:S(2)}) collective-permute-start(bf16[2,64,1728]{2,1,0:T(8,128)(2,1)S(1)} %stack.210), channel_id=1, source_target_pairs={{0,16},{8,24},{16,0},{24,8},{1,17},{9,25},{17,1},{25,9},{2,18},{10... | collective-permute-start | bytes 1327112 | tf_op jit(solution)/shard_map/act_grad_scatter/ppermute | solution.py:89
  102.6 6.1 %collective-permute-start.26 = (bf16[1,64,1728]{2,1,0:T(8,128)(2,1)S(1)}, bf16[1,64,1728]{2,1,0:T(8,128)(2,1)S(1)}, u32[]{:S(2)}, u32[]{:S(2)}) collective-permute-start(bf16[1,64,1728]{2,1,0:T(8,128)(2,1)S(1)} %get-tuple-element.50), channel_id=1, source_target_pairs={{0,16},{8,24},{16,0},{24,8},{1,17},{9,25},{17,1},{25,9},{2,18},{10... | collective-permute-start | bytes 663560 | tf_op jit(solution)/shard_map/act_grad_scatter/ppermute | solution.py:89
  103.6 6.0 %collective-permute-start.27 = (bf16[1,64,1728]{2,1,0:T(8,128)(2,1)S(1)}, bf16[1,64,1728]{2,1,0:T(8,128)(2,1)S(1)}, u32[]{:S(2)}, u32[]{:S(2)}) collective-permute-start(bf16[1,64,1728]{2,1,0:T(8,128)(2,1)S(1)} %get-tuple-element.52), channel_id=1, source_target_pairs={{0,8},{8,0},{16,24},{24,16},{1,9},{9,1},{17,25},{25,17},{2,10},{10... | collective-permute-start | bytes 663560 | tf_op jit(solution)/shard_map/act_grad_scatter/ppermute | solution.py:89
  106.5 6.0 %collective-permute-start.23 = (bf16[512,640]{1,0:T(8,128)(2,1)S(1)}, bf16[512,640]{1,0:T(8,128)(2,1)S(1)}, u32[]{:S(2)}, u32[]{:S(2)}) collective-permute-start(bf16[512,640]{1,0:T(8,128)(2,1)S(1)} %convolution_convert_fusion.1), channel_id=1, source_target_pairs={{0,1},{1,0},{2,3},{3,2},{4,5},{5,4},{6,7},{7,6},{8,9},{9,8},{10,11... | collective-permute-start | bytes 1966088 | tf_op jit(solution)/shard_map/ppermute | solution.py:95
  110.4 8.6 %collective-permute-start.33 = (bf16[1,64,1728]{2,1,0:T(8,128)(2,1)S(1)}, bf16[1,64,1728]{2,1,0:T(8,128)(2,1)S(1)}, u32[]{:S(2)}, u32[]{:S(2)}) collective-permute-start(bf16[1,64,1728]{2,1,0:T(8,128)(2,1)S(1)} %get-tuple-element.155), channel_id=1, source_target_pairs={{0,8},{8,0},{16,24},{24,16},{1,9},{9,1},{17,25},{25,17},{2,10},{10... | collective-permute-start | bytes 663560 | tf_op jit(solution)/shard_map/pre_grad_gather/ppermute | solution.py:89
  111.6 9.7 %collective-permute-start.34 = (bf16[1,64,1728]{2,1,0:T(8,128)(2,1)S(1)}, bf16[1,64,1728]{2,1,0:T(8,128)(2,1)S(1)}, u32[]{:S(2)}, u32[]{:S(2)}) collective-permute-start(bf16[1,64,1728]{2,1,0:T(8,128)(2,1)S(1)} %get-tuple-element.154), channel_id=1, source_target_pairs={{0,16},{8,24},{16,0},{24,8},{1,17},{9,25},{17,1},{25,9},{2,18},{10... | collective-permute-start | bytes 663560 | tf_op jit(solution)/shard_map/pre_grad_gather/ppermute | solution.py:89
  112.7 10.6 %collective-permute-start.30 = (bf16[128,640]{1,0:T(8,128)(2,1)S(1)}, bf16[128,640]{1,0:T(8,128)(2,1)S(1)}, u32[]{:S(2)}, u32[]{:S(2)}) collective-permute-start(bf16[128,640]{1,0:T(8,128)(2,1)S(1)} %get-tuple-element.146), channel_id=1, source_target_pairs={{0,24},{8,16},{16,8},{24,0},{1,25},{9,17},{17,9},{25,1},{2,26},{10... | collective-permute-start | bytes 491528 | tf_op jit(solution)/shard_map/projected_home/ppermute | solution.py:89
  114.3 11.3 %collective-permute-start.29 = (bf16[128,640]{1,0:T(8,128)(2,1)S(1)}, bf16[128,640]{1,0:T(8,128)(2,1)S(1)}, u32[]{:S(2)}, u32[]{:S(2)}) collective-permute-start(bf16[128,640]{1,0:T(8,128)(2,1)S(1)} %get-tuple-element.147), channel_id=1, source_target_pairs={{0,16},{8,24},{16,0},{24,8},{1,17},{9,25},{17,1},{25,9},{2,18},{10... | collective-permute-start | bytes 491528 | tf_op jit(solution)/shard_map/projected_home/ppermute | solution.py:89
  115.5 10.6 %collective-permute-start.28 = (bf16[128,640]{1,0:T(8,128)(2,1)S(1)}, bf16[128,640]{1,0:T(8,128)(2,1)S(1)}, u32[]{:S(2)}, u32[]{:S(2)}) collective-permute-start(bf16[128,640]{1,0:T(8,128)(2,1)S(1)} %get-tuple-element.148), channel_id=1, source_target_pairs={{0,8},{8,0},{16,24},{24,16},{1,9},{9,1},{17,25},{25,17},{2,10},{10... | collective-permute-start | bytes 491528 | tf_op jit(solution)/shard_map/projected_home/ppermute | solution.py:89
  121.4 11.5 %collective-permute-start.35 = (bf16[2,64,1728]{2,1,0:T(8,128)(2,1)S(1)}, bf16[2,64,1728]{2,1,0:T(8,128)(2,1)S(1)}, u32[]{:S(2)}, u32[]{:S(2)}) collective-permute-start(bf16[2,64,1728]{2,1,0:T(8,128)(2,1)S(1)} %get-tuple-element.58), channel_id=1, source_target_pairs={{0,16},{8,24},{16,0},{24,8},{1,17},{9,25},{17,1},{25,9},{2,18},{10... | collective-permute-start | bytes 1327112 | tf_op jit(solution)/shard_map/pre_grad_gather/ppermute | solution.py:89
  122.6 10.3 %collective-permute-start.36 = (bf16[2,64,1728]{2,1,0:T(8,128)(2,1)S(1)}, bf16[2,64,1728]{2,1,0:T(8,128)(2,1)S(1)}, u32[]{:S(2)}, u32[]{:S(2)}) collective-permute-start(bf16[2,64,1728]{2,1,0:T(8,128)(2,1)S(1)} %get-tuple-element.60), channel_id=1, source_target_pairs={{0,8},{8,0},{16,24},{24,16},{1,9},{9,1},{17,25},{25,17},{2,10},{10... | collective-permute-start | bytes 1327112 | tf_op jit(solution)/shard_map/pre_grad_gather/ppermute | solution.py:89
  126.2 6.9 %copy-start.2 = (bf16[1728,640]{1,0:T(8,128)(2,1)S(1)}, bf16[1728,640]{1,0:T(8,128)(2,1)}, u32[]{:S(2)}) copy-start(bf16[1728,640]{1,0:T(8,128)(2,1)} %copy-done.1) | copy-start | bytes 6635524
  126.2 8.5 %collective-permute-start.31 = (bf16[2,128,640]{2,1,0:T(8,128)(2,1)S(1)}, bf16[2,128,640]{2,1,0:T(8,128)(2,1)S(1)}, u32[]{:S(2)}, u32[]{:S(2)}) collective-permute-start(bf16[2,128,640]{2,1,0:T(8,128)(2,1)S(1)} %pad_maximum_fusion.13), channel_id=1, source_target_pairs={{0,2},{1,3},{2,0},{3,1},{4,6},{5,7},{6,4},{7,5},{8,10},{9,11},{10,... | collective-permute-start | bytes 983048 | tf_op jit(solution)/shard_map/projected_home/ppermute | solution.py:92
  134.6 2.2 %collective-permute-start.37 = (bf16[512,640]{1,0:T(8,128)(2,1)S(1)}, bf16[512,640]{1,0:T(8,128)(2,1)S(1)}, u32[]{:S(2)}, u32[]{:S(2)}) collective-permute-start(bf16[512,640]{1,0:T(8,128)(2,1)S(1)} %convolution_convert_fusion), channel_id=1, source_target_pairs={{0,1},{1,0},{2,3},{3,2},{4,5},{5,4},{6,7},{7,6},{8,9},{9,8},{10,11... | collective-permute-start | bytes 1966088 | tf_op jit(solution)/shard_map/ppermute | solution.py:95
  137.0 8.1 %collective-permute-start.40 = (bf16[128,640]{1,0:T(8,128)(2,1)S(1)}, bf16[128,640]{1,0:T(8,128)(2,1)S(1)}, u32[]{:S(2)}, u32[]{:S(2)}) collective-permute-start(bf16[128,640]{1,0:T(8,128)(2,1)S(1)} %get-tuple-element.140), channel_id=1, source_target_pairs={{0,24},{8,16},{16,8},{24,0},{1,25},{9,17},{17,9},{25,1},{2,26},{10... | collective-permute-start | bytes 491528 | tf_op jit(solution)/shard_map/in_grad_to_row/ppermute | solution.py:89
  138.5 9.2 %collective-permute-start.39 = (bf16[128,640]{1,0:T(8,128)(2,1)S(1)}, bf16[128,640]{1,0:T(8,128)(2,1)S(1)}, u32[]{:S(2)}, u32[]{:S(2)}) collective-permute-start(bf16[128,640]{1,0:T(8,128)(2,1)S(1)} %get-tuple-element.141), channel_id=1, source_target_pairs={{0,16},{8,24},{16,0},{24,8},{1,17},{9,25},{17,1},{25,9},{2,18},{10... | collective-permute-start | bytes 491528 | tf_op jit(solution)/shard_map/in_grad_to_row/ppermute | solution.py:89
  139.7 8.1 %collective-permute-start.38 = (bf16[128,640]{1,0:T(8,128)(2,1)S(1)}, bf16[128,640]{1,0:T(8,128)(2,1)S(1)}, u32[]{:S(2)}, u32[]{:S(2)}) collective-permute-start(bf16[128,640]{1,0:T(8,128)(2,1)S(1)} %get-tuple-element.142), channel_id=1, source_target_pairs={{0,8},{8,0},{16,24},{24,16},{1,9},{9,1},{17,25},{25,17},{2,10},{10... | collective-permute-start | bytes 491528 | tf_op jit(solution)/shard_map/in_grad_to_row/ppermute | solution.py:89
  140.6 13.8 %collective-permute-start.32 = (bf16[1,128,640]{2,1,0:T(8,128)(2,1)S(1)}, bf16[1,128,640]{2,1,0:T(8,128)(2,1)S(1)}, u32[]{:S(2)}, u32[]{:S(2)}) collective-permute-start(bf16[1,128,640]{2,1,0:T(8,128)(2,1)S(1)} %add_convert_fusion.8), channel_id=1, source_target_pairs={{0,4},{1,5},{2,6},{3,7},{4,0},{5,1},{6,2},{7,3},{8,12},{9,13},{10,... | collective-permute-start | bytes 491528 | tf_op jit(solution)/shard_map/projected_home/ppermute | solution.py:92
  148.7 1.2 collective-permute-start.42
  148.8 10.8 %collective-permute-start.41 = (bf16[2,128,640]{2,1,0:T(8,128)(2,1)S(1)}, bf16[2,128,640]{2,1,0:T(8,128)(2,1)S(1)}, u32[]{:S(2)}, u32[]{:S(2)}) collective-permute-start(bf16[2,128,640]{2,1,0:T(8,128)(2,1)S(1)} %pad_maximum_fusion.14), channel_id=1, source_target_pairs={{0,2},{1,3},{2,0},{3,1},{4,6},{5,7},{6,4},{7,5},{8,10},{9,11},{10,... | collective-permute-start | bytes 983048 | tf_op jit(solution)/shard_map/in_grad_over_z/ppermute | solution.py:92
  149.9 9.7 %collective-permute-start.45 = (f32[2,128]{1,0:T(2,128)S(1)}, f32[2,128]{1,0:T(2,128)S(1)}, u32[]{:S(2)}, u32[]{:S(2)}) collective-permute-start(f32[2,128]{1,0:T(2,128)S(1)} %fusion.88), channel_id=1, source_target_pairs={{0,6},{1,7},{2,4},{3,5},{4,2},{5,3},{6,0},{7,1},{8,14},{9,15},{10,... | collective-permute-start | bytes 3080 | tf_op jit(solution)/shard_map/norm_sums/ppermute | solution.py:92
  152.3 7.3 %collective-permute-start.43 = (f32[2,128]{1,0:T(2,128)S(1)}, f32[2,128]{1,0:T(2,128)S(1)}, u32[]{:S(2)}, u32[]{:S(2)}) collective-permute-start(f32[2,128]{1,0:T(2,128)S(1)} %fusion.88), channel_id=1, source_target_pairs={{0,2},{1,3},{2,0},{3,1},{4,6},{5,7},{6,4},{7,5},{8,10},{9,11},{10,... | collective-permute-start | bytes 3080 | tf_op jit(solution)/shard_map/norm_sums/ppermute | solution.py:92
  152.5 7.2 %collective-permute-start.44 = (f32[2,128]{1,0:T(2,128)S(1)}, f32[2,128]{1,0:T(2,128)S(1)}, u32[]{:S(2)}, u32[]{:S(2)}) collective-permute-start(f32[2,128]{1,0:T(2,128)S(1)} %fusion.88), channel_id=1, source_target_pairs={{0,4},{1,5},{2,6},{3,7},{4,0},{5,1},{6,2},{7,3},{8,12},{9,13},{10,... | collective-permute-start | bytes 3080 | tf_op jit(solution)/shard_map/norm_sums/ppermute | solution.py:92
  159.7 10.2 %collective-permute-start.46 = (bf16[1,128,640]{2,1,0:T(8,128)(2,1)S(1)}, bf16[1,128,640]{2,1,0:T(8,128)(2,1)S(1)}, u32[]{:S(2)}, u32[]{:S(2)}) collective-permute-start(bf16[1,128,640]{2,1,0:T(8,128)(2,1)S(1)} %fusion.16), channel_id=1, source_target_pairs={{0,4},{1,5},{2,6},{3,7},{4,0},{5,1},{6,2},{7,3},{8,12},{9,13},{10,... | collective-permute-start | bytes 491528 | tf_op jit(solution)/shard_map/in_grad_over_z/ppermute | solution.py:92
